TPU v7x, 32 devices: a whole 2x2x4 slice. The times are simulated.
32 devices in a mesh: row: 4 (over x, core), col: 8 (over z, y).
Axes of the slice: x: 2, y: 2, z: 4, core: 2. Of those that a mesh axis runs over, the one named last changes fastest.
Arguments:
- ancestor_inverse: bfloat16 [32768, 32768], P('row', 'col'), may hold values from -0.03125 to 0.03125
- panel: bfloat16 [32768, 512], P(('row', 'col')), may hold values from -0.75 to 0.75
- structure: int32 [2, 128], replicated, may hold values 0 or 1
- diag_inverse: float32 [2, 256, 256], replicated, may hold values from -6 to 6
Outputs:
- upper: bfloat16 [32768, 512], P(('row', 'col'))
- diagonal: float32 [2, 256, 256], replicated
All inputs are finite; a program needn't handle non-finite values.
Results may differ from a plain program's by a relative error of at most 0.0014.
Values may be sent and summed in bfloat16 or wider, within the bound.
No kernel may reach another device: no remote copies, remote signals or barrier semaphores. Data moves between devices by JAX's collectives and lax.ppermute only.
A program may use at most 128 MiB of HBM per device.

v0:
```python
import jax
import jax.numpy as jnp
from jax import lax
from jax.sharding import PartitionSpec as P


def from_root(block, axis, source):
    block = jnp.where(lax.axis_index(axis) == source, block, jnp.zeros_like(block))
    return lax.psum(block, axis)


def row_keep(begin_row, length, structure, blk_width):
    blocks_all = structure.shape[1]
    indices = begin_row + jnp.arange(length, dtype=jnp.int32)
    owners = indices // blk_width
    onehot = (owners[:, None] == jnp.arange(blocks_all, dtype=jnp.int32)[None, :]).astype(
        jnp.float32
    )
    keeps = jnp.dot(onehot, structure.T.astype(jnp.float32), preferred_element_type=jnp.float32)
    return jnp.repeat(keeps, blk_width, axis=1)


def diag_part(lower, upper_rows, blk_width):
    snodes = upper_rows.shape[1] // blk_width
    lower_f = lower.astype(jnp.float32).reshape(lower.shape[0], snodes, blk_width)
    upper_f = upper_rows.reshape(upper_rows.shape[0], snodes, blk_width)
    return jnp.einsum("mkw,mkv->kwv", lower_f, upper_f, precision=lax.Precision.HIGHEST)


def local(ancestor_inverse, panel, structure, diag_inverse):
    blk_width = diag_inverse.shape[1]
    row_count = lax.axis_size("row")
    col_count = lax.axis_size("col")
    row_index = lax.axis_index("row")
    col_index = lax.axis_index("col")
    piece_rows = panel.shape[0]
    span_col = piece_rows * row_count
    begin_own = (row_index * col_count + col_index) * piece_rows
    keep_own = row_keep(begin_own, piece_rows, structure, blk_width)
    masked = panel * keep_own.astype(jnp.bfloat16)
    row_block = lax.all_gather(masked, "col", axis=0, tiled=True)
    ratio = col_count // row_count
    root_row = col_index // ratio
    offset = col_index % ratio * span_col
    own_slice = lax.dynamic_slice_in_dim(row_block, offset, span_col, 0)
    col_block = from_root(own_slice, "row", root_row)
    own_rows = lax.psum_scatter(
        -jnp.dot(ancestor_inverse, col_block, preferred_element_type=jnp.float32),
        "col",
        scatter_dimension=0,
        tiled=True,
    )
    diag_sum = lax.psum(diag_part(masked, own_rows, blk_width), ("row", "col"))
    upper = (own_rows * keep_own).astype(jnp.bfloat16)
    diagonal = diag_inverse - diag_sum
    return (upper, diagonal)


def solution(mesh):
    return jax.shard_map(
        local,
        mesh=mesh,
        in_specs=(P("row", "col"), P(("row", "col"), None), P(), P()),
        out_specs=(P(("row", "col"), None), P()),
        check_vma=False,
    )
```

profile of v0, /device:TPU:0, one launch (start us, length us, event | category | flops | bytes accessed | tf_op | source)
XLA Modules:
  0.0 693.8 jit_solution(18433633879252039716)
XLA Ops:
  7.2 0.0 all-gather.2.cloned.1.call-start
  7.2 1.5 copy.6
  8.7 1.0 fusion.2
  9.7 1.1 fusion.1
  10.8 0.0 all-gather.2.cloned.1.call-update
  10.8 0.0 all-reduce.3.cloned.1.call-start
  10.9 127.7 %all-gather.2.cloned.1.call-done = bf16[8192,512]{0,1:T(8,128)(2,1)} async-done(((bf16[1024,512]{0,1:T(8,128)(2,1)}), bf16[8192,512]{0,1:T(8,128)(2,1)}) %all-gather.2.cloned.1.call-update) | async-done | bytes 8388624 | tf_op jit(solution)/shard_map/all_gather | solution.py:41
  138.6 5.2 dynamic-slice_select_fusion
  143.8 0.0 all-reduce.3.cloned.1.call-update
  143.8 0.0 reduce-scatter.2.cloned.1.call-start
  143.8 83.8 %all-reduce.3.cloned.1.call-done = bf16[4096,512]{0,1:T(8,128)(2,1)} async-done(((bf16[4096,512]{0,1:T(8,128)(2,1)}), bf16[4096,512]{0,1:T(8,128)(2,1)}) %all-reduce.3.cloned.1.call-update) | async-done | bytes 4194320 | tf_op jit(solution)/shard_map/psum | solution.py:9
  227.6 42.1 %negate_bitcast_fusion = f32[8192,512]{0,1:T(8,128)} fusion(bf16[4096,512]{0,1:T(8,128)(2,1)} %all-reduce.3.cloned.1.call-done, bf16[8192,4096]{1,0:T(8,128)(2,1)} %param.4), kind=kOutput, calls=%fused_computation | convolution fusion | flops 34363932672 | bytes 88080384 | tf_op jit(solution)/shard_map/dot_general | solution.py:48
  269.7 0.0 copy-start
  269.7 0.0 reduce-scatter.2.cloned.1.call-update
  269.8 0.0 all-reduce.5.cloned.1.call-start
  269.8 282.8 %reduce-scatter.2.cloned.1.call-done = f32[1024,512]{0,1:T(8,128)} async-done(((f32[8192,512]{0,1:T(8,128)}), f32[1024,512]{0,1:T(8,128)}) %reduce-scatter.2.cloned.1.call-update) | async-done | bytes 2097168 | tf_op jit(solution)/shard_map/reduce_scatter | solution.py:47
  552.6 0.0 copy-start.1
  552.6 0.0 copy-done
  552.6 3.8 fusion.8
  556.4 0.0 all-reduce.5.cloned.1.call-update
  556.4 0.0 copy-done.1
  556.4 0.3 fusion
  556.7 1.3 copy.8
  558.0 127.2 %all-reduce.5.cloned.1.call-done = f32[2,256,256]{2,1,0:T(8,128)} async-done(((f32[2,256,256]{2,1,0:T(8,128)}), f32[2,256,256]{2,1,0:T(8,128)}) %all-reduce.5.cloned.1.call-update) | async-done | bytes 524304 | tf_op jit(solution)/shard_map/psum | solution.py:53
  685.2 2.1 sub.15
  (1 shorter events, 0.0 us)
Async XLA Ops:
  7.2 131.4 %all-gather.2.cloned.1.call-start = ((), (), s32[]{:S(2)}) async-start(), calls=%async_computation.1 | async-start | bytes 9437184 | tf_op jit(solution)/shard_map/all_gather | solution.py:41
  10.8 216.8 %all-reduce.3.cloned.1.call-start = ((), (), s32[]{:S(2)}) async-start(), calls=%async_computation.2 | async-start | bytes 8388608 | tf_op jit(solution)/shard_map/psum | solution.py:9
  143.8 408.8 %reduce-scatter.2.cloned.1.call-start = ((), (), s32[]{:S(2)}) async-start(), calls=%async_computation.3 | async-start | bytes 18874368 | tf_op jit(solution)/shard_map/reduce_scatter | solution.py:47
  269.7 282.9 %copy-start = (bf16[1024,512]{0,1:T(8,128)(2,1)S(1)}, bf16[1024,512]{0,1:T(8,128)(2,1)}, u32[]{:S(2)}) copy-start(bf16[1024,512]{0,1:T(8,128)(2,1)} %fusion.1) | copy-start | bytes 3145732
  269.8 415.4 %all-reduce.5.cloned.1.call-start = ((), (), s32[]{:S(2)}) async-start(), calls=%async_computation.4 | async-start | bytes 1048576 | tf_op jit(solution)/shard_map/psum | solution.py:53
  552.6 3.8 copy-start.1
Sparse Core Ops, SparseCore 0:
  10.9 127.6 all-gather.1
  143.9 83.6 all-reduce.2
  269.9 282.6 reduce-scatter.1
  558.3 126.8 all-reduce.4
where the time goes:
time: 694 us
  waiting for transfers between devices  622 us (90%)
  matrix products  46.9 us (7%)
  between operations  13.8 us (2%)
  other arithmetic  8.56 us (1%)
    reduce_scatter x1, waiting for transfers between devices, local(): lax.psum_scatter(-jnp.dot(ancestor_inverse, col_block, preferred_element_...  283 us
    all_gather x1, waiting for transfers between devices, local(): row_block = lax.all_gather(masked, 'col', axis=0, tiled=True)  128 us
    psum x1, waiting for transfers between devices, local(): diag_sum = lax.psum(diag_part(masked, own_rows, blk_width), ('row', 'col'))  127 us
    psum x1, waiting for transfers between devices, from_root(): return lax.psum(block, axis)  83.8 us
    dot_general x1, matrix products, local(): jnp.dot(ancestor_inverse, col_block, preferred_element_type=jnp.float32)  42.1 us
  transfers between devices with their start and end apart: 4, of which 4 were waited for; matrix products, arithmetic and copies ran while one was open for 0% of the time, Pallas kernels for 0%

commit v1 on v0

v1 whole, which is shorter than its diff:
```python
import functools
import math

import jax
import jax.numpy as jnp
from jax import lax
from jax.experimental import pallas as pl
from jax.experimental.pallas import tpu as pltpu
from jax.sharding import PartitionSpec as P

AXES = ("row", "col")
F32 = jnp.float32
BF16 = jnp.bfloat16
SCALE_ROWS = 16
VMEM_BYTES = 48 * 1024 * 1024


def encode(values, out_ref):
    rows = values.shape[0]
    top = jnp.max(jnp.abs(values), axis=0, keepdims=True)
    power = jnp.floor(14.9 - jnp.log2(jnp.maximum(top, 1e-37)))
    power = jnp.minimum(jnp.maximum(power, -100.0), 120.0)
    coded = jnp.round(values * jnp.exp2(power)).astype(jnp.int32)
    out_ref[0, :rows, :] = coded.astype(jnp.int16)
    powers = jnp.broadcast_to(power, (SCALE_ROWS, values.shape[1]))
    out_ref[0, rows:, :] = powers.astype(jnp.int32).astype(jnp.int16)


def decode(msg_ref):
    rows = msg_ref.shape[1] - SCALE_ROWS
    power = msg_ref[0, rows:, :].astype(jnp.int32).astype(F32)[:1]
    return msg_ref[0, :rows, :].astype(jnp.int32).astype(F32) * jnp.exp2(-power)


def product_kernel(tiles, parts, info_ref, a_ref, *refs):
    b_refs, (msg_ref, own_ref) = refs[:parts], refs[parts:]
    depth = b_refs[0].shape[0]
    total = None
    for part in range(parts):
        start = pl.multiple_of(info_ref[2 + part] * depth, depth)
        term = jnp.dot(a_ref[:, pl.ds(start, depth)], b_refs[part][...], preferred_element_type=F32)
        total = term if total is None else total + term
    step = pl.program_id(0)

    @pl.when(step < tiles)
    def _():
        encode(total, msg_ref)

    @pl.when(step >= tiles)
    def _():
        own_ref[0] = total


def product(info, ancestor, pieces, tile):
    depth, n = pieces[0].shape
    tiles = depth // tile
    parts = len(pieces)
    width = ancestor.shape[1]

    def a_map(i, info_ref):
        piece = jnp.where(i < tiles, info_ref[0], info_ref[1])
        return piece * tiles + lax.rem(i, tiles), 0

    grid_spec = pltpu.PrefetchScalarGridSpec(
        num_scalar_prefetch=1,
        grid=(2 * tiles,),
        in_specs=[pl.BlockSpec((tile, width), a_map)]
        + [pl.BlockSpec((depth, n), lambda i, info_ref: (0, 0))] * parts,
        out_specs=[
            pl.BlockSpec((1, tile + SCALE_ROWS, n), lambda i, info_ref: (jnp.minimum(i, tiles - 1), 0, 0)),
            pl.BlockSpec((1, tile, n), lambda i, info_ref: (jnp.maximum(i - tiles, 0), 0, 0)),
        ],
    )
    return pl.pallas_call(
        functools.partial(product_kernel, tiles, parts),
        grid_spec=grid_spec,
        out_shape=[
            jax.ShapeDtypeStruct((tiles, tile + SCALE_ROWS, n), jnp.int16),
            jax.ShapeDtypeStruct((tiles, tile, n), F32),
        ],
        compiler_params=pltpu.CompilerParams(vmem_limit_bytes=VMEM_BYTES),
        cost_estimate=pl.CostEstimate(
            flops=4 * depth * width * n,
            bytes_accessed=4 * depth * width + 2 * width * n + 6 * depth * n,
            transcendentals=0,
        ),
        name="product",
    )(info, ancestor, *pieces)


def summed(pairs, moved, which):
    total = pairs[0][0][0] + decode(pairs[0][1])
    for place, (own, msg) in enumerate(pairs[1:], 1):
        total = jnp.where(which == place, own[0] + decode(msg), total)
    for msg in moved:
        total = total + decode(msg)
    return total


def pass_on_kernel(count, which_ref, *refs):
    pairs = [(refs[2 * i], refs[2 * i + 1]) for i in range(count)]
    encode(summed(pairs, refs[2 * count : -1], which_ref[0]), refs[-1])


def tile_spec(array):
    return pl.BlockSpec((1,) + array.shape[1:], lambda i, *_: (i, 0, 0))


def pass_on(which, pairs, moved):
    flat = [x for pair in pairs for x in pair] + moved
    msg = pairs[0][1]
    return pl.pallas_call(
        functools.partial(pass_on_kernel, len(pairs)),
        grid_spec=pltpu.PrefetchScalarGridSpec(
            num_scalar_prefetch=1,
            grid=(msg.shape[0],),
            in_specs=[tile_spec(x) for x in flat],
            out_specs=tile_spec(msg),
        ),
        out_shape=jax.ShapeDtypeStruct(msg.shape, msg.dtype),
        compiler_params=pltpu.CompilerParams(vmem_limit_bytes=VMEM_BYTES),
        cost_estimate=pl.CostEstimate(
            flops=8 * msg.size, bytes_accessed=(2 * len(flat) + 6) * msg.size, transcendentals=0
        ),
        name="pass_on",
    )(which, *flat)


def finish_kernel(moved, own_ref, msg_ref, *refs):
    masked_ref, keep_ref, upper_ref, update_ref = refs[moved:]
    total = summed([(own_ref, msg_ref)], refs[:moved], 0)
    full = -total * keep_ref[...].astype(F32)
    upper_ref[...] = full.astype(BF16)
    first = full.astype(BF16)
    rest = full - first.astype(F32)
    second = rest.astype(BF16)
    third = (rest - second.astype(F32)).astype(BF16)
    width = update_ref.shape[1]

    @pl.when(pl.program_id(0) == 0)
    def _():
        update_ref[...] = jnp.zeros_like(update_ref)

    for k in range(update_ref.shape[0]):
        cut = slice(k * width, (k + 1) * width)
        lower = masked_ref[:, cut]
        for part in (third, second, first):
            update_ref[k] += lax.dot_general(
                lower, part[:, cut], (((0,), (0,)), ((), ())), preferred_element_type=F32
            )


def finish(own, msg, moved, masked, keep, width):
    tiles, tile, n = own.shape
    flat = [own, msg] + moved
    plane = pl.BlockSpec((tile, n), lambda i: (i, 0))
    snodes = n // width
    return pl.pallas_call(
        functools.partial(finish_kernel, len(moved)),
        grid=(tiles,),
        in_specs=[tile_spec(x) for x in flat] + [plane, plane],
        out_specs=[plane, pl.BlockSpec((snodes, width, width), lambda i: (0, 0, 0))],
        out_shape=[
            jax.ShapeDtypeStruct((tiles * tile, n), BF16),
            jax.ShapeDtypeStruct((snodes, width, width), F32),
        ],
        compiler_params=pltpu.CompilerParams(vmem_limit_bytes=VMEM_BYTES),
        cost_estimate=pl.CostEstimate(
            flops=6 * own.size * width, bytes_accessed=16 * own.size, transcendentals=0
        ),
        name="finish",
    )(*flat, masked, keep)


def orders(line):
    table = []
    for place in range(line):
        up, down = line - 1 - place, place
        slots = [None] * line
        slots[line - 1] = place
        long, short = (1, -1) if up >= down else (-1, 1)
        for far in range(1, max(up, down) + 1):
            slots[line - 1 - far] = place + long * far
        free = [q for q in range(line) if slots[q] is None]
        for q, far in zip(free, range(min(up, down), 0, -1)):
            slots[q] = place + short * far
        table.append(slots)
    return table


def make_local(rows, cols):
    line = cols // 2
    table = orders(line)

    def at(row, col):
        return row * cols + col

    def swap_low():
        return [(at(r, c), at(r, c ^ 1)) for r in range(rows) for c in range(cols)]

    def along(step):
        return [
            (at(r, c), at(r, c + 2 * step))
            for r in range(rows)
            for c in range(cols)
            if 0 <= c + 2 * step < cols
        ]

    def swap_rows(bit):
        return [(at(r, c), at(r ^ bit, c)) for r in range(rows) for c in range(cols)]

    def swap_line(bit):
        return [(at(r, c), at(r, c ^ (2 * bit))) for r in range(rows) for c in range(cols)]

    def move(array, pairs):
        return lax.ppermute(array, AXES, pairs)

    ratio = cols // rows
    halves = rows // 2

    def gather_pieces(masked, row_index, col_index):
        source = col_index // ratio
        hop = lax.rem(row_index // 2 - source // 2 + halves, halves)
        mine = []
        for group in range(halves):
            got = None
            for g in range(halves):
                pairs = []
                for r in range(rows):
                    for c in range(cols):
                        part = c % rows
                        if part // 2 == group:
                            to_row = (r // 2 + g) % halves * 2 + part % 2
                            pairs.append((at(r, c), at(to_row, r * ratio + c // rows)))
                new = move(masked, pairs)
                got = new if got is None else jnp.where(hop == g, new, got)
            mine.append(got)
        other = [move(x, swap_rows(1)) for x in mine]
        odd = lax.rem(row_index, 2)
        places = [2 * g + odd for g in range(halves)] + [2 * g + 1 - odd for g in range(halves)]
        return mine + other, places

    def gather_whole(masked, row_index, col_index):
        row_block = lax.all_gather(masked, "col", axis=0, tiled=True)
        span = masked.shape[0] * rows
        own = lax.dynamic_slice_in_dim(row_block, lax.rem(col_index, ratio) * span, span, 0)
        own = jnp.where(row_index == col_index // ratio, own, jnp.zeros_like(own))
        block = lax.psum(own, "row")
        pieces = [block[i * masked.shape[0] : (i + 1) * masked.shape[0]] for i in range(rows)]
        return pieces, [jnp.int32(i) for i in range(rows)]

    gather = gather_pieces if halves * halves <= 4 else gather_whole

    def total_update(update, row_index):
        shape = update.shape
        flat = update.reshape(2, -1, shape[-1])
        odd = lax.rem(row_index, 2)
        keep = lax.dynamic_index_in_dim(flat, odd, 0, keepdims=False)
        give = lax.dynamic_index_in_dim(flat, 1 - odd, 0, keepdims=False)
        keep = keep + move(give, swap_rows(1))
        keep = keep + move(keep, swap_low())
        bit = 2
        while bit < rows:
            keep = keep + move(keep, swap_rows(bit))
            bit *= 2
        bit = 1
        while bit < line:
            keep = keep + move(keep, swap_line(bit))
            bit *= 2
        other = move(keep, swap_rows(1))
        even_part = jnp.where(odd == 0, keep, other)
        odd_part = jnp.where(odd == 0, other, keep)
        return jnp.stack([even_part, odd_part]).reshape(shape)

    def local(ancestor_inverse, panel, structure, diag_inverse):
        snodes, width = diag_inverse.shape[:2]
        depth = panel.shape[0]
        tile = min(512, depth)
        row_index, col_index = lax.axis_index("row"), lax.axis_index("col")
        low, place = lax.rem(col_index, 2), col_index // 2
        begin = (row_index * cols + col_index) * depth
        same = math.gcd(depth, width)
        blocks = depth // same
        owners = (begin + jnp.arange(blocks, dtype=jnp.int32) * same) // width
        keep = jnp.take(structure, owners, axis=1).astype(BF16)
        keep = jnp.broadcast_to(keep.T[:, None, :, None], (blocks, same, snodes, width))
        keep = keep.reshape(depth, snodes * width)
        masked = panel * keep
        order = jnp.asarray(table, jnp.int32)[place]
        uppers, updates = [], []
        for k in range(snodes):
            cut = slice(k * width, (k + 1) * width)
            masked_k, keep_k = masked[:, cut], keep[:, cut]
            pieces, places = gather(masked_k, row_index, col_index)
            own, got = [], []
            for q in range(line):
                info = jnp.stack([order[q] * 2 + 1 - low, order[q] * 2 + low] + places)
                msg, kept = product(info, ancestor_inverse, pieces, tile)
                own.append(kept)
                got.append(move(msg, swap_low()))
            moved = {1: None, -1: None}
            for far in range(line - 1, 0, -1):
                for way in (1, -1):
                    senders = [p for p in range(line) if 0 <= p + way * far < line]
                    slot = {p: table[p].index(p + way * far) for p in senders}
                    slots = sorted(set(slot.values()), reverse=True)
                    choice = [slots.index(slot[p]) if p in slot else 0 for p in range(line)]
                    which = jnp.asarray(choice, jnp.int32)[place][None]
                    before = [] if moved[way] is None else [moved[way]]
                    msg = pass_on(which, [(own[q], got[q]) for q in slots], before)
                    moved[way] = move(msg, along(way))
            arrived = [x for x in moved.values() if x is not None]
            upper, update = finish(own[-1], got[-1], arrived, masked_k, keep_k, width)
            uppers.append(upper)
            updates.append(total_update(update, row_index))
        diagonal = diag_inverse - jnp.concatenate(updates)
        return jnp.concatenate(uppers, axis=1), diagonal

    return local


def solution(mesh):
    return jax.shard_map(
        make_local(mesh.shape["row"], mesh.shape["col"]),
        mesh=mesh,
        in_specs=(P("row", "col"), P(("row", "col"), None), P(), P()),
        out_specs=(P(("row", "col"), None), P()),
        check_vma=False,
    )
```

time: 694 us -> 317 us (0.46)
  waiting for transfers between devices: 622 us -> 67.2 us
  starting transfers between devices: 0.16 us -> 111 us
  Pallas kernels: 0 us -> 108 us
  matrix products: 46.9 us -> 0 us
  local copies, waits for them, and re-layouts: 2.82 us -> 21 us
  between operations: 13.8 us -> 3.97 us
    reduce_scatter x1 -> x0, waiting for transfers between devices: 283 us -> none  [local(): lax.psum_scatter(-jnp.dot(ancestor_inverse, col_block, preferred_element_...]
    psum x2 -> x0, waiting for transfers between devices: 211 us -> none  [the longest x1 127 us: local(): diag_sum = lax.psum(diag_part(masked, own_rows, blk_width), ('row', 'col'))]
    all_gather x1 -> x0, waiting for transfers between devices: 128 us -> none  [local(): row_block = lax.all_gather(masked, 'col', axis=0, tiled=True)]
    ppermute x0 -> x44, starting transfers between devices: none -> 111 us  [move(): return lax.ppermute(array, AXES, pairs)]
    pallas_call x0 -> x20, Pallas kernels: none -> 108 us  [the longest x8 79.8 us: product(): pl.pallas_call(functools.partial(product_kernel, tiles, parts), grid_spec...]
    ppermute x0 -> x44, waiting for transfers between devices: none -> 67.2 us  [move(): return lax.ppermute(array, AXES, pairs)]
    dot_general x3 -> x0, matrix products: 46.9 us -> none  [the longest x1 42.1 us: local(): jnp.dot(ancestor_inverse, col_block, preferred_element_type=jnp.float32)]
    unnamed x6 -> x70, local copies, waits for them, and re-layouts: 2.82 us -> 15.6 us
  transfers between devices with their start and end apart: 4 -> 44, of which waited for: 4 -> 12; matrix products, arithmetic and copies ran while one was open for 0% -> 2% of each run, Pallas kernels for 0% -> 34%
where the time goes in v1:
time: 317 us; the launch traced here: 315 us
  starting transfers between devices  111 us (35%)
  Pallas kernels  108 us (34%)
  waiting for transfers between devices  67.2 us (21%)
  local copies, waits for them, and re-layouts  21 us (7%)
  other arithmetic  4.92 us (2%)
  between operations  3.97 us (1%)
    ppermute x44, starting transfers between devices, move(): return lax.ppermute(array, AXES, pairs)  111 us
    pallas_call x8, Pallas kernels, product(): pl.pallas_call(functools.partial(product_kernel, tiles, parts), grid_spec...  79.8 us
    ppermute x44, waiting for transfers between devices, move(): return lax.ppermute(array, AXES, pairs)  67.2 us
    pallas_call x10, Pallas kernels, pass_on(): pl.pallas_call(functools.partial(pass_on_kernel, len(pairs)), grid_spec=p...  22.5 us
    unnamed x70, local copies, waits for them, and re-layouts  15.6 us
  transfers between devices with their start and end apart: 44, of which 12 were waited for; matrix products, arithmetic and copies ran while one was open for 2% of the time, Pallas kernels for 34%

profile of v1, /device:TPU:0, one launch (start us, length us, event | category | flops | bytes accessed | tf_op | source)
XLA Modules:
  0.0 315.3 jit_solution(4576805532568659927)
XLA Ops:
  4.0 4.9 %collective-permute-start.16 = (bf16[1024,256]{1,0:T(8,128)(2,1)S(1)}, bf16[1024,256]{1,0:T(8,128)(2,1)S(1)}, u32[]{:S(2)}, u32[]{:S(2)}) collective-permute-start(bf16[1024,256]{1,0:T(8,128)(2,1)S(1)} %get-tuple-element.45.refs_2_), channel_id=1, source_target_pairs={{0,16},{1,24},{4,17},{5,25},{8,18},{9,26},{12,19},{13,27},{16,4},{... | collective-permute-start | bytes 1572872 | tf_op jit(solution)/shard_map/ppermute | solution.py:216
  8.9 1.5 collective-permute-start.17
  12.4 7.3 %collective-permute-start = (bf16[1024,256]{1,0:T(8,128)(2,1)S(1)}, bf16[1024,256]{1,0:T(8,128)(2,1)S(1)}, u32[]{:S(2)}, u32[]{:S(2)}) collective-permute-start(bf16[1024,256]{1,0:T(8,128)(2,1)S(1)} %get-tuple-element.44.refs_2_), channel_id=1, source_target_pairs={{0,16},{1,24},{4,17},{5,25},{8,18},{9,26},{12,19},{13,27},{16,4},{... | collective-permute-start | bytes 1572872 | tf_op jit(solution)/shard_map/ppermute | solution.py:216
  23.6 20.0 %collective-permute-done.19 = bf16[1024,256]{1,0:T(8,128)(2,1)S(1)} collective-permute-done((bf16[1024,256]{1,0:T(8,128)(2,1)S(1)}, bf16[1024,256]{1,0:T(8,128)(2,1)S(1)}, u32[]{:S(2)}, u32[]{:S(2)}) %collective-permute-start.19) | collective-permute-done | bytes 524320 | tf_op jit(solution)/shard_map/ppermute | solution.py:216
  46.3 17.0 %collective-permute-done.3 = bf16[1024,256]{1,0:T(8,128)(2,1)S(1)} collective-permute-done((bf16[1024,256]{1,0:T(8,128)(2,1)S(1)}, bf16[1024,256]{1,0:T(8,128)(2,1)S(1)}, u32[]{:S(2)}, u32[]{:S(2)}) %collective-permute-start.3) | collective-permute-done | bytes 524320 | tf_op jit(solution)/shard_map/ppermute | solution.py:216
  63.4 35.5 %collective-permute-start.5 = (bf16[1024,256]{1,0:T(8,128)(2,1)S(1)}, bf16[1024,256]{1,0:T(8,128)(2,1)S(1)}, u32[]{:S(2)}, u32[]{:S(2)}) collective-permute-start(bf16[1024,256]{1,0:T(8,128)(2,1)S(1)} %broadcast_select_fusion.2.refs_1_), channel_id=1, source_target_pairs={{0,8},{1,9},{2,10},{3,11},{4,12},{5,13},{6,14},{7,15},{8,0},{9,1},... | collective-permute-start | bytes 1572872 | tf_op jit(solution)/shard_map/ppermute | solution.py:216
  101.6 10.2 %product.14 = (s16[2,528,256]{2,1,0:T(8,128)(2,1)}, f32[2,512,256]{2,1,0:T(8,128)S(1)}) custom-call(s32[6]{0:T(128)S(1)} %stack.56.info_ref, bf16[8192,4096]{1,0:T(8,128)(2,1)} %a_ref.15, bf16[1024,256]{1,0:T(8,128)(2,1)S(1)} %broadcast_select_fusion.1.refs_0_, bf16[1024,256]{1,0:T(8,128)(2,1)S(1)} %broadcast_select_fusion.refs_1_, ...), custom_call_target="tpu_custom_call" | custom-call | flops 4294967296 | bytes 20447232 | tf_op jit(solution)/shard_map/product/pallas_call | solution.py:74
  112.8 9.6 %collective-permute-start.24 = (s16[2,528,256]{2,1,0:T(8,128)(2,1)}, s16[2,528,256]{2,1,0:T(8,128)(2,1)}, u32[]{:S(2)}, u32[]{:S(2)}) collective-permute-start(s16[2,528,256]{2,1,0:T(8,128)(2,1)} %get-tuple-element.36), channel_id=1, source_target_pairs={{0,1},{1,0},{2,3},{3,2},{4,5},{5,4},{6,7},{7,6},{8,9},{9,8},{10,11... | collective-permute-start | bytes 1622024 | tf_op jit(solution)/shard_map/ppermute | solution.py:216
  126.1 9.9 %product.10 = (s16[2,528,256]{2,1,0:T(8,128)(2,1)}, f32[2,512,256]{2,1,0:T(8,128)S(1)}) custom-call(s32[6]{0:T(128)S(1)} %stack.56.info_ref, bf16[8192,4096]{1,0:T(8,128)(2,1)} %a_ref.15, bf16[1024,256]{1,0:T(8,128)(2,1)S(1)} %broadcast_select_fusion.3.refs_0_, bf16[1024,256]{1,0:T(8,128)(2,1)S(1)} %broadcast_select_fusion.2.refs_1_, ...), custom_call_target="tpu_custom_call" | custom-call | flops 4294967296 | bytes 20447232 | tf_op jit(solution)/shard_map/product/pallas_call | solution.py:74
  136.0 10.2 %product.15 = (s16[2,528,256]{2,1,0:T(8,128)(2,1)}, f32[2,512,256]{2,1,0:T(8,128)S(1)}) custom-call(s32[6]{0:T(128)S(1)} %stack.59.info_ref, bf16[8192,4096]{1,0:T(8,128)(2,1)} %a_ref.15, bf16[1024,256]{1,0:T(8,128)(2,1)S(1)} %broadcast_select_fusion.1.refs_0_, bf16[1024,256]{1,0:T(8,128)(2,1)S(1)} %broadcast_select_fusion.refs_1_, ...), custom_call_target="tpu_custom_call" | custom-call | flops 4294967296 | bytes 20447232 | tf_op jit(solution)/shard_map/product/pallas_call | solution.py:74
  147.2 2.0 collective-permute-start.25
  151.1 2.1 pass_on.17
  153.2 2.9 collective-permute-start.26
  157.4 9.9 %product.11 = (s16[2,528,256]{2,1,0:T(8,128)(2,1)}, f32[2,512,256]{2,1,0:T(8,128)S(1)}) custom-call(s32[6]{0:T(128)S(1)} %stack.59.info_ref, bf16[8192,4096]{1,0:T(8,128)(2,1)} %a_ref.15, bf16[1024,256]{1,0:T(8,128)(2,1)S(1)} %broadcast_select_fusion.3.refs_0_, bf16[1024,256]{1,0:T(8,128)(2,1)S(1)} %broadcast_select_fusion.2.refs_1_, ...), custom_call_target="tpu_custom_call" | custom-call | flops 4294967296 | bytes 20447232 | tf_op jit(solution)/shard_map/product/pallas_call | solution.py:74
  168.4 2.0 pass_on.12
  170.4 5.3 %collective-permute-start.10 = (s16[2,528,256]{2,1,0:T(8,128)(2,1)}, s16[2,528,256]{2,1,0:T(8,128)(2,1)}, u32[]{:S(2)}, u32[]{:S(2)}) collective-permute-start(s16[2,528,256]{2,1,0:T(8,128)(2,1)} %pass_on.12), channel_id=1, source_target_pairs={{0,2},{1,3},{2,4},{3,5},{4,6},{5,7},{8,10},{9,11},{10,12},{11,13},... | collective-permute-start | bytes 1622024 | tf_op jit(solution)/shard_map/ppermute | solution.py:216
  177.0 10.2 %product.13 = (s16[2,528,256]{2,1,0:T(8,128)(2,1)}, f32[2,512,256]{2,1,0:T(8,128)S(1)}) custom-call(s32[6]{0:T(128)S(1)} %stack.53.info_ref, bf16[8192,4096]{1,0:T(8,128)(2,1)} %a_ref.15, bf16[1024,256]{1,0:T(8,128)(2,1)S(1)} %broadcast_select_fusion.1.refs_0_, bf16[1024,256]{1,0:T(8,128)(2,1)S(1)} %broadcast_select_fusion.refs_1_, ...), custom_call_target="tpu_custom_call" | custom-call | flops 4294967296 | bytes 20447232 | tf_op jit(solution)/shard_map/product/pallas_call | solution.py:74
  188.2 2.0 collective-permute-start.23
  192.2 1.6 pass_on.18
  193.8 4.6 %collective-permute-start.27 = (s16[2,528,256]{2,1,0:T(8,128)(2,1)S(1)}, s16[2,528,256]{2,1,0:T(8,128)(2,1)S(1)}, u32[]{:S(2)}, u32[]{:S(2)}) collective-permute-start(s16[2,528,256]{2,1,0:T(8,128)(2,1)S(1)} %pass_on.18), channel_id=1, source_target_pairs={{0,2},{1,3},{2,4},{3,5},{4,6},{5,7},{8,10},{9,11},{10,12},{11,13},... | collective-permute-start | bytes 1622024 | tf_op jit(solution)/shard_map/ppermute | solution.py:216
  198.4 1.5 pass_on.20
  199.9 1.6 collective-permute-start.30
  201.6 9.9 %product.9 = (s16[2,528,256]{2,1,0:T(8,128)(2,1)}, f32[2,512,256]{2,1,0:T(8,128)S(1)}) custom-call(s32[6]{0:T(128)S(1)} %stack.53.info_ref, bf16[8192,4096]{1,0:T(8,128)(2,1)} %a_ref.15, bf16[1024,256]{1,0:T(8,128)(2,1)S(1)} %broadcast_select_fusion.3.refs_0_, bf16[1024,256]{1,0:T(8,128)(2,1)S(1)} %broadcast_select_fusion.2.refs_1_, ...), custom_call_target="tpu_custom_call" | custom-call | flops 4294967296 | bytes 20447232 | tf_op jit(solution)/shard_map/product/pallas_call | solution.py:74
  211.5 1.5 pass_on.13
  213.1 4.6 %collective-permute-start.11 = (s16[2,528,256]{2,1,0:T(8,128)(2,1)S(1)}, s16[2,528,256]{2,1,0:T(8,128)(2,1)S(1)}, u32[]{:S(2)}, u32[]{:S(2)}) collective-permute-start(s16[2,528,256]{2,1,0:T(8,128)(2,1)S(1)} %pass_on.13), channel_id=1, source_target_pairs={{0,2},{1,3},{2,4},{3,5},{4,6},{5,7},{8,10},{9,11},{10,12},{11,13},... | collective-permute-start | bytes 1622024 | tf_op jit(solution)/shard_map/ppermute | solution.py:216
  217.6 1.5 pass_on.15
  219.2 1.4 collective-permute-start.14
  220.7 9.5 %product.12 = (s16[2,528,256]{2,1,0:T(8,128)(2,1)S(1)}, f32[2,512,256]{2,1,0:T(8,128)S(1)}) custom-call(s32[6]{0:T(128)S(1)} %stack.50.info_ref, bf16[8192,4096]{1,0:T(8,128)(2,1)} %a_ref.15, bf16[1024,256]{1,0:T(8,128)(2,1)S(1)} %broadcast_select_fusion.1.refs_0_, bf16[1024,256]{1,0:T(8,128)(2,1)S(1)} %broadcast_select_fusion.refs_1_, ...), custom_call_target="tpu_custom_call" | custom-call | flops 4294967296 | bytes 20447232 | tf_op jit(solution)/shard_map/product/pallas_call | solution.py:74
  231.1 2.0 collective-permute-start.22
  234.4 3.0 pass_on.19
  237.4 5.4 %collective-permute-start.28 = (s16[2,528,256]{2,1,0:T(8,128)(2,1)}, s16[2,528,256]{2,1,0:T(8,128)(2,1)}, u32[]{:S(2)}, u32[]{:S(2)}) collective-permute-start(s16[2,528,256]{2,1,0:T(8,128)(2,1)} %pass_on.19), channel_id=1, source_target_pairs={{0,2},{1,3},{2,4},{3,5},{4,6},{5,7},{8,10},{9,11},{10,12},{11,13},... | collective-permute-start | bytes 1622024 | tf_op jit(solution)/shard_map/ppermute | solution.py:216
  242.8 3.1 pass_on.21
  247.2 9.9 %product.8 = (s16[2,528,256]{2,1,0:T(8,128)(2,1)}, f32[2,512,256]{2,1,0:T(8,128)S(1)}) custom-call(s32[6]{0:T(128)S(1)} %stack.50.info_ref, bf16[8192,4096]{1,0:T(8,128)(2,1)} %a_ref.15, bf16[1024,256]{1,0:T(8,128)(2,1)S(1)} %broadcast_select_fusion.3.refs_0_, bf16[1024,256]{1,0:T(8,128)(2,1)S(1)} %broadcast_select_fusion.2.refs_1_, ...), custom_call_target="tpu_custom_call" | custom-call | flops 4294967296 | bytes 20447232 | tf_op jit(solution)/shard_map/product/pallas_call | solution.py:74
  257.2 3.0 pass_on.14
  260.2 5.4 %collective-permute-start.12 = (s16[2,528,256]{2,1,0:T(8,128)(2,1)}, s16[2,528,256]{2,1,0:T(8,128)(2,1)}, u32[]{:S(2)}, u32[]{:S(2)}) collective-permute-start(s16[2,528,256]{2,1,0:T(8,128)(2,1)} %pass_on.14), channel_id=1, source_target_pairs={{0,2},{1,3},{2,4},{3,5},{4,6},{5,7},{8,10},{9,11},{10,12},{11,13},... | collective-permute-start | bytes 1622024 | tf_op jit(solution)/shard_map/ppermute | solution.py:216
  265.6 3.0 pass_on.16
  273.2 2.6 finish.3
  276.0 4.9 %collective-permute-done.15.refs_1_ = s16[2,528,256]{2,1,0:T(8,128)(2,1)S(1)} collective-permute-done((s16[2,528,256]{2,1,0:T(8,128)(2,1)}, s16[2,528,256]{2,1,0:T(8,128)(2,1)S(1)}, u32[]{:S(2)}, u32[]{:S(2)}) %collective-permute-start.15) | collective-permute-done | bytes 540704 | tf_op jit(solution)/shard_map/ppermute | solution.py:216
  280.9 2.6 finish.2
  283.6 2.0 collective-permute-start.39
  285.7 1.3 collective-permute-start.33
  287.0 3.1 collective-permute-done.39
  290.2 2.5 collective-permute-done.33
  292.7 2.4 collective-permute-done.40
  295.3 2.7 collective-permute-done.34
  298.1 2.8 collective-permute-done.41
  300.9 3.5 %collective-permute-done.35 = f32[128,256]{1,0:T(8,128)S(1)} collective-permute-done((f32[128,256]{1,0:T(8,128)S(1)}, f32[128,256]{1,0:T(8,128)S(1)}, u32[]{:S(2)}, u32[]{:S(2)}) %collective-permute-start.35) | collective-permute-done | bytes 131104 | tf_op jit(solution)/shard_map/ppermute | solution.py:216
  304.5 6.9 %collective-permute-done.42 = f32[128,256]{1,0:T(8,128)S(1)} collective-permute-done((f32[128,256]{1,0:T(8,128)S(1)}, f32[128,256]{1,0:T(8,128)S(1)}, u32[]{:S(2)}, u32[]{:S(2)}) %collective-permute-start.42) | collective-permute-done | bytes 131104 | tf_op jit(solution)/shard_map/ppermute | solution.py:216
  (169 shorter events, 38.8 us)
Async XLA Ops:
  4.0 42.1 %copy-start.19 = (bf16[1024,256]{1,0:T(8,128)(2,1)}, bf16[1024,256]{1,0:T(8,128)(2,1)S(1)}, u32[]{:S(2)}) copy-start(bf16[1024,256]{1,0:T(8,128)(2,1)S(1)} %get-tuple-element.45.refs_2_) | copy-start | bytes 1572868
  4.0 42.2 %copy-start.17 = (bf16[1024,256]{1,0:T(8,128)(2,1)}, bf16[1024,256]{1,0:T(8,128)(2,1)S(1)}, u32[]{:S(2)}) copy-start(bf16[1024,256]{1,0:T(8,128)(2,1)S(1)} %get-tuple-element.44.refs_2_) | copy-start | bytes 1572868
  4.0 15.7 %collective-permute-start.16 = (bf16[1024,256]{1,0:T(8,128)(2,1)S(1)}, bf16[1024,256]{1,0:T(8,128)(2,1)S(1)}, u32[]{:S(2)}, u32[]{:S(2)}) collective-permute-start(bf16[1024,256]{1,0:T(8,128)(2,1)S(1)} %get-tuple-element.45.refs_2_), channel_id=1, source_target_pairs={{0,16},{1,24},{4,17},{5,25},{8,18},{9,26},{12,19},{13,27},{16,4},{... | collective-permute-start | bytes 1572872 | tf_op jit(solution)/shard_map/ppermute | solution.py:216
  8.9 11.5 %collective-permute-start.17 = (bf16[1024,256]{1,0:T(8,128)(2,1)S(1)}, bf16[1024,256]{1,0:T(8,128)(2,1)}, u32[]{:S(2)}, u32[]{:S(2)}) collective-permute-start(bf16[1024,256]{1,0:T(8,128)(2,1)S(1)} %get-tuple-element.45.refs_2_), channel_id=1, source_target_pairs={{0,0},{1,8},{4,1},{5,9},{8,2},{9,10},{12,3},{13,11},{16,20},{17,28... | collective-permute-start | bytes 1572872 | tf_op jit(solution)/shard_map/ppermute | solution.py:216
  10.4 11.9 %collective-permute-start.18 = (bf16[1024,256]{1,0:T(8,128)(2,1)S(1)}, bf16[1024,256]{1,0:T(8,128)(2,1)S(1)}, u32[]{:S(2)}, u32[]{:S(2)}) collective-permute-start(bf16[1024,256]{1,0:T(8,128)(2,1)S(1)} %get-tuple-element.45.refs_2_), channel_id=1, source_target_pairs={{2,16},{3,24},{6,17},{7,25},{10,18},{11,26},{14,19},{15,27},{18,4}... | collective-permute-start | bytes 1572872 | tf_op jit(solution)/shard_map/ppermute | solution.py:216
  11.1 32.6 %collective-permute-start.19 = (bf16[1024,256]{1,0:T(8,128)(2,1)S(1)}, bf16[1024,256]{1,0:T(8,128)(2,1)S(1)}, u32[]{:S(2)}, u32[]{:S(2)}) collective-permute-start(bf16[1024,256]{1,0:T(8,128)(2,1)S(1)} %get-tuple-element.45.refs_2_), channel_id=1, source_target_pairs={{2,0},{3,8},{6,1},{7,9},{10,2},{11,10},{14,3},{15,11},{18,20},{19,... | collective-permute-start | bytes 1572872 | tf_op jit(solution)/shard_map/ppermute | solution.py:216
  12.4 33.2 %collective-permute-start = (bf16[1024,256]{1,0:T(8,128)(2,1)S(1)}, bf16[1024,256]{1,0:T(8,128)(2,1)S(1)}, u32[]{:S(2)}, u32[]{:S(2)}) collective-permute-start(bf16[1024,256]{1,0:T(8,128)(2,1)S(1)} %get-tuple-element.44.refs_2_), channel_id=1, source_target_pairs={{0,16},{1,24},{4,17},{5,25},{8,18},{9,26},{12,19},{13,27},{16,4},{... | collective-permute-start | bytes 1572872 | tf_op jit(solution)/shard_map/ppermute | solution.py:216
  19.7 26.4 %collective-permute-start.1 = (bf16[1024,256]{1,0:T(8,128)(2,1)S(1)}, bf16[1024,256]{1,0:T(8,128)(2,1)S(1)}, u32[]{:S(2)}, u32[]{:S(2)}) collective-permute-start(bf16[1024,256]{1,0:T(8,128)(2,1)S(1)} %get-tuple-element.44.refs_2_), channel_id=1, source_target_pairs={{0,0},{1,8},{4,1},{5,9},{8,2},{9,10},{12,3},{13,11},{16,20},{17,28... | collective-permute-start | bytes 1572872 | tf_op jit(solution)/shard_map/ppermute | solution.py:216
  20.5 25.8 %collective-permute-start.2 = (bf16[1024,256]{1,0:T(8,128)(2,1)S(1)}, bf16[1024,256]{1,0:T(8,128)(2,1)S(1)}, u32[]{:S(2)}, u32[]{:S(2)}) collective-permute-start(bf16[1024,256]{1,0:T(8,128)(2,1)S(1)} %get-tuple-element.44.refs_2_), channel_id=1, source_target_pairs={{2,16},{3,24},{6,17},{7,25},{10,18},{11,26},{14,19},{15,27},{18,4}... | collective-permute-start | bytes 1572872 | tf_op jit(solution)/shard_map/ppermute | solution.py:216
  22.3 41.0 %collective-permute-start.3 = (bf16[1024,256]{1,0:T(8,128)(2,1)S(1)}, bf16[1024,256]{1,0:T(8,128)(2,1)S(1)}, u32[]{:S(2)}, u32[]{:S(2)}) collective-permute-start(bf16[1024,256]{1,0:T(8,128)(2,1)S(1)} %get-tuple-element.44.refs_2_), channel_id=1, source_target_pairs={{2,0},{3,8},{6,1},{7,9},{10,2},{11,10},{14,3},{15,11},{18,20},{19,... | collective-permute-start | bytes 1572872 | tf_op jit(solution)/shard_map/ppermute | solution.py:216
  44.4 57.2 %collective-permute-start.20 = (bf16[1024,256]{1,0:T(8,128)(2,1)S(1)}, bf16[1024,256]{1,0:T(8,128)(2,1)}, u32[]{:S(2)}, u32[]{:S(2)}) collective-permute-start(bf16[1024,256]{1,0:T(8,128)(2,1)S(1)} %broadcast_select_fusion.1.refs_0_), channel_id=1, source_target_pairs={{0,8},{1,9},{2,10},{3,11},{4,12},{5,13},{6,14},{7,15},{8,0},{9,1},... | collective-permute-start | bytes 1572872 | tf_op jit(solution)/shard_map/ppermute | solution.py:216
  45.6 56.1 %collective-permute-start.21 = (bf16[1024,256]{1,0:T(8,128)(2,1)S(1)}, bf16[1024,256]{1,0:T(8,128)(2,1)}, u32[]{:S(2)}, u32[]{:S(2)}) collective-permute-start(bf16[1024,256]{1,0:T(8,128)(2,1)S(1)} %broadcast_select_fusion.refs_1_), channel_id=1, source_target_pairs={{0,8},{1,9},{2,10},{3,11},{4,12},{5,13},{6,14},{7,15},{8,0},{9,1},... | collective-permute-start | bytes 1572872 | tf_op jit(solution)/shard_map/ppermute | solution.py:216
  46.2 76.2 %collective-permute-start.4 = (bf16[1024,256]{1,0:T(8,128)(2,1)S(1)}, bf16[1024,256]{1,0:T(8,128)(2,1)S(1)}, u32[]{:S(2)}, u32[]{:S(2)}) collective-permute-start(bf16[1024,256]{1,0:T(8,128)(2,1)S(1)} %broadcast_select_fusion.3.refs_0_), channel_id=1, source_target_pairs={{0,8},{1,9},{2,10},{3,11},{4,12},{5,13},{6,14},{7,15},{8,0},{9,1},... | collective-permute-start | bytes 1572872 | tf_op jit(solution)/shard_map/ppermute | solution.py:216
  63.4 59.9 %collective-permute-start.5 = (bf16[1024,256]{1,0:T(8,128)(2,1)S(1)}, bf16[1024,256]{1,0:T(8,128)(2,1)S(1)}, u32[]{:S(2)}, u32[]{:S(2)}) collective-permute-start(bf16[1024,256]{1,0:T(8,128)(2,1)S(1)} %broadcast_select_fusion.2.refs_1_), channel_id=1, source_target_pairs={{0,8},{1,9},{2,10},{3,11},{4,12},{5,13},{6,14},{7,15},{8,0},{9,1},... | collective-permute-start | bytes 1572872 | tf_op jit(solution)/shard_map/ppermute | solution.py:216
  112.8 37.1 %collective-permute-start.24 = (s16[2,528,256]{2,1,0:T(8,128)(2,1)}, s16[2,528,256]{2,1,0:T(8,128)(2,1)}, u32[]{:S(2)}, u32[]{:S(2)}) collective-permute-start(s16[2,528,256]{2,1,0:T(8,128)(2,1)} %get-tuple-element.36), channel_id=1, source_target_pairs={{0,1},{1,0},{2,3},{3,2},{4,5},{5,4},{6,7},{7,6},{8,9},{9,8},{10,11... | collective-permute-start | bytes 1622024 | tf_op jit(solution)/shard_map/ppermute | solution.py:216
  136.0 32.3 %collective-permute-start.8 = (s16[2,528,256]{2,1,0:T(8,128)(2,1)}, s16[2,528,256]{2,1,0:T(8,128)(2,1)}, u32[]{:S(2)}, u32[]{:S(2)}) collective-permute-start(s16[2,528,256]{2,1,0:T(8,128)(2,1)} %get-tuple-element.27), channel_id=1, source_target_pairs={{0,1},{1,0},{2,3},{3,2},{4,5},{5,4},{6,7},{7,6},{8,9},{9,8},{10,11... | collective-permute-start | bytes 1622024 | tf_op jit(solution)/shard_map/ppermute | solution.py:216
  147.2 28.5 %collective-permute-start.25 = (s16[2,528,256]{2,1,0:T(8,128)(2,1)}, s16[2,528,256]{2,1,0:T(8,128)(2,1)}, u32[]{:S(2)}, u32[]{:S(2)}) collective-permute-start(s16[2,528,256]{2,1,0:T(8,128)(2,1)} %get-tuple-element.38), channel_id=1, source_target_pairs={{0,1},{1,0},{2,3},{3,2},{4,5},{5,4},{6,7},{7,6},{8,9},{9,8},{10,11... | collective-permute-start | bytes 1622024 | tf_op jit(solution)/shard_map/ppermute | solution.py:216
  153.2 35.0 %collective-permute-start.26 = (s16[2,528,256]{2,1,0:T(8,128)(2,1)}, s16[2,528,256]{2,1,0:T(8,128)(2,1)}, u32[]{:S(2)}, u32[]{:S(2)}) collective-permute-start(s16[2,528,256]{2,1,0:T(8,128)(2,1)} %pass_on.17), channel_id=1, source_target_pairs={{0,2},{1,3},{2,4},{3,5},{4,6},{5,7},{8,10},{9,11},{10,12},{11,13},... | collective-permute-start | bytes 1622024 | tf_op jit(solution)/shard_map/ppermute | solution.py:216
  156.1 37.7 %collective-permute-start.29 = (s16[2,528,256]{2,1,0:T(8,128)(2,1)}, s16[2,528,256]{2,1,0:T(8,128)(2,1)}, u32[]{:S(2)}, u32[]{:S(2)}) collective-permute-start(s16[2,528,256]{2,1,0:T(8,128)(2,1)} %pass_on.17), channel_id=1, source_target_pairs={{2,0},{3,1},{4,2},{5,3},{6,4},{7,5},{10,8},{11,9},{12,10},{13,11},... | collective-permute-start | bytes 1622024 | tf_op jit(solution)/shard_map/ppermute | solution.py:216
  168.3 31.7 %collective-permute-start.9 = (s16[2,528,256]{2,1,0:T(8,128)(2,1)}, s16[2,528,256]{2,1,0:T(8,128)(2,1)}, u32[]{:S(2)}, u32[]{:S(2)}) collective-permute-start(s16[2,528,256]{2,1,0:T(8,128)(2,1)} %get-tuple-element.29), channel_id=1, source_target_pairs={{0,1},{1,0},{2,3},{3,2},{4,5},{5,4},{6,7},{7,6},{8,9},{9,8},{10,11... | collective-permute-start | bytes 1622024 | tf_op jit(solution)/shard_map/ppermute | solution.py:216
  170.4 41.1 %collective-permute-start.10 = (s16[2,528,256]{2,1,0:T(8,128)(2,1)}, s16[2,528,256]{2,1,0:T(8,128)(2,1)}, u32[]{:S(2)}, u32[]{:S(2)}) collective-permute-start(s16[2,528,256]{2,1,0:T(8,128)(2,1)} %pass_on.12), channel_id=1, source_target_pairs={{0,2},{1,3},{2,4},{3,5},{4,6},{5,7},{8,10},{9,11},{10,12},{11,13},... | collective-permute-start | bytes 1622024 | tf_op jit(solution)/shard_map/ppermute | solution.py:216
  175.7 37.3 %collective-permute-start.13 = (s16[2,528,256]{2,1,0:T(8,128)(2,1)}, s16[2,528,256]{2,1,0:T(8,128)(2,1)}, u32[]{:S(2)}, u32[]{:S(2)}) collective-permute-start(s16[2,528,256]{2,1,0:T(8,128)(2,1)} %pass_on.12), channel_id=1, source_target_pairs={{2,0},{3,1},{4,2},{5,3},{6,4},{7,5},{10,8},{11,9},{12,10},{13,11},... | collective-permute-start | bytes 1622024 | tf_op jit(solution)/shard_map/ppermute | solution.py:216
  188.2 31.0 %collective-permute-start.23 = (s16[2,528,256]{2,1,0:T(8,128)(2,1)}, s16[2,528,256]{2,1,0:T(8,128)(2,1)}, u32[]{:S(2)}, u32[]{:S(2)}) collective-permute-start(s16[2,528,256]{2,1,0:T(8,128)(2,1)} %get-tuple-element.34), channel_id=1, source_target_pairs={{0,1},{1,0},{2,3},{3,2},{4,5},{5,4},{6,7},{7,6},{8,9},{9,8},{10,11... | collective-permute-start | bytes 1622024 | tf_op jit(solution)/shard_map/ppermute | solution.py:216
  193.8 37.3 %collective-permute-start.27 = (s16[2,528,256]{2,1,0:T(8,128)(2,1)S(1)}, s16[2,528,256]{2,1,0:T(8,128)(2,1)S(1)}, u32[]{:S(2)}, u32[]{:S(2)}) collective-permute-start(s16[2,528,256]{2,1,0:T(8,128)(2,1)S(1)} %pass_on.18), channel_id=1, source_target_pairs={{0,2},{1,3},{2,4},{3,5},{4,6},{5,7},{8,10},{9,11},{10,12},{11,13},... | collective-permute-start | bytes 1622024 | tf_op jit(solution)/shard_map/ppermute | solution.py:216
  199.9 37.5 %collective-permute-start.30 = (s16[2,528,256]{2,1,0:T(8,128)(2,1)S(1)}, s16[2,528,256]{2,1,0:T(8,128)(2,1)S(1)}, u32[]{:S(2)}, u32[]{:S(2)}) collective-permute-start(s16[2,528,256]{2,1,0:T(8,128)(2,1)S(1)} %pass_on.20), channel_id=1, source_target_pairs={{2,0},{3,1},{4,2},{5,3},{6,4},{7,5},{10,8},{11,9},{12,10},{13,11},... | collective-permute-start | bytes 1622024 | tf_op jit(solution)/shard_map/ppermute | solution.py:216
  211.5 34.4 %collective-permute-start.7 = (s16[2,528,256]{2,1,0:T(8,128)(2,1)}, s16[2,528,256]{2,1,0:T(8,128)(2,1)S(1)}, u32[]{:S(2)}, u32[]{:S(2)}) collective-permute-start(s16[2,528,256]{2,1,0:T(8,128)(2,1)} %get-tuple-element.25), channel_id=1, source_target_pairs={{0,1},{1,0},{2,3},{3,2},{4,5},{5,4},{6,7},{7,6},{8,9},{9,8},{10,11... | collective-permute-start | bytes 1622024 | tf_op jit(solution)/shard_map/ppermute | solution.py:216
  213.1 44.1 %collective-permute-start.11 = (s16[2,528,256]{2,1,0:T(8,128)(2,1)S(1)}, s16[2,528,256]{2,1,0:T(8,128)(2,1)S(1)}, u32[]{:S(2)}, u32[]{:S(2)}) collective-permute-start(s16[2,528,256]{2,1,0:T(8,128)(2,1)S(1)} %pass_on.13), channel_id=1, source_target_pairs={{0,2},{1,3},{2,4},{3,5},{4,6},{5,7},{8,10},{9,11},{10,12},{11,13},... | collective-permute-start | bytes 1622024 | tf_op jit(solution)/shard_map/ppermute | solution.py:216
  219.2 15.2 %copy-start.2 = (f32[2,512,256]{2,1,0:T(8,128)S(1)}, f32[2,512,256]{2,1,0:T(8,128)}, u32[]{:S(2)}) copy-start(f32[2,512,256]{2,1,0:T(8,128)} %copy-done) | copy-start | bytes 3145732
  219.2 15.2 %copy-start.12 = (f32[2,512,256]{2,1,0:T(8,128)S(1)}, f32[2,512,256]{2,1,0:T(8,128)}, u32[]{:S(2)}) copy-start(f32[2,512,256]{2,1,0:T(8,128)} %copy-done.11) | copy-start | bytes 3145732
  219.2 41.0 %collective-permute-start.14 = (s16[2,528,256]{2,1,0:T(8,128)(2,1)S(1)}, s16[2,528,256]{2,1,0:T(8,128)(2,1)S(1)}, u32[]{:S(2)}, u32[]{:S(2)}) collective-permute-start(s16[2,528,256]{2,1,0:T(8,128)(2,1)S(1)} %pass_on.15), channel_id=1, source_target_pairs={{2,0},{3,1},{4,2},{5,3},{6,4},{7,5},{10,8},{11,9},{12,10},{13,11},... | collective-permute-start | bytes 1622024 | tf_op jit(solution)/shard_map/ppermute | solution.py:216
  231.1 37.5 %collective-permute-start.22 = (s16[2,528,256]{2,1,0:T(8,128)(2,1)S(1)}, s16[2,528,256]{2,1,0:T(8,128)(2,1)S(1)}, u32[]{:S(2)}, u32[]{:S(2)}) collective-permute-start(s16[2,528,256]{2,1,0:T(8,128)(2,1)S(1)} %get-tuple-element.32), channel_id=1, source_target_pairs={{0,1},{1,0},{2,3},{3,2},{4,5},{5,4},{6,7},{7,6},{8,9},{9,8},{10,11... | collective-permute-start | bytes 1622024 | tf_op jit(solution)/shard_map/ppermute | solution.py:216
  237.4 34.6 %collective-permute-start.28 = (s16[2,528,256]{2,1,0:T(8,128)(2,1)}, s16[2,528,256]{2,1,0:T(8,128)(2,1)}, u32[]{:S(2)}, u32[]{:S(2)}) collective-permute-start(s16[2,528,256]{2,1,0:T(8,128)(2,1)} %pass_on.19), channel_id=1, source_target_pairs={{0,2},{1,3},{2,4},{3,5},{4,6},{5,7},{8,10},{9,11},{10,12},{11,13},... | collective-permute-start | bytes 1622024 | tf_op jit(solution)/shard_map/ppermute | solution.py:216
  245.9 26.1 %collective-permute-start.31 = (s16[2,528,256]{2,1,0:T(8,128)(2,1)}, s16[2,528,256]{2,1,0:T(8,128)(2,1)}, u32[]{:S(2)}, u32[]{:S(2)}) collective-permute-start(s16[2,528,256]{2,1,0:T(8,128)(2,1)} %pass_on.21), channel_id=1, source_target_pairs={{2,0},{3,1},{4,2},{5,3},{6,4},{7,5},{10,8},{11,9},{12,10},{13,11},... | collective-permute-start | bytes 1622024 | tf_op jit(solution)/shard_map/ppermute | solution.py:216
  257.1 18.8 %collective-permute-start.6 = (s16[2,528,256]{2,1,0:T(8,128)(2,1)}, s16[2,528,256]{2,1,0:T(8,128)(2,1)}, u32[]{:S(2)}, u32[]{:S(2)}) collective-permute-start(s16[2,528,256]{2,1,0:T(8,128)(2,1)} %get-tuple-element.23), channel_id=1, source_target_pairs={{0,1},{1,0},{2,3},{3,2},{4,5},{5,4},{6,7},{7,6},{8,9},{9,8},{10,11... | collective-permute-start | bytes 1622024 | tf_op jit(solution)/shard_map/ppermute | solution.py:216
  260.2 15.7 %collective-permute-start.12 = (s16[2,528,256]{2,1,0:T(8,128)(2,1)}, s16[2,528,256]{2,1,0:T(8,128)(2,1)}, u32[]{:S(2)}, u32[]{:S(2)}) collective-permute-start(s16[2,528,256]{2,1,0:T(8,128)(2,1)} %pass_on.14), channel_id=1, source_target_pairs={{0,2},{1,3},{2,4},{3,5},{4,6},{5,7},{8,10},{9,11},{10,12},{11,13},... | collective-permute-start | bytes 1622024 | tf_op jit(solution)/shard_map/ppermute | solution.py:216
  269.4 11.4 %collective-permute-start.15 = (s16[2,528,256]{2,1,0:T(8,128)(2,1)}, s16[2,528,256]{2,1,0:T(8,128)(2,1)S(1)}, u32[]{:S(2)}, u32[]{:S(2)}) collective-permute-start(s16[2,528,256]{2,1,0:T(8,128)(2,1)} %pass_on.16), channel_id=1, source_target_pairs={{2,0},{3,1},{4,2},{5,3},{6,4},{7,5},{10,8},{11,9},{12,10},{13,11},... | collective-permute-start | bytes 1622024 | tf_op jit(solution)/shard_map/ppermute | solution.py:216
  275.9 7.7 %collective-permute-start.38 = (f32[128,256]{1,0:T(8,128)S(1)}, f32[128,256]{1,0:T(8,128)S(1)}, u32[]{:S(2)}, u32[]{:S(2)}) collective-permute-start(f32[128,256]{1,0:T(8,128)S(1)} %dynamic-slice_bitcast_fusion), channel_id=1, source_target_pairs={{0,8},{1,9},{2,10},{3,11},{4,12},{5,13},{6,14},{7,15},{8,0},{9,1},... | collective-permute-start | bytes 393224 | tf_op jit(solution)/shard_map/ppermute | solution.py:216
  283.5 2.2 collective-permute-start.32
  283.6 6.4 %collective-permute-start.39 = (f32[128,256]{1,0:T(8,128)S(1)}, f32[128,256]{1,0:T(8,128)S(1)}, u32[]{:S(2)}, u32[]{:S(2)}) collective-permute-start(f32[128,256]{1,0:T(8,128)S(1)} %bitcast_add_fusion), channel_id=1, source_target_pairs={{0,1},{1,0},{2,3},{3,2},{4,5},{5,4},{6,7},{7,6},{8,9},{9,8},{10,11... | collective-permute-start | bytes 393224 | tf_op jit(solution)/shard_map/ppermute | solution.py:216
  285.7 6.9 %collective-permute-start.33 = (f32[128,256]{1,0:T(8,128)S(1)}, f32[128,256]{1,0:T(8,128)S(1)}, u32[]{:S(2)}, u32[]{:S(2)}) collective-permute-start(f32[128,256]{1,0:T(8,128)S(1)} %bitcast_add_fusion.1), channel_id=1, source_target_pairs={{0,1},{1,0},{2,3},{3,2},{4,5},{5,4},{6,7},{7,6},{8,9},{9,8},{10,11... | collective-permute-start | bytes 393224 | tf_op jit(solution)/shard_map/ppermute | solution.py:216
  290.1 5.1 %collective-permute-start.40 = (f32[128,256]{1,0:T(8,128)S(1)}, f32[128,256]{1,0:T(8,128)S(1)}, u32[]{:S(2)}, u32[]{:S(2)}) collective-permute-start(f32[128,256]{1,0:T(8,128)S(1)} %add.165), channel_id=1, source_target_pairs={{0,16},{1,17},{2,18},{3,19},{4,20},{5,21},{6,22},{7,23},{8,24},{9,... | collective-permute-start | bytes 393224 | tf_op jit(solution)/shard_map/ppermute | solution.py:216
  292.6 5.3 %collective-permute-start.34 = (f32[128,256]{1,0:T(8,128)S(1)}, f32[128,256]{1,0:T(8,128)S(1)}, u32[]{:S(2)}, u32[]{:S(2)}) collective-permute-start(f32[128,256]{1,0:T(8,128)S(1)} %add.160), channel_id=1, source_target_pairs={{0,16},{1,17},{2,18},{3,19},{4,20},{5,21},{6,22},{7,23},{8,24},{9,... | collective-permute-start | bytes 393224 | tf_op jit(solution)/shard_map/ppermute | solution.py:216
  295.2 5.6 %collective-permute-start.41 = (f32[128,256]{1,0:T(8,128)S(1)}, f32[128,256]{1,0:T(8,128)S(1)}, u32[]{:S(2)}, u32[]{:S(2)}) collective-permute-start(f32[128,256]{1,0:T(8,128)S(1)} %add.166), channel_id=1, source_target_pairs={{0,2},{1,3},{2,0},{3,1},{4,6},{5,7},{6,4},{7,5},{8,10},{9,11},{10,... | collective-permute-start | bytes 393224 | tf_op jit(solution)/shard_map/ppermute | solution.py:216
  298.0 6.4 %collective-permute-start.35 = (f32[128,256]{1,0:T(8,128)S(1)}, f32[128,256]{1,0:T(8,128)S(1)}, u32[]{:S(2)}, u32[]{:S(2)}) collective-permute-start(f32[128,256]{1,0:T(8,128)S(1)} %add.161), channel_id=1, source_target_pairs={{0,2},{1,3},{2,0},{3,1},{4,6},{5,7},{6,4},{7,5},{8,10},{9,11},{10,... | collective-permute-start | bytes 393224 | tf_op jit(solution)/shard_map/ppermute | solution.py:216
  300.8 10.6 %collective-permute-start.42 = (f32[128,256]{1,0:T(8,128)S(1)}, f32[128,256]{1,0:T(8,128)S(1)}, u32[]{:S(2)}, u32[]{:S(2)}) collective-permute-start(f32[128,256]{1,0:T(8,128)S(1)} %add.167), channel_id=1, source_target_pairs={{0,4},{1,5},{2,6},{3,7},{4,0},{5,1},{6,2},{7,3},{8,12},{9,13},{10,... | collective-permute-start | bytes 393224 | tf_op jit(solution)/shard_map/ppermute | solution.py:216
  304.4 8.4 %collective-permute-start.36 = (f32[128,256]{1,0:T(8,128)S(1)}, f32[128,256]{1,0:T(8,128)S(1)}, u32[]{:S(2)}, u32[]{:S(2)}) collective-permute-start(f32[128,256]{1,0:T(8,128)S(1)} %add.162), channel_id=1, source_target_pairs={{0,4},{1,5},{2,6},{3,7},{4,0},{5,1},{6,2},{7,3},{8,12},{9,13},{10,... | collective-permute-start | bytes 393224 | tf_op jit(solution)/shard_map/ppermute | solution.py:216
  311.4 1.7 collective-permute-start.43
  312.9 1.4 collective-permute-start.37
  (30 other events, 119.9 us)

commit v2 on v1

v2 whole, which is shorter than its diff:
```python
import functools
import math

import jax
import jax.numpy as jnp
from jax import lax
from jax.experimental import pallas as pl
from jax.experimental.pallas import tpu as pltpu
from jax.sharding import PartitionSpec as P

AXES = ("row", "col")
F32 = jnp.float32
BF16 = jnp.bfloat16
SCALE_ROWS = 16
VMEM_BYTES = 16 * 1024 * 1024
LIGHT = pl.CostEstimate(flops=1, bytes_accessed=1, transcendentals=0)
PRODUCT_BYTES = 60 * 1024 * 1024


def encode(values, out_ref):
    rows = values.shape[0]
    top = jnp.max(jnp.abs(values), axis=0, keepdims=True)
    power = jnp.floor(14.9 - jnp.log2(jnp.maximum(top, 1e-37)))
    power = jnp.minimum(jnp.maximum(power, -100.0), 120.0)
    coded = jnp.round(values * jnp.exp2(power)).astype(jnp.int32)
    out_ref[0, :rows, :] = coded.astype(jnp.int16)
    powers = jnp.broadcast_to(power, (SCALE_ROWS, values.shape[1]))
    out_ref[0, rows:, :] = powers.astype(jnp.int32).astype(jnp.int16)


def decode(msg_ref):
    rows = msg_ref.shape[1] - SCALE_ROWS
    power = msg_ref[0, rows:, :].astype(jnp.int32).astype(F32)[:1]
    return msg_ref[0, :rows, :].astype(jnp.int32).astype(F32) * jnp.exp2(-power)


def product_kernel(tiles, parts, info_ref, a_ref, *refs):
    b_refs, outs = refs[:parts], refs[parts:]
    step = pl.program_id(0)
    total = None
    for part, b_ref in enumerate(b_refs):
        size = b_ref.shape[0]
        start = pl.multiple_of(info_ref[2 + part] * size, size)
        term = jnp.dot(a_ref[:, pl.ds(start, size)], b_ref[...], preferred_element_type=F32)
        total = term if total is None else total + term
    n = outs[1].shape[2]
    groups = [total[:, i * n : (i + 1) * n] for i in range(len(outs) // 2)]

    @pl.when(step < tiles)
    def _():
        for group, msg_ref in zip(groups, outs[::2]):
            encode(group, msg_ref)

    @pl.when(step >= tiles)
    def _():
        for group, own_ref in zip(groups, outs[1::2]):
            own_ref[0] = group


def product(info, ancestor, parts, depth, tile, groups):
    n = parts[0].shape[1] // groups
    tiles = depth // tile
    width = ancestor.shape[1]

    def a_map(i, info_ref):
        piece = jnp.where(i < tiles, info_ref[0], info_ref[1])
        return piece * tiles + lax.rem(i, tiles), 0

    msg_spec = pl.BlockSpec((1, tile + SCALE_ROWS, n), lambda i, info_ref: (jnp.minimum(i, tiles - 1), 0, 0))
    own_spec = pl.BlockSpec((1, tile, n), lambda i, info_ref: (jnp.maximum(i - tiles, 0), 0, 0))
    msg_shape = jax.ShapeDtypeStruct((tiles, tile + SCALE_ROWS, n), jnp.int16)
    own_shape = jax.ShapeDtypeStruct((tiles, tile, n), F32)
    outs = pl.pallas_call(
        functools.partial(product_kernel, tiles, len(parts)),
        grid_spec=pltpu.PrefetchScalarGridSpec(
            num_scalar_prefetch=1,
            grid=(2 * tiles,),
            in_specs=[pl.BlockSpec((tile, width), a_map)]
            + [pl.BlockSpec(x.shape, lambda i, info_ref: (0, 0)) for x in parts],
            out_specs=[msg_spec, own_spec] * groups,
        ),
        out_shape=[msg_shape, own_shape] * groups,
        compiler_params=pltpu.CompilerParams(vmem_limit_bytes=PRODUCT_BYTES),
        cost_estimate=LIGHT,
        name="product",
    )(info, ancestor, *parts)
    return outs[::2], outs[1::2]


def summed(pairs, moved, use_ref):
    total = pairs[0][0][0] + decode(pairs[0][1])
    for place, (own, msg) in enumerate(pairs[1:], 1):
        total = jnp.where(use_ref[0] == place, own[0] + decode(msg), total)
    for place, msg in enumerate(moved, 1):
        total = total + jnp.where(use_ref[place] != 0, decode(msg), 0.0)
    return total


def pass_on_kernel(count, use_ref, *refs):
    pairs = [(refs[2 * i], refs[2 * i + 1]) for i in range(count)]
    encode(summed(pairs, refs[2 * count : -1], use_ref), refs[-1])


def tile_spec(array):
    return pl.BlockSpec((1,) + array.shape[1:], lambda i, *_: (i, 0, 0))


def pass_on(use, pairs, moved):
    flat = [x for pair in pairs for x in pair] + moved
    msg = pairs[0][1]
    return pl.pallas_call(
        functools.partial(pass_on_kernel, len(pairs)),
        grid_spec=pltpu.PrefetchScalarGridSpec(
            num_scalar_prefetch=1,
            grid=(msg.shape[0],),
            in_specs=[tile_spec(x) for x in flat],
            out_specs=tile_spec(msg),
        ),
        out_shape=jax.ShapeDtypeStruct(msg.shape, msg.dtype),
        compiler_params=pltpu.CompilerParams(vmem_limit_bytes=VMEM_BYTES),
        cost_estimate=LIGHT,
        name="pass_on",
    )(use, *flat)


def finish_kernel(moved, use_ref, own_ref, msg_ref, *refs):
    masked_ref, keep_ref, upper_ref, update_ref = refs[moved:]
    total = summed([(own_ref, msg_ref)], refs[:moved], use_ref)
    full = -total * keep_ref[...].astype(F32)
    upper_ref[...] = full.astype(BF16)
    first = full.astype(BF16)
    rest = full - first.astype(F32)
    second = rest.astype(BF16)
    third = (rest - second.astype(F32)).astype(BF16)
    width = update_ref.shape[1]

    @pl.when(pl.program_id(0) == 0)
    def _():
        update_ref[...] = jnp.zeros_like(update_ref)

    for k in range(update_ref.shape[0]):
        cut = slice(k * width, (k + 1) * width)
        lower = masked_ref[:, cut]
        for part in (third, second, first):
            update_ref[k] += lax.dot_general(
                lower, part[:, cut], (((0,), (0,)), ((), ())), preferred_element_type=F32
            )


def finish(use, own, msg, moved, masked, keep, width):
    tiles, tile, n = own.shape
    flat = [own, msg] + moved
    plane = pl.BlockSpec((tile, n), lambda i, use_ref: (i, 0))
    snodes = n // width
    return pl.pallas_call(
        functools.partial(finish_kernel, len(moved)),
        grid_spec=pltpu.PrefetchScalarGridSpec(
            num_scalar_prefetch=1,
            grid=(tiles,),
            in_specs=[tile_spec(x) for x in flat] + [plane, plane],
            out_specs=[plane, pl.BlockSpec((snodes, width, width), lambda i, use_ref: (0, 0, 0))],
        ),
        out_shape=[
            jax.ShapeDtypeStruct((tiles * tile, n), BF16),
            jax.ShapeDtypeStruct((snodes, width, width), F32),
        ],
        compiler_params=pltpu.CompilerParams(vmem_limit_bytes=VMEM_BYTES),
        cost_estimate=LIGHT,
        name="finish",
    )(use, *flat, masked, keep)


def line_rounds(line):
    pending = {}
    for place in range(line):
        pending[place, 1] = list(range(line - 1, place, -1))
        pending[place, -1] = list(range(place))
    arrived = set()
    rounds = []
    while any(pending.values()):
        sends = {}
        for place in range(line):
            way = 1 if (place + len(rounds)) % 2 == 0 else -1
            behind = 0 <= place - way < line
            for part in pending[place, way]:
                if not behind or (place, part) in arrived:
                    sends[place] = (part, place + way)
                    break
        for place, (part, to) in sends.items():
            pending[place, to - place].remove(part)
        arrived |= {(to, part) for part, to in sends.values() if part != to}
        rounds.append(sends)
    return rounds


def orders(line, rounds):
    return [[sends[place][0] for sends in rounds if place in sends] + [place] for place in range(line)]


def make_local(rows, cols):
    line = cols // 2
    rounds = line_rounds(line)
    table = orders(line, rounds)

    def at(row, col):
        return row * cols + col

    def swap_low():
        return [(at(r, c), at(r, c ^ 1)) for r in range(rows) for c in range(cols)]

    def along(sends):
        return [
            (at(r, 2 * place + low), at(r, 2 * to + low))
            for r in range(rows)
            for place, (_, to) in sends.items()
            for low in range(2)
        ]

    def needs(turn):
        sends = rounds[turn] if turn < len(rounds) else {p: (p, p) for p in range(line)}
        slot = {p: table[p].index(part) for p, (part, _) in sends.items()}
        slots = sorted(set(slot.values()))
        choice = [slots.index(slot[p]) if p in slot else 0 for p in range(line)]
        used = {}
        for before in range(turn):
            for part, to in rounds[before].values():
                if to in sends and sends[to][0] == part:
                    used.setdefault(before, set()).add(to)
        flags = [[int(p in places) for p in range(line)] for places in used.values()]
        return slots, list(used), list(zip(choice, *flags))

    def swap_rows(bit):
        return [(at(r, c), at(r ^ bit, c)) for r in range(rows) for c in range(cols)]

    def swap_line(bit):
        return [(at(r, c), at(r, c ^ (2 * bit))) for r in range(rows) for c in range(cols)]

    def move(array, pairs):
        return lax.ppermute(array, AXES, pairs)

    ratio = cols // rows

    def gather_pieces(masked, row_index, col_index):
        half = masked.shape[0] // 2
        plane, odd = row_index // 2, lax.rem(row_index, 2)
        stay = lax.dynamic_slice_in_dim(masked, plane * half, half, 0)
        cross = lax.dynamic_slice_in_dim(masked, (1 - plane) * half, half, 0)
        cross = move(cross, swap_rows(2))
        is_own = col_index // ratio // 2 == plane
        upper_half = lax.rem(col_index, rows) // 2
        parts, places = [], []
        for turn in (0, 1):
            pairs = []
            for r in range(rows):
                for c in range(cols):
                    flip = 0 if c % rows // 2 == turn else 2
                    pairs.append((at(r, c), at(r // 2 * 2 + c % 2, (r ^ flip) * ratio + c // rows)))
            mine = move(jnp.where(upper_half == turn, stay, cross), pairs)
            other = move(mine, swap_rows(2))
            pair = jnp.where(is_own, turn, 1 - turn)
            parts += [mine, other, move(mine, swap_rows(1)), move(other, swap_rows(1))]
            for side in (odd, 1 - odd):
                places += [2 * (2 * pair + side) + plane, 2 * (2 * (1 - pair) + side) + 1 - plane]
        return parts, places

    def gather_whole(masked, row_index, col_index):
        row_block = lax.all_gather(masked, "col", axis=0, tiled=True)
        span = masked.shape[0] * rows
        own = lax.dynamic_slice_in_dim(row_block, lax.rem(col_index, ratio) * span, span, 0)
        own = jnp.where(row_index == col_index // ratio, own, jnp.zeros_like(own))
        block = lax.psum(own, "row")
        pieces = [block[i * masked.shape[0] : (i + 1) * masked.shape[0]] for i in range(rows)]
        return pieces, [jnp.int32(i) for i in range(rows)]

    gather = gather_pieces if rows == 4 else gather_whole

    def total_update(update, row_index):
        shape = update.shape
        flat = update.reshape(2, -1, shape[-1])
        odd = lax.rem(row_index, 2)
        keep = lax.dynamic_index_in_dim(flat, odd, 0, keepdims=False)
        give = lax.dynamic_index_in_dim(flat, 1 - odd, 0, keepdims=False)
        keep = keep + move(give, swap_rows(1))
        keep = keep + move(keep, swap_low())
        bit = 2
        while bit < rows:
            keep = keep + move(keep, swap_rows(bit))
            bit *= 2
        bit = 1
        while bit < line:
            keep = keep + move(keep, swap_line(bit))
            bit *= 2
        other = move(keep, swap_rows(1))
        even_part = jnp.where(odd == 0, keep, other)
        odd_part = jnp.where(odd == 0, other, keep)
        return jnp.stack([even_part, odd_part]).reshape(shape)

    def local(ancestor_inverse, panel, structure, diag_inverse):
        snodes, width = diag_inverse.shape[:2]
        depth = panel.shape[0]
        tile = min(512, depth)
        row_index, col_index = lax.axis_index("row"), lax.axis_index("col")
        low, place = lax.rem(col_index, 2), col_index // 2
        begin = (row_index * cols + col_index) * depth
        same = math.gcd(depth, width)
        blocks = depth // same
        owners = (begin + jnp.arange(blocks, dtype=jnp.int32) * same) // width
        keep = jnp.take(structure, owners, axis=1).astype(BF16)
        keep = jnp.broadcast_to(keep.T[:, None, :, None], (blocks, same, snodes, width))
        keep = keep.reshape(depth, snodes * width)
        masked = panel * keep
        order = jnp.asarray(table, jnp.int32)[place]
        cuts = [slice(k * width, (k + 1) * width) for k in range(snodes)]
        pieces, places = gather(masked, row_index, col_index)
        own = [[None] * line for _ in cuts]
        got = [[None] * line for _ in cuts]
        moved = [[] for _ in cuts]
        last = order

        def multiply(q):
            nonlocal last
            info = jnp.stack([order[q] * 2 + 1 - low, order[q] * 2 + low] + places)
            info, last = lax.optimization_barrier((info, last))
            msgs, kept = product(info, ancestor_inverse, pieces, depth, tile, snodes)
            for k in range(snodes):
                own[k][q] = kept[k]
                got[k][q] = move(msgs[k], swap_low())
            last = msgs[-1]

        def advance(turn, k):
            nonlocal last
            slots, before, use = needs(turn)
            use, last = lax.optimization_barrier((jnp.asarray(use, jnp.int32)[place], last))
            last = pass_on(use, [(own[k][q], got[k][q]) for q in slots], [moved[k][t] for t in before])
            moved[k].append(move(last, along(rounds[turn])))

        multiply(0)
        ready = 1
        for turn in range(len(rounds)):
            while ready < line and ready <= max(needs(turn)[0]) + (turn != 1):
                multiply(ready)
                ready += 1
            for k in range(snodes):
                advance(turn, k)
        while ready < line:
            multiply(ready)
            ready += 1
        _, before, use = needs(len(rounds))
        use = jnp.asarray(use, jnp.int32)[place]
        uppers, updates = [], []
        for k, cut in enumerate(cuts):
            arrived = [moved[k][t] for t in before]
            upper, update = finish(
                use, own[k][-1], got[k][-1], arrived, masked[:, cut], keep[:, cut], width
            )
            uppers.append(upper)
            updates.append(total_update(update, row_index))
        return jnp.concatenate(uppers, axis=1), diag_inverse - jnp.concatenate(updates)

    return local


def solution(mesh):
    return jax.shard_map(
        make_local(mesh.shape["row"], mesh.shape["col"]),
        mesh=mesh,
        in_specs=(P("row", "col"), P(("row", "col"), None), P(), P()),
        out_specs=(P(("row", "col"), None), P()),
        check_vma=False,
    )
```

time: 317 us -> 259 us (0.82)
  starting transfers between devices: 111 us -> 80.9 us
  Pallas kernels: 108 us -> 82.9 us
  local copies, waits for them, and re-layouts: 21 us -> 12.5 us
  waiting for transfers between devices: 67.2 us -> 74.4 us
    ppermute x44 -> x39, starting transfers between devices: 111 us -> 80.9 us  [move(): return lax.ppermute(array, AXES, pairs)]
    pallas_call x10 -> x6, Pallas kernels: 85 us -> 68.7 us  [the longest x4 61.8 us: product(): pl.pallas_call(functools.partial(product_kernel, tiles, len(parts)), grid...]
    unnamed x70 -> x38, local copies, waits for them, and re-layouts: 15.6 us -> 4.15 us
    pallas_call x10, Pallas kernels: 22.5 us -> 14.1 us  [pass_on(): pl.pallas_call(functools.partial(pass_on_kernel, len(pairs)), grid_spec=p...]
    ppermute x44 -> x39, waiting for transfers between devices: 67.2 us -> 74.4 us  [move(): return lax.ppermute(array, AXES, pairs)]
  transfers between devices with their start and end apart: 44 -> 39, of which waited for: 12 -> 19; matrix products, arithmetic and copies ran while one was open for 2% -> 3% of each run, Pallas kernels for 34% -> 26%
where the time goes in v2:
time: 259 us; the launch traced here: 258 us
  Pallas kernels  82.9 us (32%)
  starting transfers between devices  80.9 us (31%)
  waiting for transfers between devices  74.4 us (29%)
  local copies, waits for them, and re-layouts  12.5 us (5%)
  other arithmetic  4.05 us (2%)
  between operations  3.68 us (1%)
    ppermute x39, starting transfers between devices, move(): return lax.ppermute(array, AXES, pairs)  80.9 us
    ppermute x39, waiting for transfers between devices, move(): return lax.ppermute(array, AXES, pairs)  74.4 us
    pallas_call x4, Pallas kernels, product(): pl.pallas_call(functools.partial(product_kernel, tiles, len(parts)), grid...  61.8 us
    pallas_call x10, Pallas kernels, pass_on(): pl.pallas_call(functools.partial(pass_on_kernel, len(pairs)), grid_spec=p...  14.1 us
    pallas_call x2, Pallas kernels, finish(): pl.pallas_call(functools.partial(finish_kernel, len(moved)), grid_spec=pl...  6.91 us
  transfers between devices with their start and end apart: 39, of which 19 were waited for; matrix products, arithmetic and copies ran while one was open for 3% of the time, Pallas kernels for 26%

profile of v2, /device:TPU:0, one launch (start us, length us, event | category | flops | bytes accessed | tf_op | source)
XLA Modules:
  0.0 258.4 jit_solution(4523009011075131745)
XLA Ops:
  2.8 1.2 copy.19
  4.1 1.5 mul.121
  5.6 3.0 %collective-permute-start = (bf16[512,512]{1,0:T(8,128)(2,1)S(1)}, bf16[512,512]{1,0:T(8,128)(2,1)S(1)}, u32[]{:S(2)}, u32[]{:S(2)}) collective-permute-start(bf16[512,512]{1,0:T(8,128)(2,1)S(1)} %constant_dynamic-slice_fusion), channel_id=1, source_target_pairs={{0,16},{1,17},{2,18},{3,19},{4,20},{5,21},{6,22},{7,23},{8,24},{9,... | collective-permute-start | bytes 1572872 | tf_op jit(solution)/shard_map/ppermute | solution.py:239
  8.6 11.9 %collective-permute-done = bf16[512,512]{1,0:T(8,128)(2,1)S(1)} collective-permute-done((bf16[512,512]{1,0:T(8,128)(2,1)S(1)}, bf16[512,512]{1,0:T(8,128)(2,1)S(1)}, u32[]{:S(2)}, u32[]{:S(2)}) %collective-permute-start) | collective-permute-done | bytes 524320 | tf_op jit(solution)/shard_map/ppermute | solution.py:239
  21.5 7.3 %collective-permute-start.5 = (bf16[512,512]{1,0:T(8,128)(2,1)S(1)}, bf16[512,512]{1,0:T(8,128)(2,1)S(1)}, u32[]{:S(2)}, u32[]{:S(2)}) collective-permute-start(bf16[512,512]{1,0:T(8,128)(2,1)S(1)} %get-tuple-element.68), channel_id=1, source_target_pairs={{0,4},{1,12},{2,0},{3,8},{4,5},{5,13},{6,1},{7,9},{8,6},{9,14},{10... | collective-permute-start | bytes 1572872 | tf_op jit(solution)/shard_map/ppermute | solution.py:239
  28.8 10.2 %collective-permute-start.2 = (bf16[512,512]{1,0:T(8,128)(2,1)S(1)}, bf16[512,512]{1,0:T(8,128)(2,1)S(1)}, u32[]{:S(2)}, u32[]{:S(2)}) collective-permute-start(bf16[512,512]{1,0:T(8,128)(2,1)S(1)} %collective-permute-done.1.refs_0_), channel_id=1, source_target_pairs={{0,16},{1,17},{2,18},{3,19},{4,20},{5,21},{6,22},{7,23},{8,24},{9,... | collective-permute-start | bytes 1572872 | tf_op jit(solution)/shard_map/ppermute | solution.py:239
  39.0 2.1 collective-permute-done.5.refs_4_
  41.2 3.7 %collective-permute-start.3 = (bf16[512,512]{1,0:T(8,128)(2,1)S(1)}, bf16[512,512]{1,0:T(8,128)(2,1)}, u32[]{:S(2)}, u32[]{:S(2)}) collective-permute-start(bf16[512,512]{1,0:T(8,128)(2,1)S(1)} %collective-permute-done.1.refs_0_), channel_id=1, source_target_pairs={{0,8},{1,9},{2,10},{3,11},{4,12},{5,13},{6,14},{7,15},{8,0},{9,1},... | collective-permute-start | bytes 1572872 | tf_op jit(solution)/shard_map/ppermute | solution.py:239
  44.8 7.0 %collective-permute-done.2.refs_1_ = bf16[512,512]{1,0:T(8,128)(2,1)S(1)} collective-permute-done((bf16[512,512]{1,0:T(8,128)(2,1)S(1)}, bf16[512,512]{1,0:T(8,128)(2,1)S(1)}, u32[]{:S(2)}, u32[]{:S(2)}) %collective-permute-start.2) | collective-permute-done | bytes 524320 | tf_op jit(solution)/shard_map/ppermute | solution.py:239
  51.8 11.1 %collective-permute-done.6.refs_5_ = bf16[512,512]{1,0:T(8,128)(2,1)} collective-permute-done((bf16[512,512]{1,0:T(8,128)(2,1)S(1)}, bf16[512,512]{1,0:T(8,128)(2,1)}, u32[]{:S(2)}, u32[]{:S(2)}) %collective-permute-start.6) | collective-permute-done | bytes 524320 | tf_op jit(solution)/shard_map/ppermute | solution.py:239
  65.7 15.3 %product.4 = (s16[2,528,256]{2,1,0:T(8,128)(2,1)}, f32[2,512,256]{2,1,0:T(8,128)}, s16[2,528,256]{2,1,0:T(8,128)(2,1)}, f32[2,512,256]{2,1,0:T(8,128)}) custom-call(s32[10]{0:T(128)} %stack.121.info_ref, bf16[8192,4096]{1,0:T(8,128)(2,1)} %a_ref.7, bf16[512,512]{1,0:T(8,128)(2,1)} %copy-done.13, bf16[512,512]{1,0:T(8,128)(2,1)} %copy-done.15, ...), custom_call_target="tpu_custom_call" | custom-call | flops 1 | bytes 1 | tf_op jit(solution)/shard_map/product/pallas_call | solution.py:73
  81.0 11.9 %collective-permute-start.9 = (s16[2,528,256]{2,1,0:T(8,128)(2,1)}, s16[2,528,256]{2,1,0:T(8,128)(2,1)S(1)}, u32[]{:S(2)}, u32[]{:S(2)}) collective-permute-start(s16[2,528,256]{2,1,0:T(8,128)(2,1)} %get-tuple-element.40), channel_id=1, source_target_pairs={{0,1},{1,0},{2,3},{3,2},{4,5},{5,4},{6,7},{7,6},{8,9},{9,8},{10,11... | collective-permute-start | bytes 1622024 | tf_op jit(solution)/shard_map/ppermute | solution.py:239
  94.3 15.5 %product.5 = (s16[2,528,256]{2,1,0:T(8,128)(2,1)}, f32[2,512,256]{2,1,0:T(8,128)}, s16[2,528,256]{2,1,0:T(8,128)(2,1)}, f32[2,512,256]{2,1,0:T(8,128)}) custom-call(s32[10]{0:T(128)} %stack.118.info_ref, bf16[8192,4096]{1,0:T(8,128)(2,1)} %a_ref.7, bf16[512,512]{1,0:T(8,128)(2,1)} %copy-done.13, bf16[512,512]{1,0:T(8,128)(2,1)} %copy-done.15, ...), custom_call_target="tpu_custom_call" | custom-call | flops 1 | bytes 1 | tf_op jit(solution)/shard_map/product/pallas_call | solution.py:73
  110.2 4.1 %collective-permute-start.11 = (s16[2,528,256]{2,1,0:T(8,128)(2,1)S(1)}, s16[2,528,256]{2,1,0:T(8,128)(2,1)S(1)}, u32[]{:S(2)}, u32[]{:S(2)}) collective-permute-start(s16[2,528,256]{2,1,0:T(8,128)(2,1)S(1)} %pass_on.10), channel_id=1, source_target_pairs={{0,2},{1,3},{6,4},{7,5},{8,10},{9,11},{14,12},{15,13},{16,18},{17,... | collective-permute-start | bytes 1622024 | tf_op jit(solution)/shard_map/ppermute | solution.py:239
  114.3 3.4 %collective-permute-done.10.refs_1_ = s16[2,528,256]{2,1,0:T(8,128)(2,1)S(1)} collective-permute-done((s16[2,528,256]{2,1,0:T(8,128)(2,1)}, s16[2,528,256]{2,1,0:T(8,128)(2,1)S(1)}, u32[]{:S(2)}, u32[]{:S(2)}) %collective-permute-start.10) | collective-permute-done | bytes 540704 | tf_op jit(solution)/shard_map/ppermute | solution.py:239
  118.1 3.9 %collective-permute-start.12 = (s16[2,528,256]{2,1,0:T(8,128)(2,1)S(1)}, s16[2,528,256]{2,1,0:T(8,128)(2,1)S(1)}, u32[]{:S(2)}, u32[]{:S(2)}) collective-permute-start(s16[2,528,256]{2,1,0:T(8,128)(2,1)S(1)} %pass_on.11), channel_id=1, source_target_pairs={{0,2},{1,3},{6,4},{7,5},{8,10},{9,11},{14,12},{15,13},{16,18},{17,... | collective-permute-start | bytes 1622024 | tf_op jit(solution)/shard_map/ppermute | solution.py:239
  122.9 4.0 %collective-permute-done.11.refs_2_ = s16[2,528,256]{2,1,0:T(8,128)(2,1)S(1)} collective-permute-done((s16[2,528,256]{2,1,0:T(8,128)(2,1)S(1)}, s16[2,528,256]{2,1,0:T(8,128)(2,1)S(1)}, u32[]{:S(2)}, u32[]{:S(2)}) %collective-permute-start.11) | collective-permute-done | bytes 540704 | tf_op jit(solution)/shard_map/ppermute | solution.py:239
  126.9 1.8 pass_on.12
  128.7 1.5 collective-permute-start.14
  130.2 7.3 %collective-permute-done.12.refs_2_ = s16[2,528,256]{2,1,0:T(8,128)(2,1)S(1)} collective-permute-done((s16[2,528,256]{2,1,0:T(8,128)(2,1)S(1)}, s16[2,528,256]{2,1,0:T(8,128)(2,1)S(1)}, u32[]{:S(2)}, u32[]{:S(2)}) %collective-permute-start.12) | collective-permute-done | bytes 540704 | tf_op jit(solution)/shard_map/ppermute | solution.py:239
  137.5 1.8 pass_on.13
  139.3 1.5 collective-permute-start.16
  142.2 15.5 %product.6 = (s16[2,528,256]{2,1,0:T(8,128)(2,1)}, f32[2,512,256]{2,1,0:T(8,128)}, s16[2,528,256]{2,1,0:T(8,128)(2,1)}, f32[2,512,256]{2,1,0:T(8,128)}) custom-call(s32[10]{0:T(128)} %stack.115.info_ref, bf16[8192,4096]{1,0:T(8,128)(2,1)} %a_ref.7, bf16[512,512]{1,0:T(8,128)(2,1)} %copy-done.13, bf16[512,512]{1,0:T(8,128)(2,1)} %copy-done.15, ...), custom_call_target="tpu_custom_call" | custom-call | flops 1 | bytes 1 | tf_op jit(solution)/shard_map/product/pallas_call | solution.py:73
  158.0 1.8 collective-permute-start.19
  159.8 2.7 %pass_on.14 = s16[2,528,256]{2,1,0:T(8,128)(2,1)} custom-call(s32[2]{0:T(128)S(1)} %fusion.1.use_ref, f32[2,512,256]{2,1,0:T(8,128)S(1)} %copy-done.7, s16[2,528,256]{2,1,0:T(8,128)(2,1)S(1)} %collective-permute-done.13.refs_1_, s16[2,528,256]{2,1,0:T(8,128)(2,1)} %collective-permute-done.14.refs_2_), custom_call_target="tpu_custom_call" | custom-call | flops 1 | bytes 1 | tf_op jit(solution)/shard_map/pass_on/pallas_call | solution.py:111
  162.5 4.3 %collective-permute-start.18 = (s16[2,528,256]{2,1,0:T(8,128)(2,1)}, s16[2,528,256]{2,1,0:T(8,128)(2,1)S(1)}, u32[]{:S(2)}, u32[]{:S(2)}) collective-permute-start(s16[2,528,256]{2,1,0:T(8,128)(2,1)} %pass_on.14), channel_id=1, source_target_pairs={{0,2},{1,3},{2,0},{3,1},{4,6},{5,7},{6,4},{7,5},{8,10},{9,11},{10,... | collective-permute-start | bytes 1622024 | tf_op jit(solution)/shard_map/ppermute | solution.py:239
  166.8 2.8 %pass_on.15 = s16[2,528,256]{2,1,0:T(8,128)(2,1)} custom-call(s32[2]{0:T(128)S(1)} %fusion.1.use_ref, f32[2,512,256]{2,1,0:T(8,128)S(1)} %copy-done.6, s16[2,528,256]{2,1,0:T(8,128)(2,1)S(1)} %collective-permute-done.15.refs_1_, s16[2,528,256]{2,1,0:T(8,128)(2,1)} %collective-permute-done.16.refs_2_), custom_call_target="tpu_custom_call" | custom-call | flops 1 | bytes 1 | tf_op jit(solution)/shard_map/pass_on/pallas_call | solution.py:111
  170.8 15.5 %product.7 = (s16[2,528,256]{2,1,0:T(8,128)(2,1)}, f32[2,512,256]{2,1,0:T(8,128)}, s16[2,528,256]{2,1,0:T(8,128)(2,1)}, f32[2,512,256]{2,1,0:T(8,128)}) custom-call(s32[10]{0:T(128)} %stack.112.info_ref, bf16[8192,4096]{1,0:T(8,128)(2,1)} %a_ref.7, bf16[512,512]{1,0:T(8,128)(2,1)} %copy-done.13, bf16[512,512]{1,0:T(8,128)(2,1)} %copy-done.15, ...), custom_call_target="tpu_custom_call" | custom-call | flops 1 | bytes 1 | tf_op jit(solution)/shard_map/product/pallas_call | solution.py:73
  187.8 1.6 collective-permute-done.22.refs_2_.refs_0_
  189.4 1.8 pass_on.17
  191.2 1.5 collective-permute-start.25
  194.2 5.7 %collective-permute-start.26 = (s16[2,528,256]{2,1,0:T(8,128)(2,1)}, s16[2,528,256]{2,1,0:T(8,128)(2,1)}, u32[]{:S(2)}, u32[]{:S(2)}) collective-permute-start(s16[2,528,256]{2,1,0:T(8,128)(2,1)} %pass_on.19), channel_id=1, source_target_pairs={{0,2},{1,3},{6,4},{7,5},{8,10},{9,11},{14,12},{15,13},{16,18},{17,... | collective-permute-start | bytes 1622024 | tf_op jit(solution)/shard_map/ppermute | solution.py:239
  200.4 1.5 collective-permute-start.20
  201.9 3.4 %collective-permute-start.23 = (s16[2,528,256]{2,1,0:T(8,128)(2,1)}, s16[2,528,256]{2,1,0:T(8,128)(2,1)}, u32[]{:S(2)}, u32[]{:S(2)}) collective-permute-start(s16[2,528,256]{2,1,0:T(8,128)(2,1)} %copy-done.9), channel_id=1, source_target_pairs={{0,2},{1,3},{6,4},{7,5},{8,10},{9,11},{14,12},{15,13},{16,18},{17,... | collective-permute-start | bytes 1622024 | tf_op jit(solution)/shard_map/ppermute | solution.py:239
  206.0 1.7 fusion.3
  207.7 4.4 %collective-permute-done.26.refs_2_ = s16[2,528,256]{2,1,0:T(8,128)(2,1)} collective-permute-done((s16[2,528,256]{2,1,0:T(8,128)(2,1)}, s16[2,528,256]{2,1,0:T(8,128)(2,1)}, u32[]{:S(2)}, u32[]{:S(2)}) %collective-permute-start.26) | collective-permute-done | bytes 540704 | tf_op jit(solution)/shard_map/ppermute | solution.py:239
  212.1 3.4 %finish.3 = (bf16[1024,256]{1,0:T(8,128)(2,1)S(1)}, f32[1,256,256]{2,1,0:T(8,128)S(1)}) custom-call(s32[4]{0:T(128)S(1)} %fusion.use_ref, f32[2,512,256]{2,1,0:T(8,128)S(1)} %copy-done.5, s16[2,528,256]{2,1,0:T(8,128)(2,1)S(1)} %collective-permute-done.24.msg_ref, s16[2,528,256]{2,1,0:T(8,128)(2,1)S(1)} %collective-permute-done.22.refs_2_.refs_0_, ...), custom_call_target="tpu_custom_call" | custom-call | flops 1 | bytes 1 | tf_op jit(solution)/shard_map/finish/pallas_call | solution.py:155
  216.4 3.4 %collective-permute-done.23.refs_2_ = s16[2,528,256]{2,1,0:T(8,128)(2,1)} collective-permute-done((s16[2,528,256]{2,1,0:T(8,128)(2,1)}, s16[2,528,256]{2,1,0:T(8,128)(2,1)}, u32[]{:S(2)}, u32[]{:S(2)}) %collective-permute-start.23) | collective-permute-done | bytes 540704 | tf_op jit(solution)/shard_map/ppermute | solution.py:239
  219.8 1.2 copy-done.4
  221.0 3.5 %finish.2 = (bf16[1024,256]{1,0:T(8,128)(2,1)S(1)}, f32[1,256,256]{2,1,0:T(8,128)S(1)}) custom-call(s32[4]{0:T(128)S(1)} %fusion.use_ref, f32[2,512,256]{2,1,0:T(8,128)S(1)} %copy-done.4, s16[2,528,256]{2,1,0:T(8,128)(2,1)} %collective-permute-done.17.msg_ref, s16[2,528,256]{2,1,0:T(8,128)(2,1)S(1)} %collective-permute-done.18.refs_2_.refs_0_, ...), custom_call_target="tpu_custom_call" | custom-call | flops 1 | bytes 1 | tf_op jit(solution)/shard_map/finish/pallas_call | solution.py:155
  226.9 4.2 %collective-permute-done.34 = f32[128,256]{1,0:T(8,128)S(1)} collective-permute-done((f32[128,256]{1,0:T(8,128)S(1)}, f32[128,256]{1,0:T(8,128)S(1)}, u32[]{:S(2)}, u32[]{:S(2)}) %collective-permute-start.34) | collective-permute-done | bytes 131104 | tf_op jit(solution)/shard_map/ppermute | solution.py:239
  231.4 2.1 collective-permute-done.28
  233.8 2.6 collective-permute-done.35
  236.4 2.5 collective-permute-start.36
  238.9 2.5 collective-permute-start.30
  242.3 3.0 %collective-permute-start.37 = (f32[128,256]{1,0:T(8,128)S(1)}, f32[128,256]{1,0:T(8,128)S(1)}, u32[]{:S(2)}, u32[]{:S(2)}) collective-permute-start(f32[128,256]{1,0:T(8,128)S(1)} %add.227), channel_id=1, source_target_pairs={{0,4},{1,5},{2,6},{3,7},{4,0},{5,1},{6,2},{7,3},{8,12},{9,13},{10,... | collective-permute-start | bytes 393224 | tf_op jit(solution)/shard_map/ppermute | solution.py:239
  246.1 2.5 collective-permute-start.31
  248.6 5.9 %collective-permute-done.37 = f32[128,256]{1,0:T(8,128)S(1)} collective-permute-done((f32[128,256]{1,0:T(8,128)S(1)}, f32[128,256]{1,0:T(8,128)S(1)}, u32[]{:S(2)}, u32[]{:S(2)}) %collective-permute-start.37) | collective-permute-done | bytes 131104 | tf_op jit(solution)/shard_map/ppermute | solution.py:239
  (120 shorter events, 22.7 us)
Async XLA Ops:
  5.6 75.5 %copy-start.12 = (bf16[1024,512]{1,0:T(8,128)(2,1)}, bf16[1024,512]{1,0:T(8,128)(2,1)S(1)}, u32[]{:S(2)}) copy-start(bf16[1024,512]{1,0:T(8,128)(2,1)S(1)} %mul.121) | copy-start | bytes 3145732
  5.6 14.9 %collective-permute-start = (bf16[512,512]{1,0:T(8,128)(2,1)S(1)}, bf16[512,512]{1,0:T(8,128)(2,1)S(1)}, u32[]{:S(2)}, u32[]{:S(2)}) collective-permute-start(bf16[512,512]{1,0:T(8,128)(2,1)S(1)} %constant_dynamic-slice_fusion), channel_id=1, source_target_pairs={{0,16},{1,17},{2,18},{3,19},{4,20},{5,21},{6,22},{7,23},{8,24},{9,... | collective-permute-start | bytes 1572872 | tf_op jit(solution)/shard_map/ppermute | solution.py:239
  20.8 8.0 %collective-permute-start.1 = (bf16[512,512]{1,0:T(8,128)(2,1)S(1)}, bf16[512,512]{1,0:T(8,128)(2,1)S(1)}, u32[]{:S(2)}, u32[]{:S(2)}) collective-permute-start(bf16[512,512]{1,0:T(8,128)(2,1)S(1)} %get-tuple-element.69), channel_id=1, source_target_pairs={{0,0},{1,8},{2,4},{3,12},{4,1},{5,9},{6,5},{7,13},{8,2},{9,10},{10... | collective-permute-start | bytes 1572872 | tf_op jit(solution)/shard_map/ppermute | solution.py:239
  21.5 19.7 %collective-permute-start.5 = (bf16[512,512]{1,0:T(8,128)(2,1)S(1)}, bf16[512,512]{1,0:T(8,128)(2,1)S(1)}, u32[]{:S(2)}, u32[]{:S(2)}) collective-permute-start(bf16[512,512]{1,0:T(8,128)(2,1)S(1)} %get-tuple-element.68), channel_id=1, source_target_pairs={{0,4},{1,12},{2,0},{3,8},{4,5},{5,13},{6,1},{7,9},{8,6},{9,14},{10... | collective-permute-start | bytes 1572872 | tf_op jit(solution)/shard_map/ppermute | solution.py:239
  28.8 36.9 %copy-start.13 = (bf16[512,512]{1,0:T(8,128)(2,1)}, bf16[512,512]{1,0:T(8,128)(2,1)S(1)}, u32[]{:S(2)}) copy-start(bf16[512,512]{1,0:T(8,128)(2,1)S(1)} %collective-permute-done.1.refs_0_) | copy-start | bytes 1572868
  28.8 23.0 %collective-permute-start.2 = (bf16[512,512]{1,0:T(8,128)(2,1)S(1)}, bf16[512,512]{1,0:T(8,128)(2,1)S(1)}, u32[]{:S(2)}, u32[]{:S(2)}) collective-permute-start(bf16[512,512]{1,0:T(8,128)(2,1)S(1)} %collective-permute-done.1.refs_0_), channel_id=1, source_target_pairs={{0,16},{1,17},{2,18},{3,19},{4,20},{5,21},{6,22},{7,23},{8,24},{9,... | collective-permute-start | bytes 1572872 | tf_op jit(solution)/shard_map/ppermute | solution.py:239
  41.2 24.5 %copy-start.14 = (bf16[512,512]{1,0:T(8,128)(2,1)}, bf16[512,512]{1,0:T(8,128)(2,1)S(1)}, u32[]{:S(2)}) copy-start(bf16[512,512]{1,0:T(8,128)(2,1)S(1)} %collective-permute-done.5.refs_4_) | copy-start | bytes 1572868
  41.2 21.8 %collective-permute-start.6 = (bf16[512,512]{1,0:T(8,128)(2,1)S(1)}, bf16[512,512]{1,0:T(8,128)(2,1)}, u32[]{:S(2)}, u32[]{:S(2)}) collective-permute-start(bf16[512,512]{1,0:T(8,128)(2,1)S(1)} %collective-permute-done.5.refs_4_), channel_id=1, source_target_pairs={{0,16},{1,17},{2,18},{3,19},{4,20},{5,21},{6,22},{7,23},{8,24},{9,... | collective-permute-start | bytes 1572872 | tf_op jit(solution)/shard_map/ppermute | solution.py:239
  41.2 24.5 %collective-permute-start.3 = (bf16[512,512]{1,0:T(8,128)(2,1)S(1)}, bf16[512,512]{1,0:T(8,128)(2,1)}, u32[]{:S(2)}, u32[]{:S(2)}) collective-permute-start(bf16[512,512]{1,0:T(8,128)(2,1)S(1)} %collective-permute-done.1.refs_0_), channel_id=1, source_target_pairs={{0,8},{1,9},{2,10},{3,11},{4,12},{5,13},{6,14},{7,15},{8,0},{9,1},... | collective-permute-start | bytes 1572872 | tf_op jit(solution)/shard_map/ppermute | solution.py:239
  44.8 20.8 %collective-permute-start.7 = (bf16[512,512]{1,0:T(8,128)(2,1)S(1)}, bf16[512,512]{1,0:T(8,128)(2,1)}, u32[]{:S(2)}, u32[]{:S(2)}) collective-permute-start(bf16[512,512]{1,0:T(8,128)(2,1)S(1)} %collective-permute-done.5.refs_4_), channel_id=1, source_target_pairs={{0,8},{1,9},{2,10},{3,11},{4,12},{5,13},{6,14},{7,15},{8,0},{9,1},... | collective-permute-start | bytes 1572872 | tf_op jit(solution)/shard_map/ppermute | solution.py:239
  51.8 13.9 %copy-start.15 = (bf16[512,512]{1,0:T(8,128)(2,1)}, bf16[512,512]{1,0:T(8,128)(2,1)S(1)}, u32[]{:S(2)}) copy-start(bf16[512,512]{1,0:T(8,128)(2,1)S(1)} %collective-permute-done.2.refs_1_) | copy-start | bytes 1572868
  51.8 13.9 %collective-permute-start.4 = (bf16[512,512]{1,0:T(8,128)(2,1)S(1)}, bf16[512,512]{1,0:T(8,128)(2,1)}, u32[]{:S(2)}, u32[]{:S(2)}) collective-permute-start(bf16[512,512]{1,0:T(8,128)(2,1)S(1)} %collective-permute-done.2.refs_1_), channel_id=1, source_target_pairs={{0,8},{1,9},{2,10},{3,11},{4,12},{5,13},{6,14},{7,15},{8,0},{9,1},... | collective-permute-start | bytes 1572872 | tf_op jit(solution)/shard_map/ppermute | solution.py:239
  62.9 2.7 %collective-permute-start.8 = (bf16[512,512]{1,0:T(8,128)(2,1)}, bf16[512,512]{1,0:T(8,128)(2,1)}, u32[]{:S(2)}, u32[]{:S(2)}) collective-permute-start(bf16[512,512]{1,0:T(8,128)(2,1)} %collective-permute-done.6.refs_5_), channel_id=1, source_target_pairs={{0,8},{1,9},{2,10},{3,11},{4,12},{5,13},{6,14},{7,15},{8,0},{9,1},... | collective-permute-start | bytes 1572872 | tf_op jit(solution)/shard_map/ppermute | solution.py:239
  81.0 28.8 %collective-permute-start.9 = (s16[2,528,256]{2,1,0:T(8,128)(2,1)}, s16[2,528,256]{2,1,0:T(8,128)(2,1)S(1)}, u32[]{:S(2)}, u32[]{:S(2)}) collective-permute-start(s16[2,528,256]{2,1,0:T(8,128)(2,1)} %get-tuple-element.40), channel_id=1, source_target_pairs={{0,1},{1,0},{2,3},{3,2},{4,5},{5,4},{6,7},{7,6},{8,9},{9,8},{10,11... | collective-permute-start | bytes 1622024 | tf_op jit(solution)/shard_map/ppermute | solution.py:239
  93.0 24.7 %collective-permute-start.10 = (s16[2,528,256]{2,1,0:T(8,128)(2,1)}, s16[2,528,256]{2,1,0:T(8,128)(2,1)S(1)}, u32[]{:S(2)}, u32[]{:S(2)}) collective-permute-start(s16[2,528,256]{2,1,0:T(8,128)(2,1)} %get-tuple-element.35), channel_id=1, source_target_pairs={{0,1},{1,0},{2,3},{3,2},{4,5},{5,4},{6,7},{7,6},{8,9},{9,8},{10,11... | collective-permute-start | bytes 1622024 | tf_op jit(solution)/shard_map/ppermute | solution.py:239
  94.3 15.5 %copy-start.3 = (f32[2,512,256]{2,1,0:T(8,128)S(1)}, f32[2,512,256]{2,1,0:T(8,128)}, u32[]{:S(2)}) copy-start(f32[2,512,256]{2,1,0:T(8,128)} %get-tuple-element.39.refs_0_) | copy-start | bytes 3145732
  110.2 16.7 %collective-permute-start.11 = (s16[2,528,256]{2,1,0:T(8,128)(2,1)S(1)}, s16[2,528,256]{2,1,0:T(8,128)(2,1)S(1)}, u32[]{:S(2)}, u32[]{:S(2)}) collective-permute-start(s16[2,528,256]{2,1,0:T(8,128)(2,1)S(1)} %pass_on.10), channel_id=1, source_target_pairs={{0,2},{1,3},{6,4},{7,5},{8,10},{9,11},{14,12},{15,13},{16,18},{17,... | collective-permute-start | bytes 1622024 | tf_op jit(solution)/shard_map/ppermute | solution.py:239
  118.1 19.4 %collective-permute-start.12 = (s16[2,528,256]{2,1,0:T(8,128)(2,1)S(1)}, s16[2,528,256]{2,1,0:T(8,128)(2,1)S(1)}, u32[]{:S(2)}, u32[]{:S(2)}) collective-permute-start(s16[2,528,256]{2,1,0:T(8,128)(2,1)S(1)} %pass_on.11), channel_id=1, source_target_pairs={{0,2},{1,3},{6,4},{7,5},{8,10},{9,11},{14,12},{15,13},{16,18},{17,... | collective-permute-start | bytes 1622024 | tf_op jit(solution)/shard_map/ppermute | solution.py:239
  122.6 35.3 %collective-permute-start.13 = (s16[2,528,256]{2,1,0:T(8,128)(2,1)}, s16[2,528,256]{2,1,0:T(8,128)(2,1)S(1)}, u32[]{:S(2)}, u32[]{:S(2)}) collective-permute-start(s16[2,528,256]{2,1,0:T(8,128)(2,1)} %get-tuple-element.49), channel_id=1, source_target_pairs={{0,1},{1,0},{2,3},{3,2},{4,5},{5,4},{6,7},{7,6},{8,9},{9,8},{10,11... | collective-permute-start | bytes 1622024 | tf_op jit(solution)/shard_map/ppermute | solution.py:239
  128.7 31.1 %collective-permute-start.14 = (s16[2,528,256]{2,1,0:T(8,128)(2,1)}, s16[2,528,256]{2,1,0:T(8,128)(2,1)}, u32[]{:S(2)}, u32[]{:S(2)}) collective-permute-start(s16[2,528,256]{2,1,0:T(8,128)(2,1)} %pass_on.12), channel_id=1, source_target_pairs={{2,4},{3,5},{4,2},{5,3},{10,12},{11,13},{12,10},{13,11},{18,20},{1... | collective-permute-start | bytes 1622024 | tf_op jit(solution)/shard_map/ppermute | solution.py:239
  130.2 36.6 %collective-permute-start.15 = (s16[2,528,256]{2,1,0:T(8,128)(2,1)}, s16[2,528,256]{2,1,0:T(8,128)(2,1)S(1)}, u32[]{:S(2)}, u32[]{:S(2)}) collective-permute-start(s16[2,528,256]{2,1,0:T(8,128)(2,1)} %get-tuple-element.37), channel_id=1, source_target_pairs={{0,1},{1,0},{2,3},{3,2},{4,5},{5,4},{6,7},{7,6},{8,9},{9,8},{10,11... | collective-permute-start | bytes 1622024 | tf_op jit(solution)/shard_map/ppermute | solution.py:239
  139.3 27.5 %collective-permute-start.16 = (s16[2,528,256]{2,1,0:T(8,128)(2,1)}, s16[2,528,256]{2,1,0:T(8,128)(2,1)}, u32[]{:S(2)}, u32[]{:S(2)}) collective-permute-start(s16[2,528,256]{2,1,0:T(8,128)(2,1)} %pass_on.13), channel_id=1, source_target_pairs={{2,4},{3,5},{4,2},{5,3},{10,12},{11,13},{12,10},{13,11},{18,20},{1... | collective-permute-start | bytes 1622024 | tf_op jit(solution)/shard_map/ppermute | solution.py:239
  142.2 17.6 %copy-start.7 = (f32[2,512,256]{2,1,0:T(8,128)S(1)}, f32[2,512,256]{2,1,0:T(8,128)}, u32[]{:S(2)}) copy-start(f32[2,512,256]{2,1,0:T(8,128)} %get-tuple-element.48.refs_0_) | copy-start | bytes 3145732
  157.7 9.1 %copy-start.6 = (f32[2,512,256]{2,1,0:T(8,128)S(1)}, f32[2,512,256]{2,1,0:T(8,128)}, u32[]{:S(2)}) copy-start(f32[2,512,256]{2,1,0:T(8,128)} %get-tuple-element.51.refs_0_) | copy-start | bytes 3145732
  157.7 30.1 %collective-permute-start.21 = (s16[2,528,256]{2,1,0:T(8,128)(2,1)}, s16[2,528,256]{2,1,0:T(8,128)(2,1)S(1)}, u32[]{:S(2)}, u32[]{:S(2)}) collective-permute-start(s16[2,528,256]{2,1,0:T(8,128)(2,1)} %get-tuple-element.46), channel_id=1, source_target_pairs={{0,1},{1,0},{2,3},{3,2},{4,5},{5,4},{6,7},{7,6},{8,9},{9,8},{10,11... | collective-permute-start | bytes 1622024 | tf_op jit(solution)/shard_map/ppermute | solution.py:239
  158.0 28.7 %collective-permute-start.19 = (s16[2,528,256]{2,1,0:T(8,128)(2,1)}, s16[2,528,256]{2,1,0:T(8,128)(2,1)S(1)}, u32[]{:S(2)}, u32[]{:S(2)}) collective-permute-start(s16[2,528,256]{2,1,0:T(8,128)(2,1)} %get-tuple-element.58), channel_id=1, source_target_pairs={{0,1},{1,0},{2,3},{3,2},{4,5},{5,4},{6,7},{7,6},{8,9},{9,8},{10,11... | collective-permute-start | bytes 1622024 | tf_op jit(solution)/shard_map/ppermute | solution.py:239
  162.5 24.2 %collective-permute-start.18 = (s16[2,528,256]{2,1,0:T(8,128)(2,1)}, s16[2,528,256]{2,1,0:T(8,128)(2,1)S(1)}, u32[]{:S(2)}, u32[]{:S(2)}) collective-permute-start(s16[2,528,256]{2,1,0:T(8,128)(2,1)} %pass_on.14), channel_id=1, source_target_pairs={{0,2},{1,3},{2,0},{3,1},{4,6},{5,7},{6,4},{7,5},{8,10},{9,11},{10,... | collective-permute-start | bytes 1622024 | tf_op jit(solution)/shard_map/ppermute | solution.py:239
  169.6 19.8 %collective-permute-start.22 = (s16[2,528,256]{2,1,0:T(8,128)(2,1)}, s16[2,528,256]{2,1,0:T(8,128)(2,1)S(1)}, u32[]{:S(2)}, u32[]{:S(2)}) collective-permute-start(s16[2,528,256]{2,1,0:T(8,128)(2,1)} %pass_on.15), channel_id=1, source_target_pairs={{0,2},{1,3},{2,0},{3,1},{4,6},{5,7},{6,4},{7,5},{8,10},{9,11},{10,... | collective-permute-start | bytes 1622024 | tf_op jit(solution)/shard_map/ppermute | solution.py:239
  170.8 15.9 %copy-start.1 = (f32[2,512,256]{2,1,0:T(8,128)S(1)}, f32[2,512,256]{2,1,0:T(8,128)}, u32[]{:S(2)}) copy-start(f32[2,512,256]{2,1,0:T(8,128)} %get-tuple-element.57.refs_0_) | copy-start | bytes 3145732
  186.3 15.6 %collective-permute-start.24 = (s16[2,528,256]{2,1,0:T(8,128)(2,1)}, s16[2,528,256]{2,1,0:T(8,128)(2,1)S(1)}, u32[]{:S(2)}, u32[]{:S(2)}) collective-permute-start(s16[2,528,256]{2,1,0:T(8,128)(2,1)} %get-tuple-element.55), channel_id=1, source_target_pairs={{0,1},{1,0},{2,3},{3,2},{4,5},{5,4},{6,7},{7,6},{8,9},{9,8},{10,11... | collective-permute-start | bytes 1622024 | tf_op jit(solution)/shard_map/ppermute | solution.py:239
  191.2 16.5 %collective-permute-start.25 = (s16[2,528,256]{2,1,0:T(8,128)(2,1)}, s16[2,528,256]{2,1,0:T(8,128)(2,1)}, u32[]{:S(2)}, u32[]{:S(2)}) collective-permute-start(s16[2,528,256]{2,1,0:T(8,128)(2,1)} %pass_on.17), channel_id=1, source_target_pairs={{2,4},{3,5},{4,2},{5,3},{10,12},{11,13},{12,10},{13,11},{18,20},{1... | collective-permute-start | bytes 1622024 | tf_op jit(solution)/shard_map/ppermute | solution.py:239
  194.2 17.9 %collective-permute-start.26 = (s16[2,528,256]{2,1,0:T(8,128)(2,1)}, s16[2,528,256]{2,1,0:T(8,128)(2,1)}, u32[]{:S(2)}, u32[]{:S(2)}) collective-permute-start(s16[2,528,256]{2,1,0:T(8,128)(2,1)} %pass_on.19), channel_id=1, source_target_pairs={{0,2},{1,3},{6,4},{7,5},{8,10},{9,11},{14,12},{15,13},{16,18},{17,... | collective-permute-start | bytes 1622024 | tf_op jit(solution)/shard_map/ppermute | solution.py:239
  199.9 16.6 %collective-permute-start.17 = (s16[2,528,256]{2,1,0:T(8,128)(2,1)}, s16[2,528,256]{2,1,0:T(8,128)(2,1)}, u32[]{:S(2)}, u32[]{:S(2)}) collective-permute-start(s16[2,528,256]{2,1,0:T(8,128)(2,1)} %get-tuple-element.54), channel_id=1, source_target_pairs={{0,1},{1,0},{2,3},{3,2},{4,5},{5,4},{6,7},{7,6},{8,9},{9,8},{10,11... | collective-permute-start | bytes 1622024 | tf_op jit(solution)/shard_map/ppermute | solution.py:239
  200.4 16.0 %collective-permute-start.20 = (s16[2,528,256]{2,1,0:T(8,128)(2,1)}, s16[2,528,256]{2,1,0:T(8,128)(2,1)}, u32[]{:S(2)}, u32[]{:S(2)}) collective-permute-start(s16[2,528,256]{2,1,0:T(8,128)(2,1)} %copy-done.8), channel_id=1, source_target_pairs={{2,4},{3,5},{4,2},{5,3},{10,12},{11,13},{12,10},{13,11},{18,20},{1... | collective-permute-start | bytes 1622024 | tf_op jit(solution)/shard_map/ppermute | solution.py:239
  201.9 18.0 %collective-permute-start.23 = (s16[2,528,256]{2,1,0:T(8,128)(2,1)}, s16[2,528,256]{2,1,0:T(8,128)(2,1)}, u32[]{:S(2)}, u32[]{:S(2)}) collective-permute-start(s16[2,528,256]{2,1,0:T(8,128)(2,1)} %copy-done.9), channel_id=1, source_target_pairs={{0,2},{1,3},{6,4},{7,5},{8,10},{9,11},{14,12},{15,13},{16,18},{17,... | collective-permute-start | bytes 1622024 | tf_op jit(solution)/shard_map/ppermute | solution.py:239
  216.3 8.3 %collective-permute-start.33 = (f32[128,256]{1,0:T(8,128)S(1)}, f32[128,256]{1,0:T(8,128)S(1)}, u32[]{:S(2)}, u32[]{:S(2)}) collective-permute-start(f32[128,256]{1,0:T(8,128)S(1)} %dynamic-slice_bitcast_fusion), channel_id=1, source_target_pairs={{0,8},{1,9},{2,10},{3,11},{4,12},{5,13},{6,14},{7,15},{8,0},{9,1},... | collective-permute-start | bytes 393224 | tf_op jit(solution)/shard_map/ppermute | solution.py:239
  224.5 30.1 %copy-start.11 = (bf16[1024,256]{1,0:T(8,128)(2,1)S(1)}, bf16[1024,256]{1,0:T(8,128)(2,1)}, u32[]{:S(2)}) copy-start(bf16[1024,256]{1,0:T(8,128)(2,1)} %copy-done.10) | copy-start | bytes 1572868
  224.6 1.4 collective-permute-start.27
  224.7 6.4 %collective-permute-start.34 = (f32[128,256]{1,0:T(8,128)S(1)}, f32[128,256]{1,0:T(8,128)S(1)}, u32[]{:S(2)}, u32[]{:S(2)}) collective-permute-start(f32[128,256]{1,0:T(8,128)S(1)} %bitcast_add_fusion), channel_id=1, source_target_pairs={{0,1},{1,0},{2,3},{3,2},{4,5},{5,4},{6,7},{7,6},{8,9},{9,8},{10,11... | collective-permute-start | bytes 393224 | tf_op jit(solution)/shard_map/ppermute | solution.py:239
  226.0 7.4 %collective-permute-start.28 = (f32[128,256]{1,0:T(8,128)S(1)}, f32[128,256]{1,0:T(8,128)S(1)}, u32[]{:S(2)}, u32[]{:S(2)}) collective-permute-start(f32[128,256]{1,0:T(8,128)S(1)} %bitcast_add_fusion.1), channel_id=1, source_target_pairs={{0,1},{1,0},{2,3},{3,2},{4,5},{5,4},{6,7},{7,6},{8,9},{9,8},{10,11... | collective-permute-start | bytes 393224 | tf_op jit(solution)/shard_map/ppermute | solution.py:239
  231.1 5.3 %collective-permute-start.35 = (f32[128,256]{1,0:T(8,128)S(1)}, f32[128,256]{1,0:T(8,128)S(1)}, u32[]{:S(2)}, u32[]{:S(2)}) collective-permute-start(f32[128,256]{1,0:T(8,128)S(1)} %add.225), channel_id=1, source_target_pairs={{0,16},{1,17},{2,18},{3,19},{4,20},{5,21},{6,22},{7,23},{8,24},{9,... | collective-permute-start | bytes 393224 | tf_op jit(solution)/shard_map/ppermute | solution.py:239
  233.5 5.4 %collective-permute-start.29 = (f32[128,256]{1,0:T(8,128)S(1)}, f32[128,256]{1,0:T(8,128)S(1)}, u32[]{:S(2)}, u32[]{:S(2)}) collective-permute-start(f32[128,256]{1,0:T(8,128)S(1)} %add.220), channel_id=1, source_target_pairs={{0,16},{1,17},{2,18},{3,19},{4,20},{5,21},{6,22},{7,23},{8,24},{9,... | collective-permute-start | bytes 393224 | tf_op jit(solution)/shard_map/ppermute | solution.py:239
  236.4 6.0 %collective-permute-start.36 = (f32[128,256]{1,0:T(8,128)S(1)}, f32[128,256]{1,0:T(8,128)S(1)}, u32[]{:S(2)}, u32[]{:S(2)}) collective-permute-start(f32[128,256]{1,0:T(8,128)S(1)} %add.226), channel_id=1, source_target_pairs={{0,2},{1,3},{2,0},{3,1},{4,6},{5,7},{6,4},{7,5},{8,10},{9,11},{10,... | collective-permute-start | bytes 393224 | tf_op jit(solution)/shard_map/ppermute | solution.py:239
  238.9 7.1 %collective-permute-start.30 = (f32[128,256]{1,0:T(8,128)S(1)}, f32[128,256]{1,0:T(8,128)S(1)}, u32[]{:S(2)}, u32[]{:S(2)}) collective-permute-start(f32[128,256]{1,0:T(8,128)S(1)} %add.221), channel_id=1, source_target_pairs={{0,2},{1,3},{2,0},{3,1},{4,6},{5,7},{6,4},{7,5},{8,10},{9,11},{10,... | collective-permute-start | bytes 393224 | tf_op jit(solution)/shard_map/ppermute | solution.py:239
  242.3 12.2 %collective-permute-start.37 = (f32[128,256]{1,0:T(8,128)S(1)}, f32[128,256]{1,0:T(8,128)S(1)}, u32[]{:S(2)}, u32[]{:S(2)}) collective-permute-start(f32[128,256]{1,0:T(8,128)S(1)} %add.227), channel_id=1, source_target_pairs={{0,4},{1,5},{2,6},{3,7},{4,0},{5,1},{6,2},{7,3},{8,12},{9,13},{10,... | collective-permute-start | bytes 393224 | tf_op jit(solution)/shard_map/ppermute | solution.py:239
  246.1 10.0 %collective-permute-start.31 = (f32[128,256]{1,0:T(8,128)S(1)}, f32[128,256]{1,0:T(8,128)S(1)}, u32[]{:S(2)}, u32[]{:S(2)}) collective-permute-start(f32[128,256]{1,0:T(8,128)S(1)} %add.222), channel_id=1, source_target_pairs={{0,4},{1,5},{2,6},{3,7},{4,0},{5,1},{6,2},{7,3},{8,12},{9,13},{10,... | collective-permute-start | bytes 393224 | tf_op jit(solution)/shard_map/ppermute | solution.py:239
  254.6 1.7 collective-permute-start.38
  256.1 1.4 collective-permute-start.32
  (9 other events, 31.9 us)

commit v3 on v2

--- a/solution.py
+++ b/solution.py
@@ -13,8 +13,13 @@
 BF16 = jnp.bfloat16
 SCALE_ROWS = 16
 VMEM_BYTES = 16 * 1024 * 1024
-LIGHT = pl.CostEstimate(flops=1, bytes_accessed=1, transcendentals=0)
-PRODUCT_BYTES = 60 * 1024 * 1024
+
+
+def cost(flops, size):
+    return pl.CostEstimate(flops=int(flops), bytes_accessed=int(size), transcendentals=0)
+
+
+PRODUCT_BYTES = 36 * 1024 * 1024
 
 
 def encode(values, out_ref):
@@ -81,7 +86,7 @@
         ),
         out_shape=[msg_shape, own_shape] * groups,
         compiler_params=pltpu.CompilerParams(vmem_limit_bytes=PRODUCT_BYTES),
-        cost_estimate=LIGHT,
+        cost_estimate=cost(4 * depth * width * n * groups, 4 * depth * width),
         name="product",
     )(info, ancestor, *parts)
     return outs[::2], outs[1::2]
@@ -118,7 +123,7 @@
         ),
         out_shape=jax.ShapeDtypeStruct(msg.shape, msg.dtype),
         compiler_params=pltpu.CompilerParams(vmem_limit_bytes=VMEM_BYTES),
-        cost_estimate=LIGHT,
+        cost_estimate=cost(0, 8 * msg.size),
         name="pass_on",
     )(use, *flat)
 
@@ -165,7 +170,7 @@
             jax.ShapeDtypeStruct((snodes, width, width), F32),
         ],
         compiler_params=pltpu.CompilerParams(vmem_limit_bytes=VMEM_BYTES),
-        cost_estimate=LIGHT,
+        cost_estimate=cost(0, 12 * masked.size),
         name="finish",
     )(use, *flat, masked, keep)
 
@@ -320,7 +325,6 @@
         def multiply(q):
             nonlocal last
             info = jnp.stack([order[q] * 2 + 1 - low, order[q] * 2 + low] + places)
-            info, last = lax.optimization_barrier((info, last))
             msgs, kept = product(info, ancestor_inverse, pieces, depth, tile, snodes)
             for k in range(snodes):
                 own[k][q] = kept[k]
@@ -328,11 +332,10 @@
             last = msgs[-1]
 
         def advance(turn, k):
-            nonlocal last
             slots, before, use = needs(turn)
-            use, last = lax.optimization_barrier((jnp.asarray(use, jnp.int32)[place], last))
-            last = pass_on(use, [(own[k][q], got[k][q]) for q in slots], [moved[k][t] for t in before])
-            moved[k].append(move(last, along(rounds[turn])))
+            use = jnp.asarray(use, jnp.int32)[place]
+            sent = pass_on(use, [(own[k][q], got[k][q]) for q in slots], [moved[k][t] for t in before])
+            moved[k].append(move(sent, along(rounds[turn])))
 
         multiply(0)
         ready = 1

time: 259 us -> 248 us (0.958)
  waiting for transfers between devices: 74.4 us -> 66.2 us
  Pallas kernels: 82.9 us -> 78.4 us
    ppermute x39, waiting for transfers between devices: 74.4 us -> 66.2 us  [move(): return lax.ppermute(array, AXES, pairs)]
    pallas_call x4, Pallas kernels: 61.8 us -> 54.2 us  [product(): pl.pallas_call(functools.partial(product_kernel, tiles, len(parts)), grid...]
    unnamed x38 -> x50, local copies, waits for them, and re-layouts: 4.15 us -> 8.24 us
    pallas_call x10, Pallas kernels: 14.1 us -> 17.4 us  [pass_on(): pl.pallas_call(functools.partial(pass_on_kernel, len(pairs)), grid_spec=p...]
  transfers between devices with their start and end apart: 39 -> 39, of which waited for: 19 -> 15; matrix products, arithmetic and copies ran while one was open for 3% -> 2% of each run, Pallas kernels for 26% -> 26%
where the time goes in v3:
time: 248 us; the launch traced here: 247 us
  starting transfers between devices  81.6 us (33%)
  Pallas kernels  78.4 us (32%)
  waiting for transfers between devices  66.2 us (27%)
  local copies, waits for them, and re-layouts  13.4 us (5%)
  other arithmetic  3.7 us (1%)
  between operations  3.64 us (1%)
    ppermute x39, starting transfers between devices, move(): return lax.ppermute(array, AXES, pairs)  81.6 us
    ppermute x39, waiting for transfers between devices, move(): return lax.ppermute(array, AXES, pairs)  66.2 us
    pallas_call x4, Pallas kernels, product(): pl.pallas_call(functools.partial(product_kernel, tiles, len(parts)), grid...  54.2 us
    pallas_call x10, Pallas kernels, pass_on(): pl.pallas_call(functools.partial(pass_on_kernel, len(pairs)), grid_spec=p...  17.4 us
    unnamed x50, local copies, waits for them, and re-layouts  8.24 us
    pallas_call x2, Pallas kernels, finish(): pl.pallas_call(functools.partial(finish_kernel, len(moved)), grid_spec=pl...  6.82 us
  transfers between devices with their start and end apart: 39, of which 15 were waited for; matrix products, arithmetic and copies ran while one was open for 2% of the time, Pallas kernels for 26%

profile of v3, /device:TPU:0, one launch (start us, length us, event | category | flops | bytes accessed | tf_op | source)
XLA Modules:
  0.0 246.9 jit_solution(3476013098345733859)
XLA Ops:
  4.1 2.9 %collective-permute-start = (bf16[512,512]{1,0:T(8,128)(2,1)S(1)}, bf16[512,512]{1,0:T(8,128)(2,1)S(1)}, u32[]{:S(2)}, u32[]{:S(2)}) collective-permute-start(bf16[512,512]{1,0:T(8,128)(2,1)S(1)} %constant_dynamic-slice_fusion.1), channel_id=1, source_target_pairs={{0,16},{1,17},{2,18},{3,19},{4,20},{5,21},{6,22},{7,23},{8,24},{9,... | collective-permute-start | bytes 1572872 | tf_op jit(solution)/shard_map/ppermute | solution.py:244
  7.0 11.9 %collective-permute-done = bf16[512,512]{1,0:T(8,128)(2,1)S(1)} collective-permute-done((bf16[512,512]{1,0:T(8,128)(2,1)S(1)}, bf16[512,512]{1,0:T(8,128)(2,1)S(1)}, u32[]{:S(2)}, u32[]{:S(2)}) %collective-permute-start) | collective-permute-done | bytes 524320 | tf_op jit(solution)/shard_map/ppermute | solution.py:244
  19.9 7.3 %collective-permute-start.5 = (bf16[512,512]{1,0:T(8,128)(2,1)S(1)}, bf16[512,512]{1,0:T(8,128)(2,1)S(1)}, u32[]{:S(2)}, u32[]{:S(2)}) collective-permute-start(bf16[512,512]{1,0:T(8,128)(2,1)S(1)} %get-tuple-element.42), channel_id=1, source_target_pairs={{0,4},{1,12},{2,0},{3,8},{4,5},{5,13},{6,1},{7,9},{8,6},{9,14},{10... | collective-permute-start | bytes 1572872 | tf_op jit(solution)/shard_map/ppermute | solution.py:244
  27.2 10.2 %collective-permute-start.2 = (bf16[512,512]{1,0:T(8,128)(2,1)S(1)}, bf16[512,512]{1,0:T(8,128)(2,1)S(1)}, u32[]{:S(2)}, u32[]{:S(2)}) collective-permute-start(bf16[512,512]{1,0:T(8,128)(2,1)S(1)} %collective-permute-done.1.refs_0_), channel_id=1, source_target_pairs={{0,16},{1,17},{2,18},{3,19},{4,20},{5,21},{6,22},{7,23},{8,24},{9,... | collective-permute-start | bytes 1572872 | tf_op jit(solution)/shard_map/ppermute | solution.py:244
  37.4 2.1 collective-permute-done.5.refs_4_
  39.6 3.7 %collective-permute-start.3 = (bf16[512,512]{1,0:T(8,128)(2,1)S(1)}, bf16[512,512]{1,0:T(8,128)(2,1)S(1)}, u32[]{:S(2)}, u32[]{:S(2)}) collective-permute-start(bf16[512,512]{1,0:T(8,128)(2,1)S(1)} %collective-permute-done.1.refs_0_), channel_id=1, source_target_pairs={{0,8},{1,9},{2,10},{3,11},{4,12},{5,13},{6,14},{7,15},{8,0},{9,1},... | collective-permute-start | bytes 1572872 | tf_op jit(solution)/shard_map/ppermute | solution.py:244
  43.2 7.0 %collective-permute-done.2.refs_1_ = bf16[512,512]{1,0:T(8,128)(2,1)S(1)} collective-permute-done((bf16[512,512]{1,0:T(8,128)(2,1)S(1)}, bf16[512,512]{1,0:T(8,128)(2,1)S(1)}, u32[]{:S(2)}, u32[]{:S(2)}) %collective-permute-start.2) | collective-permute-done | bytes 524320 | tf_op jit(solution)/shard_map/ppermute | solution.py:244
  50.2 11.0 %collective-permute-done.6.refs_5_ = bf16[512,512]{1,0:T(8,128)(2,1)S(1)} collective-permute-done((bf16[512,512]{1,0:T(8,128)(2,1)S(1)}, bf16[512,512]{1,0:T(8,128)(2,1)S(1)}, u32[]{:S(2)}, u32[]{:S(2)}) %collective-permute-start.6) | collective-permute-done | bytes 524320 | tf_op jit(solution)/shard_map/ppermute | solution.py:244
  63.3 13.8 %product.6 = (s16[2,528,256]{2,1,0:T(8,128)(2,1)}, f32[2,512,256]{2,1,0:T(8,128)S(1)}, s16[2,528,256]{2,1,0:T(8,128)(2,1)}, f32[2,512,256]{2,1,0:T(8,128)S(1)}) custom-call(s32[10]{0:T(128)S(1)} %stack.118.info_ref, bf16[8192,4096]{1,0:T(8,128)(2,1)} %a_ref.7, bf16[512,512]{1,0:T(8,128)(2,1)S(1)} %collective-permute-done.1.refs_0_, ...), custom_call_target="tpu_custom_call" | custom-call | flops 8589934592 | bytes 16777216 | tf_op jit(solution)/shard_map/product/pallas_call | solution.py:78
  79.1 11.9 %collective-permute-start.11 = (s16[2,528,256]{2,1,0:T(8,128)(2,1)}, s16[2,528,256]{2,1,0:T(8,128)(2,1)}, u32[]{:S(2)}, u32[]{:S(2)}) collective-permute-start(s16[2,528,256]{2,1,0:T(8,128)(2,1)} %get-tuple-element.27), channel_id=1, source_target_pairs={{0,1},{1,0},{2,3},{3,2},{4,5},{5,4},{6,7},{7,6},{8,9},{9,8},{10,11... | collective-permute-start | bytes 1622024 | tf_op jit(solution)/shard_map/ppermute | solution.py:244
  93.8 10.6 %collective-permute-done.11.refs_1_ = s16[2,528,256]{2,1,0:T(8,128)(2,1)} collective-permute-done((s16[2,528,256]{2,1,0:T(8,128)(2,1)}, s16[2,528,256]{2,1,0:T(8,128)(2,1)}, u32[]{:S(2)}, u32[]{:S(2)}) %collective-permute-start.11) | collective-permute-done | bytes 540704 | tf_op jit(solution)/shard_map/ppermute | solution.py:244
  104.4 1.2 copy-done.5
  105.6 1.3 pass_on.10
  107.0 4.0 %collective-permute-start.12 = (s16[2,528,256]{2,1,0:T(8,128)(2,1)S(1)}, s16[2,528,256]{2,1,0:T(8,128)(2,1)S(1)}, u32[]{:S(2)}, u32[]{:S(2)}) collective-permute-start(s16[2,528,256]{2,1,0:T(8,128)(2,1)S(1)} %pass_on.10), channel_id=1, source_target_pairs={{0,2},{1,3},{6,4},{7,5},{8,10},{9,11},{14,12},{15,13},{16,18},{17,... | collective-permute-start | bytes 1622024 | tf_op jit(solution)/shard_map/ppermute | solution.py:244
  111.0 4.8 %collective-permute-done.20.refs_1_ = s16[2,528,256]{2,1,0:T(8,128)(2,1)} collective-permute-done((s16[2,528,256]{2,1,0:T(8,128)(2,1)}, s16[2,528,256]{2,1,0:T(8,128)(2,1)}, u32[]{:S(2)}, u32[]{:S(2)}) %collective-permute-start.20) | collective-permute-done | bytes 540704 | tf_op jit(solution)/shard_map/ppermute | solution.py:244
  115.8 1.3 pass_on.15
  117.1 4.0 %collective-permute-start.21 = (s16[2,528,256]{2,1,0:T(8,128)(2,1)S(1)}, s16[2,528,256]{2,1,0:T(8,128)(2,1)S(1)}, u32[]{:S(2)}, u32[]{:S(2)}) collective-permute-start(s16[2,528,256]{2,1,0:T(8,128)(2,1)S(1)} %pass_on.15), channel_id=1, source_target_pairs={{0,2},{1,3},{6,4},{7,5},{8,10},{9,11},{14,12},{15,13},{16,18},{17,... | collective-permute-start | bytes 1622024 | tf_op jit(solution)/shard_map/ppermute | solution.py:244
  121.1 13.0 %product.5 = (s16[2,528,256]{2,1,0:T(8,128)(2,1)S(1)}, f32[2,512,256]{2,1,0:T(8,128)S(1)}, s16[2,528,256]{2,1,0:T(8,128)(2,1)S(1)}, f32[2,512,256]{2,1,0:T(8,128)S(1)}) custom-call(s32[10]{0:T(128)S(1)} %stack.115.info_ref, bf16[8192,4096]{1,0:T(8,128)(2,1)} %a_ref.7, bf16[512,512]{1,0:T(8,128)(2,1)S(1)} %collective-permute-done.1.refs_0_, ...), custom_call_target="tpu_custom_call" | custom-call | flops 8589934592 | bytes 16777216 | tf_op jit(solution)/shard_map/product/pallas_call | solution.py:78
  134.4 1.7 collective-permute-start.19
  136.2 2.0 pass_on.11
  139.0 2.0 pass_on.16
  141.9 13.7 %product.7 = (s16[2,528,256]{2,1,0:T(8,128)(2,1)S(1)}, f32[2,512,256]{2,1,0:T(8,128)S(1)}, s16[2,528,256]{2,1,0:T(8,128)(2,1)}, f32[2,512,256]{2,1,0:T(8,128)S(1)}) custom-call(s32[10]{0:T(128)S(1)} %stack.121.info_ref, bf16[8192,4096]{1,0:T(8,128)(2,1)} %a_ref.7, bf16[512,512]{1,0:T(8,128)(2,1)S(1)} %collective-permute-done.1.refs_0_, ...), custom_call_target="tpu_custom_call" | custom-call | flops 8589934592 | bytes 16777216 | tf_op jit(solution)/shard_map/product/pallas_call | solution.py:78
  155.9 1.7 collective-permute-start.24
  157.6 1.1 pass_on.12
  158.7 3.9 %collective-permute-start.14 = (s16[2,528,256]{2,1,0:T(8,128)(2,1)S(1)}, s16[2,528,256]{2,1,0:T(8,128)(2,1)S(1)}, u32[]{:S(2)}, u32[]{:S(2)}) collective-permute-start(s16[2,528,256]{2,1,0:T(8,128)(2,1)S(1)} %pass_on.12), channel_id=1, source_target_pairs={{0,2},{1,3},{2,0},{3,1},{4,6},{5,7},{6,4},{7,5},{8,10},{9,11},{10,... | collective-permute-start | bytes 1622024 | tf_op jit(solution)/shard_map/ppermute | solution.py:244
  162.6 1.8 pass_on.17
  164.4 1.8 collective-permute-start.23
  166.2 13.7 %product.4 = (s16[2,528,256]{2,1,0:T(8,128)(2,1)}, f32[2,512,256]{2,1,0:T(8,128)S(1)}, s16[2,528,256]{2,1,0:T(8,128)(2,1)S(1)}, f32[2,512,256]{2,1,0:T(8,128)S(1)}) custom-call(s32[10]{0:T(128)S(1)} %stack.112.info_ref, bf16[8192,4096]{1,0:T(8,128)(2,1)} %a_ref.7, bf16[512,512]{1,0:T(8,128)(2,1)S(1)} %collective-permute-done.1.refs_0_, ...), custom_call_target="tpu_custom_call" | custom-call | flops 8589934592 | bytes 16777216 | tf_op jit(solution)/shard_map/product/pallas_call | solution.py:78
  181.5 2.1 collective-permute-start.17
  183.6 1.8 pass_on.13
  185.4 1.5 collective-permute-start.16
  186.9 1.6 collective-permute-start.18
  188.5 2.2 pass_on.19
  190.7 3.9 %collective-permute-start.26 = (s16[2,528,256]{2,1,0:T(8,128)(2,1)}, s16[2,528,256]{2,1,0:T(8,128)(2,1)}, u32[]{:S(2)}, u32[]{:S(2)}) collective-permute-start(s16[2,528,256]{2,1,0:T(8,128)(2,1)} %pass_on.19), channel_id=1, source_target_pairs={{0,2},{1,3},{6,4},{7,5},{8,10},{9,11},{14,12},{15,13},{16,18},{17,... | collective-permute-start | bytes 1622024 | tf_op jit(solution)/shard_map/ppermute | solution.py:244
  194.5 2.8 %pass_on.18 = s16[2,528,256]{2,1,0:T(8,128)(2,1)} custom-call(s32[2]{0:T(128)S(1)} %fusion.1.use_ref, f32[2,512,256]{2,1,0:T(8,128)S(1)} %copy-done.1, s16[2,528,256]{2,1,0:T(8,128)(2,1)} %collective-permute-done.24.refs_1_, s16[2,528,256]{2,1,0:T(8,128)(2,1)} %collective-permute-done.23.refs_2_.refs_0_), custom_call_target="tpu_custom_call" | custom-call | bytes 2162688 | tf_op jit(solution)/shard_map/pass_on/pallas_call | solution.py:116
  197.4 1.4 collective-permute-start.25
  202.2 3.3 %finish.2 = (bf16[1024,256]{1,0:T(8,128)(2,1)S(1)}, f32[1,256,256]{2,1,0:T(8,128)S(1)}) custom-call(s32[4]{0:T(128)S(1)} %fusion.use_ref, f32[2,512,256]{2,1,0:T(8,128)S(1)} %copy-done.12, s16[2,528,256]{2,1,0:T(8,128)(2,1)S(1)} %collective-permute-done.9.msg_ref, s16[2,528,256]{2,1,0:T(8,128)(2,1)S(1)} %copy-done.8, ...), custom_call_target="tpu_custom_call" | custom-call | bytes 3145728 | tf_op jit(solution)/shard_map/finish/pallas_call | solution.py:160
  207.2 3.5 %finish.3 = (bf16[1024,256]{1,0:T(8,128)(2,1)S(1)}, f32[1,256,256]{2,1,0:T(8,128)S(1)}) custom-call(s32[4]{0:T(128)S(1)} %fusion.use_ref, f32[2,512,256]{2,1,0:T(8,128)S(1)} %copy-done.10, s16[2,528,256]{2,1,0:T(8,128)(2,1)S(1)} %collective-permute-done.18.msg_ref, s16[2,528,256]{2,1,0:T(8,128)(2,1)} %collective-permute-done.23.refs_2_.refs_0_, ...), custom_call_target="tpu_custom_call" | custom-call | bytes 3145728 | tf_op jit(solution)/shard_map/finish/pallas_call | solution.py:160
  212.4 1.8 collective-permute-start.34
  214.2 4.2 %collective-permute-done.28 = f32[128,256]{1,0:T(8,128)S(1)} collective-permute-done((f32[128,256]{1,0:T(8,128)S(1)}, f32[128,256]{1,0:T(8,128)S(1)}, u32[]{:S(2)}, u32[]{:S(2)}) %collective-permute-start.28) | collective-permute-done | bytes 131104 | tf_op jit(solution)/shard_map/ppermute | solution.py:244
  218.8 1.7 collective-permute-done.34
  220.9 3.5 %collective-permute-done.29 = f32[128,256]{1,0:T(8,128)S(1)} collective-permute-done((f32[128,256]{1,0:T(8,128)S(1)}, f32[128,256]{1,0:T(8,128)S(1)}, u32[]{:S(2)}, u32[]{:S(2)}) %collective-permute-start.29) | collective-permute-done | bytes 131104 | tf_op jit(solution)/shard_map/ppermute | solution.py:244
  224.4 2.8 %collective-permute-start.30 = (f32[128,256]{1,0:T(8,128)S(1)}, f32[128,256]{1,0:T(8,128)S(1)}, u32[]{:S(2)}, u32[]{:S(2)}) collective-permute-start(f32[128,256]{1,0:T(8,128)S(1)} %add.221), channel_id=1, source_target_pairs={{0,2},{1,3},{2,0},{3,1},{4,6},{5,7},{6,4},{7,5},{8,10},{9,11},{10,... | collective-permute-start | bytes 393224 | tf_op jit(solution)/shard_map/ppermute | solution.py:244
  227.2 2.5 collective-permute-start.36
  230.7 3.2 %collective-permute-start.31 = (f32[128,256]{1,0:T(8,128)S(1)}, f32[128,256]{1,0:T(8,128)S(1)}, u32[]{:S(2)}, u32[]{:S(2)}) collective-permute-start(f32[128,256]{1,0:T(8,128)S(1)} %add.222), channel_id=1, source_target_pairs={{0,4},{1,5},{2,6},{3,7},{4,0},{5,1},{6,2},{7,3},{8,12},{9,13},{10,... | collective-permute-start | bytes 393224 | tf_op jit(solution)/shard_map/ppermute | solution.py:244
  234.4 2.6 %collective-permute-start.37 = (f32[128,256]{1,0:T(8,128)S(1)}, f32[128,256]{1,0:T(8,128)S(1)}, u32[]{:S(2)}, u32[]{:S(2)}) collective-permute-start(f32[128,256]{1,0:T(8,128)S(1)} %add.227), channel_id=1, source_target_pairs={{0,4},{1,5},{2,6},{3,7},{4,0},{5,1},{6,2},{7,3},{8,12},{9,13},{10,... | collective-permute-start | bytes 393224 | tf_op jit(solution)/shard_map/ppermute | solution.py:244
  237.0 6.0 %collective-permute-done.31 = f32[128,256]{1,0:T(8,128)S(1)} collective-permute-done((f32[128,256]{1,0:T(8,128)S(1)}, f32[128,256]{1,0:T(8,128)S(1)}, u32[]{:S(2)}, u32[]{:S(2)}) %collective-permute-start.31) | collective-permute-done | bytes 131104 | tf_op jit(solution)/shard_map/ppermute | solution.py:244
  244.8 1.2 collective-permute-done.38
  (132 shorter events, 24.2 us)
Async XLA Ops:
  3.4 23.8 %copy-start.20 = (bf16[1024,512]{1,0:T(8,128)(2,1)}, bf16[1024,512]{1,0:T(8,128)(2,1)S(1)}, u32[]{:S(2)}) copy-start(bf16[1024,512]{1,0:T(8,128)(2,1)S(1)} %mul.115) | copy-start | bytes 3145732
  4.1 14.9 %collective-permute-start = (bf16[512,512]{1,0:T(8,128)(2,1)S(1)}, bf16[512,512]{1,0:T(8,128)(2,1)S(1)}, u32[]{:S(2)}, u32[]{:S(2)}) collective-permute-start(bf16[512,512]{1,0:T(8,128)(2,1)S(1)} %constant_dynamic-slice_fusion.1), channel_id=1, source_target_pairs={{0,16},{1,17},{2,18},{3,19},{4,20},{5,21},{6,22},{7,23},{8,24},{9,... | collective-permute-start | bytes 1572872 | tf_op jit(solution)/shard_map/ppermute | solution.py:244
  19.2 8.0 %collective-permute-start.1 = (bf16[512,512]{1,0:T(8,128)(2,1)S(1)}, bf16[512,512]{1,0:T(8,128)(2,1)S(1)}, u32[]{:S(2)}, u32[]{:S(2)}) collective-permute-start(bf16[512,512]{1,0:T(8,128)(2,1)S(1)} %get-tuple-element.43), channel_id=1, source_target_pairs={{0,0},{1,8},{2,4},{3,12},{4,1},{5,9},{6,5},{7,13},{8,2},{9,10},{10... | collective-permute-start | bytes 1572872 | tf_op jit(solution)/shard_map/ppermute | solution.py:244
  19.9 19.7 %collective-permute-start.5 = (bf16[512,512]{1,0:T(8,128)(2,1)S(1)}, bf16[512,512]{1,0:T(8,128)(2,1)S(1)}, u32[]{:S(2)}, u32[]{:S(2)}) collective-permute-start(bf16[512,512]{1,0:T(8,128)(2,1)S(1)} %get-tuple-element.42), channel_id=1, source_target_pairs={{0,4},{1,12},{2,0},{3,8},{4,5},{5,13},{6,1},{7,9},{8,6},{9,14},{10... | collective-permute-start | bytes 1572872 | tf_op jit(solution)/shard_map/ppermute | solution.py:244
  27.2 23.0 %collective-permute-start.2 = (bf16[512,512]{1,0:T(8,128)(2,1)S(1)}, bf16[512,512]{1,0:T(8,128)(2,1)S(1)}, u32[]{:S(2)}, u32[]{:S(2)}) collective-permute-start(bf16[512,512]{1,0:T(8,128)(2,1)S(1)} %collective-permute-done.1.refs_0_), channel_id=1, source_target_pairs={{0,16},{1,17},{2,18},{3,19},{4,20},{5,21},{6,22},{7,23},{8,24},{9,... | collective-permute-start | bytes 1572872 | tf_op jit(solution)/shard_map/ppermute | solution.py:244
  39.6 21.7 %collective-permute-start.6 = (bf16[512,512]{1,0:T(8,128)(2,1)S(1)}, bf16[512,512]{1,0:T(8,128)(2,1)S(1)}, u32[]{:S(2)}, u32[]{:S(2)}) collective-permute-start(bf16[512,512]{1,0:T(8,128)(2,1)S(1)} %collective-permute-done.5.refs_4_), channel_id=1, source_target_pairs={{0,16},{1,17},{2,18},{3,19},{4,20},{5,21},{6,22},{7,23},{8,24},{9,... | collective-permute-start | bytes 1572872 | tf_op jit(solution)/shard_map/ppermute | solution.py:244
  39.6 23.7 %collective-permute-start.3 = (bf16[512,512]{1,0:T(8,128)(2,1)S(1)}, bf16[512,512]{1,0:T(8,128)(2,1)S(1)}, u32[]{:S(2)}, u32[]{:S(2)}) collective-permute-start(bf16[512,512]{1,0:T(8,128)(2,1)S(1)} %collective-permute-done.1.refs_0_), channel_id=1, source_target_pairs={{0,8},{1,9},{2,10},{3,11},{4,12},{5,13},{6,14},{7,15},{8,0},{9,1},... | collective-permute-start | bytes 1572872 | tf_op jit(solution)/shard_map/ppermute | solution.py:244
  43.2 20.1 %collective-permute-start.7 = (bf16[512,512]{1,0:T(8,128)(2,1)S(1)}, bf16[512,512]{1,0:T(8,128)(2,1)S(1)}, u32[]{:S(2)}, u32[]{:S(2)}) collective-permute-start(bf16[512,512]{1,0:T(8,128)(2,1)S(1)} %collective-permute-done.5.refs_4_), channel_id=1, source_target_pairs={{0,8},{1,9},{2,10},{3,11},{4,12},{5,13},{6,14},{7,15},{8,0},{9,1},... | collective-permute-start | bytes 1572872 | tf_op jit(solution)/shard_map/ppermute | solution.py:244
  50.2 13.1 %collective-permute-start.4 = (bf16[512,512]{1,0:T(8,128)(2,1)S(1)}, bf16[512,512]{1,0:T(8,128)(2,1)}, u32[]{:S(2)}, u32[]{:S(2)}) collective-permute-start(bf16[512,512]{1,0:T(8,128)(2,1)S(1)} %collective-permute-done.2.refs_1_), channel_id=1, source_target_pairs={{0,8},{1,9},{2,10},{3,11},{4,12},{5,13},{6,14},{7,15},{8,0},{9,1},... | collective-permute-start | bytes 1572872 | tf_op jit(solution)/shard_map/ppermute | solution.py:244
  61.2 2.1 collective-permute-start.8
  79.1 25.3 %collective-permute-start.11 = (s16[2,528,256]{2,1,0:T(8,128)(2,1)}, s16[2,528,256]{2,1,0:T(8,128)(2,1)}, u32[]{:S(2)}, u32[]{:S(2)}) collective-permute-start(s16[2,528,256]{2,1,0:T(8,128)(2,1)} %get-tuple-element.27), channel_id=1, source_target_pairs={{0,1},{1,0},{2,3},{3,2},{4,5},{5,4},{6,7},{7,6},{8,9},{9,8},{10,11... | collective-permute-start | bytes 1622024 | tf_op jit(solution)/shard_map/ppermute | solution.py:244
  91.0 24.8 %collective-permute-start.20 = (s16[2,528,256]{2,1,0:T(8,128)(2,1)}, s16[2,528,256]{2,1,0:T(8,128)(2,1)}, u32[]{:S(2)}, u32[]{:S(2)}) collective-permute-start(s16[2,528,256]{2,1,0:T(8,128)(2,1)} %get-tuple-element.36), channel_id=1, source_target_pairs={{0,1},{1,0},{2,3},{3,2},{4,5},{5,4},{6,7},{7,6},{8,9},{9,8},{10,11... | collective-permute-start | bytes 1622024 | tf_op jit(solution)/shard_map/ppermute | solution.py:244
  93.1 22.8 %copy-start.3 = (f32[2,512,256]{2,1,0:T(8,128)S(1)}, f32[2,512,256]{2,1,0:T(8,128)}, u32[]{:S(2)}) copy-start(f32[2,512,256]{2,1,0:T(8,128)} %copy-done.2) | copy-start | bytes 3145732
  107.0 29.2 %collective-permute-start.12 = (s16[2,528,256]{2,1,0:T(8,128)(2,1)S(1)}, s16[2,528,256]{2,1,0:T(8,128)(2,1)S(1)}, u32[]{:S(2)}, u32[]{:S(2)}) collective-permute-start(s16[2,528,256]{2,1,0:T(8,128)(2,1)S(1)} %pass_on.10), channel_id=1, source_target_pairs={{0,2},{1,3},{6,4},{7,5},{8,10},{9,11},{14,12},{15,13},{16,18},{17,... | collective-permute-start | bytes 1622024 | tf_op jit(solution)/shard_map/ppermute | solution.py:244
  117.1 19.1 %copy-start.6 = (f32[2,512,256]{2,1,0:T(8,128)S(1)}, f32[2,512,256]{2,1,0:T(8,128)}, u32[]{:S(2)}) copy-start(f32[2,512,256]{2,1,0:T(8,128)} %copy-done.4) | copy-start | bytes 3145732
  117.1 21.8 %collective-permute-start.21 = (s16[2,528,256]{2,1,0:T(8,128)(2,1)S(1)}, s16[2,528,256]{2,1,0:T(8,128)(2,1)S(1)}, u32[]{:S(2)}, u32[]{:S(2)}) collective-permute-start(s16[2,528,256]{2,1,0:T(8,128)(2,1)S(1)} %pass_on.15), channel_id=1, source_target_pairs={{0,2},{1,3},{6,4},{7,5},{8,10},{9,11},{14,12},{15,13},{16,18},{17,... | collective-permute-start | bytes 1622024 | tf_op jit(solution)/shard_map/ppermute | solution.py:244
  134.1 21.8 %collective-permute-start.10 = (s16[2,528,256]{2,1,0:T(8,128)(2,1)S(1)}, s16[2,528,256]{2,1,0:T(8,128)(2,1)S(1)}, u32[]{:S(2)}, u32[]{:S(2)}) collective-permute-start(s16[2,528,256]{2,1,0:T(8,128)(2,1)S(1)} %get-tuple-element.25), channel_id=1, source_target_pairs={{0,1},{1,0},{2,3},{3,2},{4,5},{5,4},{6,7},{7,6},{8,9},{9,8},{10,11... | collective-permute-start | bytes 1622024 | tf_op jit(solution)/shard_map/ppermute | solution.py:244
  134.4 28.1 %collective-permute-start.19 = (s16[2,528,256]{2,1,0:T(8,128)(2,1)S(1)}, s16[2,528,256]{2,1,0:T(8,128)(2,1)S(1)}, u32[]{:S(2)}, u32[]{:S(2)}) collective-permute-start(s16[2,528,256]{2,1,0:T(8,128)(2,1)S(1)} %get-tuple-element.34), channel_id=1, source_target_pairs={{0,1},{1,0},{2,3},{3,2},{4,5},{5,4},{6,7},{7,6},{8,9},{9,8},{10,11... | collective-permute-start | bytes 1622024 | tf_op jit(solution)/shard_map/ppermute | solution.py:244
  138.2 19.4 %collective-permute-start.13 = (s16[2,528,256]{2,1,0:T(8,128)(2,1)S(1)}, s16[2,528,256]{2,1,0:T(8,128)(2,1)S(1)}, u32[]{:S(2)}, u32[]{:S(2)}) collective-permute-start(s16[2,528,256]{2,1,0:T(8,128)(2,1)S(1)} %pass_on.11), channel_id=1, source_target_pairs={{2,4},{3,5},{4,2},{5,3},{10,12},{11,13},{12,10},{13,11},{18,20},{1... | collective-permute-start | bytes 1622024 | tf_op jit(solution)/shard_map/ppermute | solution.py:244
  141.0 21.6 %collective-permute-start.22 = (s16[2,528,256]{2,1,0:T(8,128)(2,1)S(1)}, s16[2,528,256]{2,1,0:T(8,128)(2,1)S(1)}, u32[]{:S(2)}, u32[]{:S(2)}) collective-permute-start(s16[2,528,256]{2,1,0:T(8,128)(2,1)S(1)} %pass_on.16), channel_id=1, source_target_pairs={{2,4},{3,5},{4,2},{5,3},{10,12},{11,13},{12,10},{13,11},{18,20},{1... | collective-permute-start | bytes 1622024 | tf_op jit(solution)/shard_map/ppermute | solution.py:244
  155.6 8.8 %copy-start = (f32[2,512,256]{2,1,0:T(8,128)}, f32[2,512,256]{2,1,0:T(8,128)S(1)}, u32[]{:S(2)}) copy-start(f32[2,512,256]{2,1,0:T(8,128)S(1)} %get-tuple-element.37.refs_0_) | copy-start | bytes 3145732
  155.6 24.8 %collective-permute-start.15 = (s16[2,528,256]{2,1,0:T(8,128)(2,1)S(1)}, s16[2,528,256]{2,1,0:T(8,128)(2,1)S(1)}, u32[]{:S(2)}, u32[]{:S(2)}) collective-permute-start(s16[2,528,256]{2,1,0:T(8,128)(2,1)S(1)} %get-tuple-element.29), channel_id=1, source_target_pairs={{0,1},{1,0},{2,3},{3,2},{4,5},{5,4},{6,7},{7,6},{8,9},{9,8},{10,11... | collective-permute-start | bytes 1622024 | tf_op jit(solution)/shard_map/ppermute | solution.py:244
  155.9 31.0 %collective-permute-start.24 = (s16[2,528,256]{2,1,0:T(8,128)(2,1)}, s16[2,528,256]{2,1,0:T(8,128)(2,1)}, u32[]{:S(2)}, u32[]{:S(2)}) collective-permute-start(s16[2,528,256]{2,1,0:T(8,128)(2,1)} %get-tuple-element.38), channel_id=1, source_target_pairs={{0,1},{1,0},{2,3},{3,2},{4,5},{5,4},{6,7},{7,6},{8,9},{9,8},{10,11... | collective-permute-start | bytes 1622024 | tf_op jit(solution)/shard_map/ppermute | solution.py:244
  158.7 24.9 %collective-permute-start.14 = (s16[2,528,256]{2,1,0:T(8,128)(2,1)S(1)}, s16[2,528,256]{2,1,0:T(8,128)(2,1)S(1)}, u32[]{:S(2)}, u32[]{:S(2)}) collective-permute-start(s16[2,528,256]{2,1,0:T(8,128)(2,1)S(1)} %pass_on.12), channel_id=1, source_target_pairs={{0,2},{1,3},{2,0},{3,1},{4,6},{5,7},{6,4},{7,5},{8,10},{9,11},{10,... | collective-permute-start | bytes 1622024 | tf_op jit(solution)/shard_map/ppermute | solution.py:244
  164.4 26.3 %collective-permute-start.23 = (s16[2,528,256]{2,1,0:T(8,128)(2,1)}, s16[2,528,256]{2,1,0:T(8,128)(2,1)}, u32[]{:S(2)}, u32[]{:S(2)}) collective-permute-start(s16[2,528,256]{2,1,0:T(8,128)(2,1)} %pass_on.17), channel_id=1, source_target_pairs={{0,2},{1,3},{2,0},{3,1},{4,6},{5,7},{6,4},{7,5},{8,10},{9,11},{10,... | collective-permute-start | bytes 1622024 | tf_op jit(solution)/shard_map/ppermute | solution.py:244
  179.9 5.5 %copy-start.17 = (s16[2,528,256]{2,1,0:T(8,128)(2,1)}, s16[2,528,256]{2,1,0:T(8,128)(2,1)S(1)}, u32[]{:S(2)}) copy-start(s16[2,528,256]{2,1,0:T(8,128)(2,1)S(1)} %get-tuple-element.32) | copy-start | bytes 1622020
  179.9 17.5 %collective-permute-start.9 = (s16[2,528,256]{2,1,0:T(8,128)(2,1)}, s16[2,528,256]{2,1,0:T(8,128)(2,1)S(1)}, u32[]{:S(2)}, u32[]{:S(2)}) collective-permute-start(s16[2,528,256]{2,1,0:T(8,128)(2,1)} %get-tuple-element.23), channel_id=1, source_target_pairs={{0,1},{1,0},{2,3},{3,2},{4,5},{5,4},{6,7},{7,6},{8,9},{9,8},{10,11... | collective-permute-start | bytes 1622024 | tf_op jit(solution)/shard_map/ppermute | solution.py:244
  180.4 8.1 %copy-start.1 = (f32[2,512,256]{2,1,0:T(8,128)S(1)}, f32[2,512,256]{2,1,0:T(8,128)}, u32[]{:S(2)}) copy-start(f32[2,512,256]{2,1,0:T(8,128)} %copy-done) | copy-start | bytes 3145732
  181.5 18.2 %collective-permute-start.17 = (s16[2,528,256]{2,1,0:T(8,128)(2,1)}, s16[2,528,256]{2,1,0:T(8,128)(2,1)S(1)}, u32[]{:S(2)}, u32[]{:S(2)}) collective-permute-start(s16[2,528,256]{2,1,0:T(8,128)(2,1)} %pass_on.14), channel_id=1, source_target_pairs={{0,2},{1,3},{6,4},{7,5},{8,10},{9,11},{14,12},{15,13},{16,18},{17,... | collective-permute-start | bytes 1622024 | tf_op jit(solution)/shard_map/ppermute | solution.py:244
  185.4 15.1 %collective-permute-start.16 = (s16[2,528,256]{2,1,0:T(8,128)(2,1)}, s16[2,528,256]{2,1,0:T(8,128)(2,1)}, u32[]{:S(2)}, u32[]{:S(2)}) collective-permute-start(s16[2,528,256]{2,1,0:T(8,128)(2,1)} %pass_on.13), channel_id=1, source_target_pairs={{2,4},{3,5},{4,2},{5,3},{10,12},{11,13},{12,10},{13,11},{18,20},{1... | collective-permute-start | bytes 1622024 | tf_op jit(solution)/shard_map/ppermute | solution.py:244
  186.9 20.1 %collective-permute-start.18 = (s16[2,528,256]{2,1,0:T(8,128)(2,1)}, s16[2,528,256]{2,1,0:T(8,128)(2,1)S(1)}, u32[]{:S(2)}, u32[]{:S(2)}) collective-permute-start(s16[2,528,256]{2,1,0:T(8,128)(2,1)} %copy-done.17), channel_id=1, source_target_pairs={{0,1},{1,0},{2,3},{3,2},{4,5},{5,4},{6,7},{7,6},{8,9},{9,8},{10,11... | collective-permute-start | bytes 1622024 | tf_op jit(solution)/shard_map/ppermute | solution.py:244
  188.5 11.0 %copy-start.19 = (bf16[128,8,2,256]{3,1,2,0:T(8,128)(2,1)S(1)}, bf16[128,8,2,256]{3,1,2,0:T(8,128)(2,1)}, u32[]{:S(2)}) copy-start(bf16[128,8,2,256]{3,1,2,0:T(8,128)(2,1)} %copy-done.18) | copy-start | bytes 3145732
  188.5 11.0 %copy-start.21 = (bf16[1024,512]{1,0:T(8,128)(2,1)S(1)}, bf16[1024,512]{1,0:T(8,128)(2,1)}, u32[]{:S(2)}) copy-start(bf16[1024,512]{1,0:T(8,128)(2,1)} %copy-done.20) | copy-start | bytes 3145732
  190.7 16.5 %collective-permute-start.26 = (s16[2,528,256]{2,1,0:T(8,128)(2,1)}, s16[2,528,256]{2,1,0:T(8,128)(2,1)}, u32[]{:S(2)}, u32[]{:S(2)}) collective-permute-start(s16[2,528,256]{2,1,0:T(8,128)(2,1)} %pass_on.19), channel_id=1, source_target_pairs={{0,2},{1,3},{6,4},{7,5},{8,10},{9,11},{14,12},{15,13},{16,18},{17,... | collective-permute-start | bytes 1622024 | tf_op jit(solution)/shard_map/ppermute | solution.py:244
  197.4 9.8 %collective-permute-start.25 = (s16[2,528,256]{2,1,0:T(8,128)(2,1)}, s16[2,528,256]{2,1,0:T(8,128)(2,1)}, u32[]{:S(2)}, u32[]{:S(2)}) collective-permute-start(s16[2,528,256]{2,1,0:T(8,128)(2,1)} %pass_on.18), channel_id=1, source_target_pairs={{2,4},{3,5},{4,2},{5,3},{10,12},{11,13},{12,10},{13,11},{18,20},{1... | collective-permute-start | bytes 1622024 | tf_op jit(solution)/shard_map/ppermute | solution.py:244
  206.9 4.1 %collective-permute-start.27 = (f32[128,256]{1,0:T(8,128)}, f32[128,256]{1,0:T(8,128)}, u32[]{:S(2)}, u32[]{:S(2)}) collective-permute-start(f32[128,256]{1,0:T(8,128)} %dynamic-slice_bitcast_fusion.1), channel_id=1, source_target_pairs={{0,8},{1,9},{2,10},{3,11},{4,12},{5,13},{6,14},{7,15},{8,0},{9,1},... | collective-permute-start | bytes 393224 | tf_op jit(solution)/shard_map/ppermute | solution.py:244
  210.7 32.4 %copy-start.16 = (bf16[1024,256]{1,0:T(8,128)(2,1)S(1)}, bf16[1024,256]{1,0:T(8,128)(2,1)}, u32[]{:S(2)}) copy-start(bf16[1024,256]{1,0:T(8,128)(2,1)} %copy-done.15) | copy-start | bytes 1572868
  210.7 1.7 collective-permute-start.33
  212.0 6.4 %collective-permute-start.28 = (f32[128,256]{1,0:T(8,128)S(1)}, f32[128,256]{1,0:T(8,128)S(1)}, u32[]{:S(2)}, u32[]{:S(2)}) collective-permute-start(f32[128,256]{1,0:T(8,128)S(1)} %bitcast_add_fusion.1), channel_id=1, source_target_pairs={{0,1},{1,0},{2,3},{3,2},{4,5},{5,4},{6,7},{7,6},{8,9},{9,8},{10,11... | collective-permute-start | bytes 393224 | tf_op jit(solution)/shard_map/ppermute | solution.py:244
  212.4 8.1 %collective-permute-start.34 = (f32[128,256]{1,0:T(8,128)S(1)}, f32[128,256]{1,0:T(8,128)S(1)}, u32[]{:S(2)}, u32[]{:S(2)}) collective-permute-start(f32[128,256]{1,0:T(8,128)S(1)} %bitcast_add_fusion), channel_id=1, source_target_pairs={{0,1},{1,0},{2,3},{3,2},{4,5},{5,4},{6,7},{7,6},{8,9},{9,8},{10,11... | collective-permute-start | bytes 393224 | tf_op jit(solution)/shard_map/ppermute | solution.py:244
  218.4 6.0 %collective-permute-start.29 = (f32[128,256]{1,0:T(8,128)S(1)}, f32[128,256]{1,0:T(8,128)S(1)}, u32[]{:S(2)}, u32[]{:S(2)}) collective-permute-start(f32[128,256]{1,0:T(8,128)S(1)} %add.220), channel_id=1, source_target_pairs={{0,16},{1,17},{2,18},{3,19},{4,20},{5,21},{6,22},{7,23},{8,24},{9,... | collective-permute-start | bytes 393224 | tf_op jit(solution)/shard_map/ppermute | solution.py:244
  220.5 6.7 %collective-permute-start.35 = (f32[128,256]{1,0:T(8,128)S(1)}, f32[128,256]{1,0:T(8,128)S(1)}, u32[]{:S(2)}, u32[]{:S(2)}) collective-permute-start(f32[128,256]{1,0:T(8,128)S(1)} %add.225), channel_id=1, source_target_pairs={{0,16},{1,17},{2,18},{3,19},{4,20},{5,21},{6,22},{7,23},{8,24},{9,... | collective-permute-start | bytes 393224 | tf_op jit(solution)/shard_map/ppermute | solution.py:244
  224.4 6.2 %collective-permute-start.30 = (f32[128,256]{1,0:T(8,128)S(1)}, f32[128,256]{1,0:T(8,128)S(1)}, u32[]{:S(2)}, u32[]{:S(2)}) collective-permute-start(f32[128,256]{1,0:T(8,128)S(1)} %add.221), channel_id=1, source_target_pairs={{0,2},{1,3},{2,0},{3,1},{4,6},{5,7},{6,4},{7,5},{8,10},{9,11},{10,... | collective-permute-start | bytes 393224 | tf_op jit(solution)/shard_map/ppermute | solution.py:244
  227.2 7.1 %collective-permute-start.36 = (f32[128,256]{1,0:T(8,128)S(1)}, f32[128,256]{1,0:T(8,128)S(1)}, u32[]{:S(2)}, u32[]{:S(2)}) collective-permute-start(f32[128,256]{1,0:T(8,128)S(1)} %add.226), channel_id=1, source_target_pairs={{0,2},{1,3},{2,0},{3,1},{4,6},{5,7},{6,4},{7,5},{8,10},{9,11},{10,... | collective-permute-start | bytes 393224 | tf_op jit(solution)/shard_map/ppermute | solution.py:244
  230.7 12.4 %collective-permute-start.31 = (f32[128,256]{1,0:T(8,128)S(1)}, f32[128,256]{1,0:T(8,128)S(1)}, u32[]{:S(2)}, u32[]{:S(2)}) collective-permute-start(f32[128,256]{1,0:T(8,128)S(1)} %add.222), channel_id=1, source_target_pairs={{0,4},{1,5},{2,6},{3,7},{4,0},{5,1},{6,2},{7,3},{8,12},{9,13},{10,... | collective-permute-start | bytes 393224 | tf_op jit(solution)/shard_map/ppermute | solution.py:244
  234.4 10.2 %collective-permute-start.37 = (f32[128,256]{1,0:T(8,128)S(1)}, f32[128,256]{1,0:T(8,128)S(1)}, u32[]{:S(2)}, u32[]{:S(2)}) collective-permute-start(f32[128,256]{1,0:T(8,128)S(1)} %add.227), channel_id=1, source_target_pairs={{0,4},{1,5},{2,6},{3,7},{4,0},{5,1},{6,2},{7,3},{8,12},{9,13},{10,... | collective-permute-start | bytes 393224 | tf_op jit(solution)/shard_map/ppermute | solution.py:244
  243.0 1.7 collective-permute-start.32
  244.6 1.4 collective-permute-start.38
  (15 other events, 32.7 us)

commit v4 on v3

--- a/solution.py
+++ b/solution.py
@@ -19,7 +19,7 @@
     return pl.CostEstimate(flops=int(flops), bytes_accessed=int(size), transcendentals=0)
 
 
-PRODUCT_BYTES = 36 * 1024 * 1024
+PRODUCT_BYTES = 32 * 1024 * 1024
 
 
 def encode(values, out_ref):
@@ -81,7 +81,7 @@
             num_scalar_prefetch=1,
             grid=(2 * tiles,),
             in_specs=[pl.BlockSpec((tile, width), a_map)]
-            + [pl.BlockSpec(x.shape, lambda i, info_ref: (0, 0)) for x in parts],
+            + [pl.BlockSpec(x.shape, lambda i, info_ref: (0, 0), pipeline_mode=pl.Buffered(1)) for x in parts],
             out_specs=[msg_spec, own_spec] * groups,
         ),
         out_shape=[msg_shape, own_shape] * groups,
@@ -245,12 +245,13 @@
 
     ratio = cols // rows
 
-    def gather_pieces(masked, row_index, col_index):
+    def gather_pieces(masked, row_index, col_index, panel, keep_of):
         half = masked.shape[0] // 2
         plane, odd = row_index // 2, lax.rem(row_index, 2)
         stay = lax.dynamic_slice_in_dim(masked, plane * half, half, 0)
-        cross = lax.dynamic_slice_in_dim(masked, (1 - plane) * half, half, 0)
-        cross = move(cross, swap_rows(2))
+        cross = lax.dynamic_slice_in_dim(panel, (1 - plane) * half, half, 0)
+        begin = ((row_index + 2 - 4 * lax.rem(plane, 2)) * cols + col_index) * 2 * half + plane * half
+        cross = move(cross, swap_rows(2)) * keep_of(begin, half)
         is_own = col_index // ratio // 2 == plane
         upper_half = lax.rem(col_index, rows) // 2
         parts, places = [], []
@@ -268,7 +269,7 @@
                 places += [2 * (2 * pair + side) + plane, 2 * (2 * (1 - pair) + side) + 1 - plane]
         return parts, places
 
-    def gather_whole(masked, row_index, col_index):
+    def gather_whole(masked, row_index, col_index, panel, keep_of):
         row_block = lax.all_gather(masked, "col", axis=0, tiled=True)
         span = masked.shape[0] * rows
         own = lax.dynamic_slice_in_dim(row_block, lax.rem(col_index, ratio) * span, span, 0)
@@ -306,17 +307,20 @@
         tile = min(512, depth)
         row_index, col_index = lax.axis_index("row"), lax.axis_index("col")
         low, place = lax.rem(col_index, 2), col_index // 2
-        begin = (row_index * cols + col_index) * depth
-        same = math.gcd(depth, width)
-        blocks = depth // same
-        owners = (begin + jnp.arange(blocks, dtype=jnp.int32) * same) // width
-        keep = jnp.take(structure, owners, axis=1).astype(BF16)
-        keep = jnp.broadcast_to(keep.T[:, None, :, None], (blocks, same, snodes, width))
-        keep = keep.reshape(depth, snodes * width)
+
+        def keep_of(begin, length):
+            same = math.gcd(length, width)
+            blocks = length // same
+            owners = (begin + jnp.arange(blocks, dtype=jnp.int32) * same) // width
+            keep = jnp.take(structure, owners, axis=1).astype(BF16)
+            keep = jnp.broadcast_to(keep.T[:, None, :, None], (blocks, same, snodes, width))
+            return keep.reshape(length, snodes * width)
+
+        keep = keep_of((row_index * cols + col_index) * depth, depth)
         masked = panel * keep
         order = jnp.asarray(table, jnp.int32)[place]
         cuts = [slice(k * width, (k + 1) * width) for k in range(snodes)]
-        pieces, places = gather(masked, row_index, col_index)
+        pieces, places = gather(masked, row_index, col_index, panel, keep_of)
         own = [[None] * line for _ in cuts]
         got = [[None] * line for _ in cuts]
         moved = [[] for _ in cuts]

time: 248 us -> 251 us (1.012)
  local copies, waits for them, and re-layouts: 13.4 us -> 19 us
  Pallas kernels: 78.4 us -> 74.8 us
    unnamed x50 -> x51, local copies, waits for them, and re-layouts: 8.24 us -> 11.3 us
    pallas_call x10, Pallas kernels: 17.4 us -> 14.6 us  [pass_on(): pl.pallas_call(functools.partial(pass_on_kernel, len(pairs)), grid_spec=p...]
  transfers between devices with their start and end apart: 39 -> 39, of which waited for: 15 -> 17; matrix products, arithmetic and copies ran while one was open for 2% -> 4% of each run, Pallas kernels for 26% -> 24%
where the time goes in v4:
time: 251 us; the launch traced here: 250 us
  starting transfers between devices  84 us (33%)
  Pallas kernels  74.8 us (30%)
  waiting for transfers between devices  64 us (25%)
  local copies, waits for them, and re-layouts  19 us (8%)
  other arithmetic  3.99 us (2%)
  between operations  3.99 us (2%)
    ppermute x39, starting transfers between devices, move(): return lax.ppermute(array, AXES, pairs)  84 us
    ppermute x39, waiting for transfers between devices, move(): return lax.ppermute(array, AXES, pairs)  64 us
    pallas_call x4, Pallas kernels, product(): pl.pallas_call(functools.partial(product_kernel, tiles, len(parts)), grid...  53.5 us
    pallas_call x10, Pallas kernels, pass_on(): pl.pallas_call(functools.partial(pass_on_kernel, len(pairs)), grid_spec=p...  14.6 us
    unnamed x51, local copies, waits for them, and re-layouts  11.3 us
    pallas_call x2, Pallas kernels, finish(): pl.pallas_call(functools.partial(finish_kernel, len(moved)), grid_spec=pl...  6.72 us
  transfers between devices with their start and end apart: 39, of which 17 were waited for; matrix products, arithmetic and copies ran while one was open for 4% of the time, Pallas kernels for 24%

profile of v4, /device:TPU:0, one launch (start us, length us, event | category | flops | bytes accessed | tf_op | source)
XLA Modules:
  0.0 249.9 jit_solution(16928263039193316334)
XLA Ops:
  1.7 3.0 %collective-permute-start = (bf16[512,512]{1,0:T(8,128)(2,1)S(1)}, bf16[512,512]{1,0:T(8,128)(2,1)}, u32[]{:S(2)}, u32[]{:S(2)}) collective-permute-start(bf16[512,512]{1,0:T(8,128)(2,1)S(1)} %constant_dynamic-slice_fusion.1), channel_id=1, source_target_pairs={{0,16},{1,17},{2,18},{3,19},{4,20},{5,21},{6,22},{7,23},{8,24},{9,... | collective-permute-start | bytes 1572872 | tf_op jit(solution)/shard_map/ppermute | solution.py:244
  9.6 7.2 %collective-permute-done = bf16[512,512]{1,0:T(8,128)(2,1)} collective-permute-done((bf16[512,512]{1,0:T(8,128)(2,1)S(1)}, bf16[512,512]{1,0:T(8,128)(2,1)}, u32[]{:S(2)}, u32[]{:S(2)}) %collective-permute-start) | collective-permute-done | bytes 524320 | tf_op jit(solution)/shard_map/ppermute | solution.py:244
  16.8 1.3 broadcast_select_fusion
  18.8 7.3 %collective-permute-start.5 = (bf16[512,512]{1,0:T(8,128)(2,1)S(1)}, bf16[512,512]{1,0:T(8,128)(2,1)S(1)}, u32[]{:S(2)}, u32[]{:S(2)}) collective-permute-start(bf16[512,512]{1,0:T(8,128)(2,1)S(1)} %get-tuple-element.42), channel_id=1, source_target_pairs={{0,4},{1,12},{2,0},{3,8},{4,5},{5,13},{6,1},{7,9},{8,6},{9,14},{10... | collective-permute-start | bytes 1572872 | tf_op jit(solution)/shard_map/ppermute | solution.py:244
  26.0 10.3 %collective-permute-start.2 = (bf16[512,512]{1,0:T(8,128)(2,1)S(1)}, bf16[512,512]{1,0:T(8,128)(2,1)S(1)}, u32[]{:S(2)}, u32[]{:S(2)}) collective-permute-start(bf16[512,512]{1,0:T(8,128)(2,1)S(1)} %collective-permute-done.1.refs_0_), channel_id=1, source_target_pairs={{0,16},{1,17},{2,18},{3,19},{4,20},{5,21},{6,22},{7,23},{8,24},{9,... | collective-permute-start | bytes 1572872 | tf_op jit(solution)/shard_map/ppermute | solution.py:244
  36.3 2.1 collective-permute-done.5.refs_4_
  38.4 3.7 %collective-permute-start.3 = (bf16[512,512]{1,0:T(8,128)(2,1)S(1)}, bf16[512,512]{1,0:T(8,128)(2,1)S(1)}, u32[]{:S(2)}, u32[]{:S(2)}) collective-permute-start(bf16[512,512]{1,0:T(8,128)(2,1)S(1)} %collective-permute-done.1.refs_0_), channel_id=1, source_target_pairs={{0,8},{1,9},{2,10},{3,11},{4,12},{5,13},{6,14},{7,15},{8,0},{9,1},... | collective-permute-start | bytes 1572872 | tf_op jit(solution)/shard_map/ppermute | solution.py:244
  42.1 7.0 %collective-permute-done.2.refs_1_ = bf16[512,512]{1,0:T(8,128)(2,1)S(1)} collective-permute-done((bf16[512,512]{1,0:T(8,128)(2,1)S(1)}, bf16[512,512]{1,0:T(8,128)(2,1)S(1)}, u32[]{:S(2)}, u32[]{:S(2)}) %collective-permute-start.2) | collective-permute-done | bytes 524320 | tf_op jit(solution)/shard_map/ppermute | solution.py:244
  49.1 11.0 %collective-permute-done.6.refs_5_ = bf16[512,512]{1,0:T(8,128)(2,1)S(1)} collective-permute-done((bf16[512,512]{1,0:T(8,128)(2,1)S(1)}, bf16[512,512]{1,0:T(8,128)(2,1)S(1)}, u32[]{:S(2)}, u32[]{:S(2)}) %collective-permute-start.6) | collective-permute-done | bytes 524320 | tf_op jit(solution)/shard_map/ppermute | solution.py:244
  62.3 13.8 %product.6 = (s16[2,528,256]{2,1,0:T(8,128)(2,1)}, f32[2,512,256]{2,1,0:T(8,128)S(1)}, s16[2,528,256]{2,1,0:T(8,128)(2,1)}, f32[2,512,256]{2,1,0:T(8,128)S(1)}) custom-call(s32[10]{0:T(128)S(1)} %stack.118.info_ref, bf16[8192,4096]{1,0:T(8,128)(2,1)} %a_ref.7, bf16[512,512]{1,0:T(8,128)(2,1)S(1)} %collective-permute-done.1.refs_0_, ...), custom_call_target="tpu_custom_call" | custom-call | flops 8589934592 | bytes 16777216 | tf_op jit(solution)/shard_map/product/pallas_call | solution.py:78
  78.1 11.9 %collective-permute-start.11 = (s16[2,528,256]{2,1,0:T(8,128)(2,1)}, s16[2,528,256]{2,1,0:T(8,128)(2,1)}, u32[]{:S(2)}, u32[]{:S(2)}) collective-permute-start(s16[2,528,256]{2,1,0:T(8,128)(2,1)} %get-tuple-element.27), channel_id=1, source_target_pairs={{0,1},{1,0},{2,3},{3,2},{4,5},{5,4},{6,7},{7,6},{8,9},{9,8},{10,11... | collective-permute-start | bytes 1622024 | tf_op jit(solution)/shard_map/ppermute | solution.py:244
  93.0 10.3 %collective-permute-done.11.refs_1_ = s16[2,528,256]{2,1,0:T(8,128)(2,1)} collective-permute-done((s16[2,528,256]{2,1,0:T(8,128)(2,1)}, s16[2,528,256]{2,1,0:T(8,128)(2,1)}, u32[]{:S(2)}, u32[]{:S(2)}) %collective-permute-start.11) | collective-permute-done | bytes 540704 | tf_op jit(solution)/shard_map/ppermute | solution.py:244
  103.4 1.2 copy-done.3
  104.6 1.3 pass_on.10
  105.9 4.0 %collective-permute-start.12 = (s16[2,528,256]{2,1,0:T(8,128)(2,1)S(1)}, s16[2,528,256]{2,1,0:T(8,128)(2,1)S(1)}, u32[]{:S(2)}, u32[]{:S(2)}) collective-permute-start(s16[2,528,256]{2,1,0:T(8,128)(2,1)S(1)} %pass_on.10), channel_id=1, source_target_pairs={{0,2},{1,3},{6,4},{7,5},{8,10},{9,11},{14,12},{15,13},{16,18},{17,... | collective-permute-start | bytes 1622024 | tf_op jit(solution)/shard_map/ppermute | solution.py:244
  110.0 4.8 %collective-permute-done.20.refs_1_ = s16[2,528,256]{2,1,0:T(8,128)(2,1)} collective-permute-done((s16[2,528,256]{2,1,0:T(8,128)(2,1)}, s16[2,528,256]{2,1,0:T(8,128)(2,1)}, u32[]{:S(2)}, u32[]{:S(2)}) %collective-permute-start.20) | collective-permute-done | bytes 540704 | tf_op jit(solution)/shard_map/ppermute | solution.py:244
  114.8 1.3 pass_on.15
  116.1 4.0 %collective-permute-start.21 = (s16[2,528,256]{2,1,0:T(8,128)(2,1)S(1)}, s16[2,528,256]{2,1,0:T(8,128)(2,1)S(1)}, u32[]{:S(2)}, u32[]{:S(2)}) collective-permute-start(s16[2,528,256]{2,1,0:T(8,128)(2,1)S(1)} %pass_on.15), channel_id=1, source_target_pairs={{0,2},{1,3},{6,4},{7,5},{8,10},{9,11},{14,12},{15,13},{16,18},{17,... | collective-permute-start | bytes 1622024 | tf_op jit(solution)/shard_map/ppermute | solution.py:244
  120.1 13.0 %product.5 = (s16[2,528,256]{2,1,0:T(8,128)(2,1)S(1)}, f32[2,512,256]{2,1,0:T(8,128)S(1)}, s16[2,528,256]{2,1,0:T(8,128)(2,1)S(1)}, f32[2,512,256]{2,1,0:T(8,128)S(1)}) custom-call(s32[10]{0:T(128)S(1)} %stack.115.info_ref, bf16[8192,4096]{1,0:T(8,128)(2,1)} %a_ref.7, bf16[512,512]{1,0:T(8,128)(2,1)S(1)} %collective-permute-done.1.refs_0_, ...), custom_call_target="tpu_custom_call" | custom-call | flops 8589934592 | bytes 16777216 | tf_op jit(solution)/shard_map/product/pallas_call | solution.py:78
  133.4 1.7 collective-permute-start.19
  135.2 2.1 pass_on.11
  137.9 2.1 pass_on.16
  140.9 13.0 %product.7 = (s16[2,528,256]{2,1,0:T(8,128)(2,1)S(1)}, f32[2,512,256]{2,1,0:T(8,128)S(1)}, s16[2,528,256]{2,1,0:T(8,128)(2,1)S(1)}, f32[2,512,256]{2,1,0:T(8,128)S(1)}) custom-call(s32[10]{0:T(128)S(1)} %stack.121.info_ref, bf16[8192,4096]{1,0:T(8,128)(2,1)} %a_ref.7, bf16[512,512]{1,0:T(8,128)(2,1)S(1)} %collective-permute-done.1.refs_0_, ...), custom_call_target="tpu_custom_call" | custom-call | flops 8589934592 | bytes 16777216 | tf_op jit(solution)/shard_map/product/pallas_call | solution.py:78
  154.2 1.7 collective-permute-start.24
  157.0 3.9 %collective-permute-start.14 = (s16[2,528,256]{2,1,0:T(8,128)(2,1)S(1)}, s16[2,528,256]{2,1,0:T(8,128)(2,1)S(1)}, u32[]{:S(2)}, u32[]{:S(2)}) collective-permute-start(s16[2,528,256]{2,1,0:T(8,128)(2,1)S(1)} %pass_on.12), channel_id=1, source_target_pairs={{0,2},{1,3},{2,0},{3,1},{4,6},{5,7},{6,4},{7,5},{8,10},{9,11},{10,... | collective-permute-start | bytes 1622024 | tf_op jit(solution)/shard_map/ppermute | solution.py:244
  162.0 2.5 %collective-permute-start.23 = (s16[2,528,256]{2,1,0:T(8,128)(2,1)S(1)}, s16[2,528,256]{2,1,0:T(8,128)(2,1)S(1)}, u32[]{:S(2)}, u32[]{:S(2)}) collective-permute-start(s16[2,528,256]{2,1,0:T(8,128)(2,1)S(1)} %pass_on.17), channel_id=1, source_target_pairs={{0,2},{1,3},{2,0},{3,1},{4,6},{5,7},{6,4},{7,5},{8,10},{9,11},{10,... | collective-permute-start | bytes 1622024 | tf_op jit(solution)/shard_map/ppermute | solution.py:244
  164.6 13.7 %product.4 = (s16[2,528,256]{2,1,0:T(8,128)(2,1)S(1)}, f32[2,512,256]{2,1,0:T(8,128)S(1)}, s16[2,528,256]{2,1,0:T(8,128)(2,1)}, f32[2,512,256]{2,1,0:T(8,128)S(1)}) custom-call(s32[10]{0:T(128)S(1)} %stack.112.info_ref, bf16[8192,4096]{1,0:T(8,128)(2,1)} %a_ref.7, bf16[512,512]{1,0:T(8,128)(2,1)S(1)} %collective-permute-done.1.refs_0_, ...), custom_call_target="tpu_custom_call" | custom-call | flops 8589934592 | bytes 16777216 | tf_op jit(solution)/shard_map/product/pallas_call | solution.py:78
  178.7 1.6 collective-permute-start.18
  181.3 1.8 collective-permute-done.24.refs_1_
  183.1 3.4 %collective-permute-start.17 = (s16[2,528,256]{2,1,0:T(8,128)(2,1)}, s16[2,528,256]{2,1,0:T(8,128)(2,1)S(1)}, u32[]{:S(2)}, u32[]{:S(2)}) collective-permute-start(s16[2,528,256]{2,1,0:T(8,128)(2,1)} %pass_on.14), channel_id=1, source_target_pairs={{0,2},{1,3},{6,4},{7,5},{8,10},{9,11},{14,12},{15,13},{16,18},{17,... | collective-permute-start | bytes 1622024 | tf_op jit(solution)/shard_map/ppermute | solution.py:244
  187.6 2.2 collective-permute-start.26
  189.8 1.8 pass_on.13
  191.6 1.5 collective-permute-start.16
  193.1 1.8 pass_on.18
  195.7 1.6 collective-permute-start.25
  198.1 1.3 fusion.4
  200.3 1.2 copy-done.12
  202.6 3.3 %finish.2 = (bf16[1024,256]{1,0:T(8,128)(2,1)S(1)}, f32[1,256,256]{2,1,0:T(8,128)S(1)}) custom-call(s32[4]{0:T(128)S(1)} %fusion.use_ref, f32[2,512,256]{2,1,0:T(8,128)S(1)} %copy-done.12, s16[2,528,256]{2,1,0:T(8,128)(2,1)S(1)} %copy-done.14, s16[2,528,256]{2,1,0:T(8,128)(2,1)S(1)} %copy-done.8, s16[2,528,256]{2,1,0:T(8,128)(2,1)} %collective-permute-done.16.refs_1_, ...), custom_call_target="tpu_custom_call" | custom-call | bytes 3145728 | tf_op jit(solution)/shard_map/finish/pallas_call | solution.py:160
  206.9 1.2 copy-done.10
  208.1 3.4 %finish.3 = (bf16[1024,256]{1,0:T(8,128)(2,1)S(1)}, f32[1,256,256]{2,1,0:T(8,128)S(1)}) custom-call(s32[4]{0:T(128)S(1)} %fusion.use_ref, f32[2,512,256]{2,1,0:T(8,128)S(1)} %copy-done.10, s16[2,528,256]{2,1,0:T(8,128)(2,1)S(1)} %collective-permute-done.18.msg_ref, s16[2,528,256]{2,1,0:T(8,128)(2,1)S(1)} %copy-done.6, ...), custom_call_target="tpu_custom_call" | custom-call | bytes 3145728 | tf_op jit(solution)/shard_map/finish/pallas_call | solution.py:160
  214.3 4.2 %collective-permute-done.28 = f32[128,256]{1,0:T(8,128)S(1)} collective-permute-done((f32[128,256]{1,0:T(8,128)S(1)}, f32[128,256]{1,0:T(8,128)S(1)}, u32[]{:S(2)}, u32[]{:S(2)}) %collective-permute-start.28) | collective-permute-done | bytes 131104 | tf_op jit(solution)/shard_map/ppermute | solution.py:244
  218.9 1.5 collective-permute-done.34
  220.8 4.1 %collective-permute-done.29 = f32[128,256]{1,0:T(8,128)S(1)} collective-permute-done((f32[128,256]{1,0:T(8,128)S(1)}, f32[128,256]{1,0:T(8,128)S(1)}, u32[]{:S(2)}, u32[]{:S(2)}) %collective-permute-start.29) | collective-permute-done | bytes 131104 | tf_op jit(solution)/shard_map/ppermute | solution.py:244
  224.9 5.2 %collective-permute-start.30 = (f32[128,256]{1,0:T(8,128)S(1)}, f32[128,256]{1,0:T(8,128)S(1)}, u32[]{:S(2)}, u32[]{:S(2)}) collective-permute-start(f32[128,256]{1,0:T(8,128)S(1)} %add.283), channel_id=1, source_target_pairs={{0,2},{1,3},{2,0},{3,1},{4,6},{5,7},{6,4},{7,5},{8,10},{9,11},{10,... | collective-permute-start | bytes 393224 | tf_op jit(solution)/shard_map/ppermute | solution.py:244
  230.2 2.4 collective-permute-start.36
  233.7 3.1 %collective-permute-start.31 = (f32[128,256]{1,0:T(8,128)S(1)}, f32[128,256]{1,0:T(8,128)S(1)}, u32[]{:S(2)}, u32[]{:S(2)}) collective-permute-start(f32[128,256]{1,0:T(8,128)S(1)} %add.284), channel_id=1, source_target_pairs={{0,4},{1,5},{2,6},{3,7},{4,0},{5,1},{6,2},{7,3},{8,12},{9,13},{10,... | collective-permute-start | bytes 393224 | tf_op jit(solution)/shard_map/ppermute | solution.py:244
  237.3 2.5 %collective-permute-start.37 = (f32[128,256]{1,0:T(8,128)S(1)}, f32[128,256]{1,0:T(8,128)S(1)}, u32[]{:S(2)}, u32[]{:S(2)}) collective-permute-start(f32[128,256]{1,0:T(8,128)S(1)} %add.289), channel_id=1, source_target_pairs={{0,4},{1,5},{2,6},{3,7},{4,0},{5,1},{6,2},{7,3},{8,12},{9,13},{10,... | collective-permute-start | bytes 393224 | tf_op jit(solution)/shard_map/ppermute | solution.py:244
  239.8 6.1 %collective-permute-done.31 = f32[128,256]{1,0:T(8,128)S(1)} collective-permute-done((f32[128,256]{1,0:T(8,128)S(1)}, f32[128,256]{1,0:T(8,128)S(1)}, u32[]{:S(2)}, u32[]{:S(2)}) %collective-permute-start.31) | collective-permute-done | bytes 131104 | tf_op jit(solution)/shard_map/ppermute | solution.py:244
  (140 shorter events, 31.5 us)
Async XLA Ops:
  1.7 15.0 %collective-permute-start = (bf16[512,512]{1,0:T(8,128)(2,1)S(1)}, bf16[512,512]{1,0:T(8,128)(2,1)}, u32[]{:S(2)}, u32[]{:S(2)}) collective-permute-start(bf16[512,512]{1,0:T(8,128)(2,1)S(1)} %constant_dynamic-slice_fusion.1), channel_id=1, source_target_pairs={{0,16},{1,17},{2,18},{3,19},{4,20},{5,21},{6,22},{7,23},{8,24},{9,... | collective-permute-start | bytes 1572872 | tf_op jit(solution)/shard_map/ppermute | solution.py:244
  9.6 8.5 %copy-start.20 = (bf16[1024,512]{1,0:T(8,128)(2,1)}, bf16[1024,512]{1,0:T(8,128)(2,1)S(1)}, u32[]{:S(2)}) copy-start(bf16[1024,512]{1,0:T(8,128)(2,1)S(1)} %mul.143) | copy-start | bytes 3145732
  18.1 8.0 %collective-permute-start.1 = (bf16[512,512]{1,0:T(8,128)(2,1)S(1)}, bf16[512,512]{1,0:T(8,128)(2,1)S(1)}, u32[]{:S(2)}, u32[]{:S(2)}) collective-permute-start(bf16[512,512]{1,0:T(8,128)(2,1)S(1)} %get-tuple-element.43), channel_id=1, source_target_pairs={{0,0},{1,8},{2,4},{3,12},{4,1},{5,9},{6,5},{7,13},{8,2},{9,10},{10... | collective-permute-start | bytes 1572872 | tf_op jit(solution)/shard_map/ppermute | solution.py:244
  18.8 19.7 %collective-permute-start.5 = (bf16[512,512]{1,0:T(8,128)(2,1)S(1)}, bf16[512,512]{1,0:T(8,128)(2,1)S(1)}, u32[]{:S(2)}, u32[]{:S(2)}) collective-permute-start(bf16[512,512]{1,0:T(8,128)(2,1)S(1)} %get-tuple-element.42), channel_id=1, source_target_pairs={{0,4},{1,12},{2,0},{3,8},{4,5},{5,13},{6,1},{7,9},{8,6},{9,14},{10... | collective-permute-start | bytes 1572872 | tf_op jit(solution)/shard_map/ppermute | solution.py:244
  26.0 23.0 %collective-permute-start.2 = (bf16[512,512]{1,0:T(8,128)(2,1)S(1)}, bf16[512,512]{1,0:T(8,128)(2,1)S(1)}, u32[]{:S(2)}, u32[]{:S(2)}) collective-permute-start(bf16[512,512]{1,0:T(8,128)(2,1)S(1)} %collective-permute-done.1.refs_0_), channel_id=1, source_target_pairs={{0,16},{1,17},{2,18},{3,19},{4,20},{5,21},{6,22},{7,23},{8,24},{9,... | collective-permute-start | bytes 1572872 | tf_op jit(solution)/shard_map/ppermute | solution.py:244
  38.4 21.7 %collective-permute-start.6 = (bf16[512,512]{1,0:T(8,128)(2,1)S(1)}, bf16[512,512]{1,0:T(8,128)(2,1)S(1)}, u32[]{:S(2)}, u32[]{:S(2)}) collective-permute-start(bf16[512,512]{1,0:T(8,128)(2,1)S(1)} %collective-permute-done.5.refs_4_), channel_id=1, source_target_pairs={{0,16},{1,17},{2,18},{3,19},{4,20},{5,21},{6,22},{7,23},{8,24},{9,... | collective-permute-start | bytes 1572872 | tf_op jit(solution)/shard_map/ppermute | solution.py:244
  38.4 23.8 %collective-permute-start.3 = (bf16[512,512]{1,0:T(8,128)(2,1)S(1)}, bf16[512,512]{1,0:T(8,128)(2,1)S(1)}, u32[]{:S(2)}, u32[]{:S(2)}) collective-permute-start(bf16[512,512]{1,0:T(8,128)(2,1)S(1)} %collective-permute-done.1.refs_0_), channel_id=1, source_target_pairs={{0,8},{1,9},{2,10},{3,11},{4,12},{5,13},{6,14},{7,15},{8,0},{9,1},... | collective-permute-start | bytes 1572872 | tf_op jit(solution)/shard_map/ppermute | solution.py:244
  42.1 20.1 %collective-permute-start.7 = (bf16[512,512]{1,0:T(8,128)(2,1)S(1)}, bf16[512,512]{1,0:T(8,128)(2,1)S(1)}, u32[]{:S(2)}, u32[]{:S(2)}) collective-permute-start(bf16[512,512]{1,0:T(8,128)(2,1)S(1)} %collective-permute-done.5.refs_4_), channel_id=1, source_target_pairs={{0,8},{1,9},{2,10},{3,11},{4,12},{5,13},{6,14},{7,15},{8,0},{9,1},... | collective-permute-start | bytes 1572872 | tf_op jit(solution)/shard_map/ppermute | solution.py:244
  49.1 13.2 %collective-permute-start.4 = (bf16[512,512]{1,0:T(8,128)(2,1)S(1)}, bf16[512,512]{1,0:T(8,128)(2,1)}, u32[]{:S(2)}, u32[]{:S(2)}) collective-permute-start(bf16[512,512]{1,0:T(8,128)(2,1)S(1)} %collective-permute-done.2.refs_1_), channel_id=1, source_target_pairs={{0,8},{1,9},{2,10},{3,11},{4,12},{5,13},{6,14},{7,15},{8,0},{9,1},... | collective-permute-start | bytes 1572872 | tf_op jit(solution)/shard_map/ppermute | solution.py:244
  60.1 2.2 collective-permute-start.8
  78.1 25.3 %collective-permute-start.11 = (s16[2,528,256]{2,1,0:T(8,128)(2,1)}, s16[2,528,256]{2,1,0:T(8,128)(2,1)}, u32[]{:S(2)}, u32[]{:S(2)}) collective-permute-start(s16[2,528,256]{2,1,0:T(8,128)(2,1)} %get-tuple-element.27), channel_id=1, source_target_pairs={{0,1},{1,0},{2,3},{3,2},{4,5},{5,4},{6,7},{7,6},{8,9},{9,8},{10,11... | collective-permute-start | bytes 1622024 | tf_op jit(solution)/shard_map/ppermute | solution.py:244
  89.9 24.8 %collective-permute-start.20 = (s16[2,528,256]{2,1,0:T(8,128)(2,1)}, s16[2,528,256]{2,1,0:T(8,128)(2,1)}, u32[]{:S(2)}, u32[]{:S(2)}) collective-permute-start(s16[2,528,256]{2,1,0:T(8,128)(2,1)} %get-tuple-element.36), channel_id=1, source_target_pairs={{0,1},{1,0},{2,3},{3,2},{4,5},{5,4},{6,7},{7,6},{8,9},{9,8},{10,11... | collective-permute-start | bytes 1622024 | tf_op jit(solution)/shard_map/ppermute | solution.py:244
  92.2 22.5 %copy-start.1 = (f32[2,512,256]{2,1,0:T(8,128)S(1)}, f32[2,512,256]{2,1,0:T(8,128)}, u32[]{:S(2)}) copy-start(f32[2,512,256]{2,1,0:T(8,128)} %copy-done) | copy-start | bytes 3145732
  105.9 29.2 %collective-permute-start.12 = (s16[2,528,256]{2,1,0:T(8,128)(2,1)S(1)}, s16[2,528,256]{2,1,0:T(8,128)(2,1)S(1)}, u32[]{:S(2)}, u32[]{:S(2)}) collective-permute-start(s16[2,528,256]{2,1,0:T(8,128)(2,1)S(1)} %pass_on.10), channel_id=1, source_target_pairs={{0,2},{1,3},{6,4},{7,5},{8,10},{9,11},{14,12},{15,13},{16,18},{17,... | collective-permute-start | bytes 1622024 | tf_op jit(solution)/shard_map/ppermute | solution.py:244
  116.1 19.1 %copy-start.4 = (f32[2,512,256]{2,1,0:T(8,128)S(1)}, f32[2,512,256]{2,1,0:T(8,128)}, u32[]{:S(2)}) copy-start(f32[2,512,256]{2,1,0:T(8,128)} %copy-done.2) | copy-start | bytes 3145732
  116.1 21.8 %collective-permute-start.21 = (s16[2,528,256]{2,1,0:T(8,128)(2,1)S(1)}, s16[2,528,256]{2,1,0:T(8,128)(2,1)S(1)}, u32[]{:S(2)}, u32[]{:S(2)}) collective-permute-start(s16[2,528,256]{2,1,0:T(8,128)(2,1)S(1)} %pass_on.15), channel_id=1, source_target_pairs={{0,2},{1,3},{6,4},{7,5},{8,10},{9,11},{14,12},{15,13},{16,18},{17,... | collective-permute-start | bytes 1622024 | tf_op jit(solution)/shard_map/ppermute | solution.py:244
  133.1 21.2 %collective-permute-start.10 = (s16[2,528,256]{2,1,0:T(8,128)(2,1)S(1)}, s16[2,528,256]{2,1,0:T(8,128)(2,1)S(1)}, u32[]{:S(2)}, u32[]{:S(2)}) collective-permute-start(s16[2,528,256]{2,1,0:T(8,128)(2,1)S(1)} %get-tuple-element.25), channel_id=1, source_target_pairs={{0,1},{1,0},{2,3},{3,2},{4,5},{5,4},{6,7},{7,6},{8,9},{9,8},{10,11... | collective-permute-start | bytes 1622024 | tf_op jit(solution)/shard_map/ppermute | solution.py:244
  133.4 27.5 %collective-permute-start.19 = (s16[2,528,256]{2,1,0:T(8,128)(2,1)S(1)}, s16[2,528,256]{2,1,0:T(8,128)(2,1)S(1)}, u32[]{:S(2)}, u32[]{:S(2)}) collective-permute-start(s16[2,528,256]{2,1,0:T(8,128)(2,1)S(1)} %get-tuple-element.34), channel_id=1, source_target_pairs={{0,1},{1,0},{2,3},{3,2},{4,5},{5,4},{6,7},{7,6},{8,9},{9,8},{10,11... | collective-permute-start | bytes 1622024 | tf_op jit(solution)/shard_map/ppermute | solution.py:244
  137.2 18.7 %collective-permute-start.13 = (s16[2,528,256]{2,1,0:T(8,128)(2,1)S(1)}, s16[2,528,256]{2,1,0:T(8,128)(2,1)S(1)}, u32[]{:S(2)}, u32[]{:S(2)}) collective-permute-start(s16[2,528,256]{2,1,0:T(8,128)(2,1)S(1)} %pass_on.11), channel_id=1, source_target_pairs={{2,4},{3,5},{4,2},{5,3},{10,12},{11,13},{12,10},{13,11},{18,20},{1... | collective-permute-start | bytes 1622024 | tf_op jit(solution)/shard_map/ppermute | solution.py:244
  140.0 20.9 %collective-permute-start.22 = (s16[2,528,256]{2,1,0:T(8,128)(2,1)S(1)}, s16[2,528,256]{2,1,0:T(8,128)(2,1)S(1)}, u32[]{:S(2)}, u32[]{:S(2)}) collective-permute-start(s16[2,528,256]{2,1,0:T(8,128)(2,1)S(1)} %pass_on.16), channel_id=1, source_target_pairs={{2,4},{3,5},{4,2},{5,3},{10,12},{11,13},{12,10},{13,11},{18,20},{1... | collective-permute-start | bytes 1622024 | tf_op jit(solution)/shard_map/ppermute | solution.py:244
  153.9 24.8 %collective-permute-start.15 = (s16[2,528,256]{2,1,0:T(8,128)(2,1)S(1)}, s16[2,528,256]{2,1,0:T(8,128)(2,1)S(1)}, u32[]{:S(2)}, u32[]{:S(2)}) collective-permute-start(s16[2,528,256]{2,1,0:T(8,128)(2,1)S(1)} %get-tuple-element.29), channel_id=1, source_target_pairs={{0,1},{1,0},{2,3},{3,2},{4,5},{5,4},{6,7},{7,6},{8,9},{9,8},{10,11... | collective-permute-start | bytes 1622024 | tf_op jit(solution)/shard_map/ppermute | solution.py:244
  154.2 28.9 %collective-permute-start.24 = (s16[2,528,256]{2,1,0:T(8,128)(2,1)S(1)}, s16[2,528,256]{2,1,0:T(8,128)(2,1)S(1)}, u32[]{:S(2)}, u32[]{:S(2)}) collective-permute-start(s16[2,528,256]{2,1,0:T(8,128)(2,1)S(1)} %get-tuple-element.38), channel_id=1, source_target_pairs={{0,1},{1,0},{2,3},{3,2},{4,5},{5,4},{6,7},{7,6},{8,9},{9,8},{10,11... | collective-permute-start | bytes 1622024 | tf_op jit(solution)/shard_map/ppermute | solution.py:244
  157.0 30.5 %collective-permute-start.14 = (s16[2,528,256]{2,1,0:T(8,128)(2,1)S(1)}, s16[2,528,256]{2,1,0:T(8,128)(2,1)S(1)}, u32[]{:S(2)}, u32[]{:S(2)}) collective-permute-start(s16[2,528,256]{2,1,0:T(8,128)(2,1)S(1)} %pass_on.12), channel_id=1, source_target_pairs={{0,2},{1,3},{2,0},{3,1},{4,6},{5,7},{6,4},{7,5},{8,10},{9,11},{10,... | collective-permute-start | bytes 1622024 | tf_op jit(solution)/shard_map/ppermute | solution.py:244
  162.0 29.6 %collective-permute-start.23 = (s16[2,528,256]{2,1,0:T(8,128)(2,1)S(1)}, s16[2,528,256]{2,1,0:T(8,128)(2,1)S(1)}, u32[]{:S(2)}, u32[]{:S(2)}) collective-permute-start(s16[2,528,256]{2,1,0:T(8,128)(2,1)S(1)} %pass_on.17), channel_id=1, source_target_pairs={{0,2},{1,3},{2,0},{3,1},{4,6},{5,7},{6,4},{7,5},{8,10},{9,11},{10,... | collective-permute-start | bytes 1622024 | tf_op jit(solution)/shard_map/ppermute | solution.py:244
  178.2 9.3 %copy-start.9 = (f32[2,512,256]{2,1,0:T(8,128)}, f32[2,512,256]{2,1,0:T(8,128)S(1)}, u32[]{:S(2)}) copy-start(f32[2,512,256]{2,1,0:T(8,128)S(1)} %get-tuple-element.31.own_ref) | copy-start | bytes 3145732
  178.2 9.3 %copy-start.11 = (f32[2,512,256]{2,1,0:T(8,128)}, f32[2,512,256]{2,1,0:T(8,128)S(1)}, u32[]{:S(2)}) copy-start(f32[2,512,256]{2,1,0:T(8,128)S(1)} %get-tuple-element.22.own_ref) | copy-start | bytes 3145732
  178.3 16.6 %collective-permute-start.9 = (s16[2,528,256]{2,1,0:T(8,128)(2,1)S(1)}, s16[2,528,256]{2,1,0:T(8,128)(2,1)S(1)}, u32[]{:S(2)}, u32[]{:S(2)}) collective-permute-start(s16[2,528,256]{2,1,0:T(8,128)(2,1)S(1)} %get-tuple-element.23), channel_id=1, source_target_pairs={{0,1},{1,0},{2,3},{3,2},{4,5},{5,4},{6,7},{7,6},{8,9},{9,8},{10,11... | collective-permute-start | bytes 1622024 | tf_op jit(solution)/shard_map/ppermute | solution.py:244
  178.7 28.1 %collective-permute-start.18 = (s16[2,528,256]{2,1,0:T(8,128)(2,1)}, s16[2,528,256]{2,1,0:T(8,128)(2,1)S(1)}, u32[]{:S(2)}, u32[]{:S(2)}) collective-permute-start(s16[2,528,256]{2,1,0:T(8,128)(2,1)} %get-tuple-element.32), channel_id=1, source_target_pairs={{0,1},{1,0},{2,3},{3,2},{4,5},{5,4},{6,7},{7,6},{8,9},{9,8},{10,11... | collective-permute-start | bytes 1622024 | tf_op jit(solution)/shard_map/ppermute | solution.py:244
  183.1 16.4 %collective-permute-start.17 = (s16[2,528,256]{2,1,0:T(8,128)(2,1)}, s16[2,528,256]{2,1,0:T(8,128)(2,1)S(1)}, u32[]{:S(2)}, u32[]{:S(2)}) collective-permute-start(s16[2,528,256]{2,1,0:T(8,128)(2,1)} %pass_on.14), channel_id=1, source_target_pairs={{0,2},{1,3},{6,4},{7,5},{8,10},{9,11},{14,12},{15,13},{16,18},{17,... | collective-permute-start | bytes 1622024 | tf_op jit(solution)/shard_map/ppermute | solution.py:244
  187.6 9.7 %copy-start.21 = (bf16[1024,512]{1,0:T(8,128)(2,1)S(1)}, bf16[1024,512]{1,0:T(8,128)(2,1)}, u32[]{:S(2)}) copy-start(bf16[1024,512]{1,0:T(8,128)(2,1)} %copy-done.20) | copy-start | bytes 3145732
  187.6 7.3 %copy-start.7 = (s16[2,528,256]{2,1,0:T(8,128)(2,1)}, s16[2,528,256]{2,1,0:T(8,128)(2,1)S(1)}, u32[]{:S(2)}) copy-start(s16[2,528,256]{2,1,0:T(8,128)(2,1)S(1)} %collective-permute-done.14.refs_2_.refs_0_) | copy-start | bytes 1622020
  187.6 19.2 %collective-permute-start.26 = (s16[2,528,256]{2,1,0:T(8,128)(2,1)}, s16[2,528,256]{2,1,0:T(8,128)(2,1)}, u32[]{:S(2)}, u32[]{:S(2)}) collective-permute-start(s16[2,528,256]{2,1,0:T(8,128)(2,1)} %pass_on.19), channel_id=1, source_target_pairs={{0,2},{1,3},{6,4},{7,5},{8,10},{9,11},{14,12},{15,13},{16,18},{17,... | collective-permute-start | bytes 1622024 | tf_op jit(solution)/shard_map/ppermute | solution.py:244
  191.6 8.7 %collective-permute-start.16 = (s16[2,528,256]{2,1,0:T(8,128)(2,1)}, s16[2,528,256]{2,1,0:T(8,128)(2,1)}, u32[]{:S(2)}, u32[]{:S(2)}) collective-permute-start(s16[2,528,256]{2,1,0:T(8,128)(2,1)} %pass_on.13), channel_id=1, source_target_pairs={{2,4},{3,5},{4,2},{5,3},{10,12},{11,13},{12,10},{13,11},{18,20},{1... | collective-permute-start | bytes 1622024 | tf_op jit(solution)/shard_map/ppermute | solution.py:244
  195.7 4.6 %copy-start.8 = (s16[2,528,256]{2,1,0:T(8,128)(2,1)S(1)}, s16[2,528,256]{2,1,0:T(8,128)(2,1)}, u32[]{:S(2)}) copy-start(s16[2,528,256]{2,1,0:T(8,128)(2,1)} %copy-done.7) | copy-start | bytes 1622020
  195.7 11.1 %collective-permute-start.25 = (s16[2,528,256]{2,1,0:T(8,128)(2,1)}, s16[2,528,256]{2,1,0:T(8,128)(2,1)}, u32[]{:S(2)}, u32[]{:S(2)}) collective-permute-start(s16[2,528,256]{2,1,0:T(8,128)(2,1)} %pass_on.18), channel_id=1, source_target_pairs={{2,4},{3,5},{4,2},{5,3},{10,12},{11,13},{12,10},{13,11},{18,20},{1... | collective-permute-start | bytes 1622024 | tf_op jit(solution)/shard_map/ppermute | solution.py:244
  206.7 5.3 %collective-permute-start.27 = (f32[128,256]{1,0:T(8,128)S(1)}, f32[128,256]{1,0:T(8,128)S(1)}, u32[]{:S(2)}, u32[]{:S(2)}) collective-permute-start(f32[128,256]{1,0:T(8,128)S(1)} %dynamic-slice_bitcast_fusion.1), channel_id=1, source_target_pairs={{0,8},{1,9},{2,10},{3,11},{4,12},{5,13},{6,14},{7,15},{8,0},{9,1},... | collective-permute-start | bytes 393224 | tf_op jit(solution)/shard_map/ppermute | solution.py:244
  211.5 34.5 %copy-start.18 = (bf16[1024,256]{1,0:T(8,128)(2,1)S(1)}, bf16[1024,256]{1,0:T(8,128)(2,1)}, u32[]{:S(2)}) copy-start(bf16[1024,256]{1,0:T(8,128)(2,1)} %copy-done.17) | copy-start | bytes 1572868
  211.6 1.5 collective-permute-start.33
  212.1 6.4 %collective-permute-start.28 = (f32[128,256]{1,0:T(8,128)S(1)}, f32[128,256]{1,0:T(8,128)S(1)}, u32[]{:S(2)}, u32[]{:S(2)}) collective-permute-start(f32[128,256]{1,0:T(8,128)S(1)} %bitcast_add_fusion.1), channel_id=1, source_target_pairs={{0,1},{1,0},{2,3},{3,2},{4,5},{5,4},{6,7},{7,6},{8,9},{9,8},{10,11... | collective-permute-start | bytes 393224 | tf_op jit(solution)/shard_map/ppermute | solution.py:244
  213.1 7.3 %collective-permute-start.34 = (f32[128,256]{1,0:T(8,128)S(1)}, f32[128,256]{1,0:T(8,128)S(1)}, u32[]{:S(2)}, u32[]{:S(2)}) collective-permute-start(f32[128,256]{1,0:T(8,128)S(1)} %bitcast_add_fusion), channel_id=1, source_target_pairs={{0,1},{1,0},{2,3},{3,2},{4,5},{5,4},{6,7},{7,6},{8,9},{9,8},{10,11... | collective-permute-start | bytes 393224 | tf_op jit(solution)/shard_map/ppermute | solution.py:244
  218.6 6.3 %collective-permute-start.29 = (f32[128,256]{1,0:T(8,128)S(1)}, f32[128,256]{1,0:T(8,128)S(1)}, u32[]{:S(2)}, u32[]{:S(2)}) collective-permute-start(f32[128,256]{1,0:T(8,128)S(1)} %add.282), channel_id=1, source_target_pairs={{0,16},{1,17},{2,18},{3,19},{4,20},{5,21},{6,22},{7,23},{8,24},{9,... | collective-permute-start | bytes 393224 | tf_op jit(solution)/shard_map/ppermute | solution.py:244
  220.4 9.7 %collective-permute-start.35 = (f32[128,256]{1,0:T(8,128)S(1)}, f32[128,256]{1,0:T(8,128)S(1)}, u32[]{:S(2)}, u32[]{:S(2)}) collective-permute-start(f32[128,256]{1,0:T(8,128)S(1)} %add.287), channel_id=1, source_target_pairs={{0,16},{1,17},{2,18},{3,19},{4,20},{5,21},{6,22},{7,23},{8,24},{9,... | collective-permute-start | bytes 393224 | tf_op jit(solution)/shard_map/ppermute | solution.py:244
  224.9 8.7 %collective-permute-start.30 = (f32[128,256]{1,0:T(8,128)S(1)}, f32[128,256]{1,0:T(8,128)S(1)}, u32[]{:S(2)}, u32[]{:S(2)}) collective-permute-start(f32[128,256]{1,0:T(8,128)S(1)} %add.283), channel_id=1, source_target_pairs={{0,2},{1,3},{2,0},{3,1},{4,6},{5,7},{6,4},{7,5},{8,10},{9,11},{10,... | collective-permute-start | bytes 393224 | tf_op jit(solution)/shard_map/ppermute | solution.py:244
  230.2 7.1 %collective-permute-start.36 = (f32[128,256]{1,0:T(8,128)S(1)}, f32[128,256]{1,0:T(8,128)S(1)}, u32[]{:S(2)}, u32[]{:S(2)}) collective-permute-start(f32[128,256]{1,0:T(8,128)S(1)} %add.288), channel_id=1, source_target_pairs={{0,2},{1,3},{2,0},{3,1},{4,6},{5,7},{6,4},{7,5},{8,10},{9,11},{10,... | collective-permute-start | bytes 393224 | tf_op jit(solution)/shard_map/ppermute | solution.py:244
  233.7 12.3 %collective-permute-start.31 = (f32[128,256]{1,0:T(8,128)S(1)}, f32[128,256]{1,0:T(8,128)S(1)}, u32[]{:S(2)}, u32[]{:S(2)}) collective-permute-start(f32[128,256]{1,0:T(8,128)S(1)} %add.284), channel_id=1, source_target_pairs={{0,4},{1,5},{2,6},{3,7},{4,0},{5,1},{6,2},{7,3},{8,12},{9,13},{10,... | collective-permute-start | bytes 393224 | tf_op jit(solution)/shard_map/ppermute | solution.py:244
  237.3 10.2 %collective-permute-start.37 = (f32[128,256]{1,0:T(8,128)S(1)}, f32[128,256]{1,0:T(8,128)S(1)}, u32[]{:S(2)}, u32[]{:S(2)}) collective-permute-start(f32[128,256]{1,0:T(8,128)S(1)} %add.289), channel_id=1, source_target_pairs={{0,4},{1,5},{2,6},{3,7},{4,0},{5,1},{6,2},{7,3},{8,12},{9,13},{10,... | collective-permute-start | bytes 393224 | tf_op jit(solution)/shard_map/ppermute | solution.py:244
  246.0 1.7 collective-permute-start.32
  247.5 1.4 collective-permute-start.38
  (15 other events, 26.3 us)
